TPU v7x, 128 devices: a whole 4x4x4 slice. The times are simulated.
128 devices in a mesh: tm: 16 (over z, y), scene: 8 (over x, core).
Axes of the slice: x: 4, y: 4, z: 4, core: 2. Of those that a mesh axis runs over, the one named last changes fastest.
Arguments:
- frames: bfloat16 [1024, 2, 64, 384], P('tm', None, 'scene'), may hold values from -6 to 6
- conv_weight: bfloat16 [3, 3, 3, 384, 384], replicated, may hold values from -0.0625 to 0.0625
- down_weight: bfloat16 [8, 384, 384], replicated, may hold values from -0.109375 to 0.109375
- w_query: bfloat16 [384, 384], replicated, may hold values from -64 to 64
- w_key: bfloat16 [384, 384], replicated, may hold values from -2 to 2
- w_value: bfloat16 [384, 384], replicated, may hold values from -0.3125 to 0.3125
- w_out: bfloat16 [384, 384], replicated, may hold values from -0.3125 to 0.3125
- shot_lengths: int32 [8], replicated, may hold values from 1 to 64, 128 in all
- scene_label: int32 [128, 1], P('tm'), may hold values from 0 to 7; in each aligned block of 8 rows (0 to 7, 8 to 15, ...) at most 2 rows name the same one
- out_grad: bfloat16 [1024, 2, 64, 384], P('tm', None, 'scene'), may hold values from -6 to 6
Outputs:
- latent_out: bfloat16 [128, 2, 64, 384], P('tm', None, 'scene')
- frame_grad: bfloat16 [1024, 2, 64, 384], P('tm', None, 'scene')
Inputs may be any that keep to these rules, and one draw needn't show every extreme that they name: `shot_lengths`: the lengths sum to 128; the longest is exactly 64. `scene_label`: within each aligned block of 8 latent frames (those of one index of tm) no label occurs more than 2 times; in some block one label occurs exactly 2 times.
All inputs are finite; a program needn't handle non-finite values.
Results may differ from a plain program's by a relative error of at most 0.008.
Values may be sent and summed in bfloat16 or wider, within the bound.
No kernel may reach another device: no remote copies, remote signals or barrier semaphores. Data moves between devices by JAX's collectives and lax.ppermute only.
A program may use at most 128 MiB of HBM per device.

v0:
```python
import math

import jax
import jax.numpy as jnp
from jax import lax
from jax.experimental import pallas as pl
from jax.experimental.pallas import tpu as pltpu
from jax.sharding import PartitionSpec as P

HEAD = 64
BF16 = jnp.bfloat16
F32 = jnp.float32
VMEM = pl.BlockSpec(memory_space=pltpu.VMEM)
SMEM = pl.BlockSpec(memory_space=pltpu.SMEM)
ANY = pl.BlockSpec(memory_space=pl.ANY)
NT = (((1,), (1,)), ((), ()))
NN = (((1,), (0,)), ((), ()))

TAPS = [(off, side) for side in (1, 0, 2) for off in (0, 2, 1)]


def dot(a, b, dims=NN):
    return lax.dot_general(a, b, dims, preferred_element_type=F32)


def weight_copies(weight_ref, folded, sems, taps):
    chans = weight_ref.shape[-1]
    copies = []
    for k, (shift_t, shift_w) in enumerate(taps):
        group = []
        for h_in in range(2):
            for h_out in range(2):
                group.append(
                    pltpu.make_async_copy(
                        weight_ref.at[shift_t, h_in - h_out + 1, shift_w],
                        folded.at[k, pl.ds(h_in * chans, chans), pl.ds(h_out * chans, chans)],
                        sems.at[k, 2 * h_in + h_out],
                    )
                )
        copies.append(group)
    return copies


def build_shifted(frame_of, low, high, even, odd):
    count = even.shape[1] // 8
    width = even.shape[2]
    sub = lax.broadcasted_iota(jnp.int32, (8, width), 0)
    before = None
    for t in range(count):
        own = frame_of(t).astype(F32)
        left = jnp.where(
            sub == 0, jnp.broadcast_to(low[t : t + 1, :], (8, width)), pltpu.roll(own, 1, 0)
        )
        right = jnp.where(
            sub == 7, jnp.broadcast_to(high[t : t + 1, :], (8, width)), pltpu.roll(own, 7, 0)
        )
        now = (left, own, right)
        if t % 2 == 1:
            for s in range(3):
                even[s, 8 * (t - 1) : 8 * (t + 1), :] = jnp.concatenate(
                    [before[s], now[s]], axis=0
                ).astype(BF16)
        elif t > 0:
            for s in range(3):
                odd[s, 8 * (t - 2) : 8 * t, :] = jnp.concatenate(
                    [before[s], now[s]], axis=0
                ).astype(BF16)
        before = now


def conv_taps(even, odd, folded, copies, total, dims):
    rows = total.shape[0]
    for k, (off, side) in enumerate(TAPS):
        for copy in copies[k]:
            copy.wait()
        if off == 1:
            lhs = odd[side, :, :]
        else:
            lhs = even[side, 8 * off : 8 * off + rows, :]
        part = dot(lhs, folded[k], dims)
        if k == 0:
            total[...] = part
        else:
            total[...] += part


def pick_sides(parity, from_core, from_chip, low, high):
    core = from_core[...].astype(F32)
    chip = from_chip[...].astype(F32)
    even_core = parity == 0
    low[0 : core.shape[0], :] = jnp.where(even_core, chip, core)
    high[0 : core.shape[0], :] = jnp.where(even_core, core, chip)


def forward_kernel(
    place,
    lengths,
    frames,
    rim,
    from_core,
    from_chip,
    out_grad,
    weight,
    down,
    latent_out,
    sums_out,
    tail_out,
    grad_out,
    core_out,
    chip_out,
    block,
    grad_block,
    down_block,
    low,
    high,
    even,
    odd,
    folded,
    total,
    act,
    sems,
    weight_sems,
):
    chans = frames.shape[-1]
    count = frames.shape[0]
    first = [
        pltpu.make_async_copy(
            frames.at[:, h], block.at[:, :, pl.ds(h * chans, chans)], sems.at[h]
        )
        for h in range(2)
    ]
    for copy in first:
        copy.start()
    copies = weight_copies(weight, folded, weight_sems, TAPS)
    for copy in copies[0]:
        copy.start()
    later = [
        pltpu.make_async_copy(
            out_grad.at[:, h], grad_block.at[:, :, pl.ds(h * chans, chans)], sems.at[2 + h]
        )
        for h in range(2)
    ] + [pltpu.make_async_copy(down, down_block, sems.at[4])]
    for group in copies[1:]:
        for copy in group:
            copy.start()
    for copy in later:
        copy.start()
    parity = place[1]
    pick_sides(parity, from_core, from_chip, low, high)
    for copy in first:
        copy.wait()

    def frame_of(t):
        if t < 2:
            return rim[t]
        return block[t - 2]

    build_shifted(frame_of, low, high, even, odd)
    conv_taps(even, odd, folded, copies, total, NN)
    for copy in later:
        copy.wait()

    for j in range(count // 8):
        rows = slice(64 * j, 64 * (j + 1))
        pre = total[rows, :]
        gate = 1.0 / (1.0 + jnp.exp(-pre))
        own = block[8 * j : 8 * (j + 1)].astype(F32)
        act[j] = own + (pre * gate).reshape(own.shape)
        slope = gate * (1.0 + pre * (1.0 - gate))
        grad = grad_block[8 * j : 8 * (j + 1)].astype(F32) * slope.reshape(own.shape)
        grad_out[8 * j : 8 * (j + 1)] = grad.astype(BF16)
        first_col = grad[:, 0, :]
        last_col = grad[:, 7, :]
        core_out[8 * j : 8 * (j + 1), :] = jnp.where(parity == 0, last_col, first_col)
        chip_out[8 * j : 8 * (j + 1), :] = jnp.where(parity == 0, first_col, last_col)

    latent = jnp.zeros((2 * count, chans), F32)
    for k in range(8):
        lhs = jnp.concatenate(
            [
                act[:, k, :, h * chans : (h + 1) * chans].reshape(count, chans)
                for h in range(2)
            ],
            axis=0,
        ).astype(BF16)
        latent = latent + dot(lhs, down_block[k])
    latent = latent.astype(BF16).astype(F32)
    rounded = [
        jnp.concatenate([latent[8 * j : 8 * j + 8], latent[count + 8 * j : count + 8 * j + 8]], 0)
        for j in range(count // 8)
    ]
    running = jnp.zeros_like(rounded[0])
    for j in range(count // 8):
        now = place[0] * (count // 8) + j
        start = jnp.int32(0)
        begins = jnp.int32(0)
        for k in range(lengths.shape[0]):
            begins = jnp.where(start == now, 1, begins)
            start = start + lengths[k]
        running = jnp.where(begins > 0, rounded[j], running + rounded[j])
        sums_out[j] = running
        latent_out[j] = rounded[j]
    tail_out[...] = running


def forward(place, lengths, frames, rim, from_core, from_chip, out_grad, weight, down):
    count, _, cols, chans = frames.shape
    rows, wide = count * cols, 2 * chans
    lat = count // 8
    return pl.pallas_call(
        forward_kernel,
        out_shape=(
            jax.ShapeDtypeStruct((lat, 16, chans), F32),
            jax.ShapeDtypeStruct((lat, 16, chans), F32),
            jax.ShapeDtypeStruct((16, chans), F32),
            jax.ShapeDtypeStruct((count, cols, wide), BF16),
            jax.ShapeDtypeStruct((count, wide), F32),
            jax.ShapeDtypeStruct((count, wide), F32),
        ),
        in_specs=[SMEM, SMEM, ANY, VMEM, VMEM, VMEM, ANY, ANY, ANY],
        out_specs=[VMEM] * 6,
        scratch_shapes=[
            pltpu.VMEM((count, cols, wide), BF16),
            pltpu.VMEM((count, cols, wide), BF16),
            pltpu.VMEM(down.shape, BF16),
            pltpu.VMEM((count + 8, wide), F32),
            pltpu.VMEM((count + 8, wide), F32),
            pltpu.VMEM((3, rows + 16, wide), BF16),
            pltpu.VMEM((3, rows, wide), BF16),
            pltpu.VMEM((9, wide, wide), BF16),
            pltpu.VMEM((rows, wide), F32),
            pltpu.VMEM((lat, 8, cols, wide), F32),
            pltpu.SemaphoreType.DMA((5,)),
            pltpu.SemaphoreType.DMA((9, 4)),
        ],
        compiler_params=pltpu.CompilerParams(vmem_limit_bytes=48 * 2**20),
        cost_estimate=pl.CostEstimate(
            flops=2 * 9 * rows * wide * wide, bytes_accessed=16 * 2**20, transcendentals=rows * wide
        ),
        name="forward",
    )(place, lengths, frames, rim, from_core, from_chip, out_grad, weight, down)


def backward_kernel(
    place,
    grad,
    rim,
    from_core,
    from_chip,
    out_grad,
    weight,
    result,
    low,
    high,
    even,
    odd,
    folded,
    total,
    weight_sems,
):
    count, _, cols, chans = out_grad.shape
    copies = weight_copies(
        weight, folded, weight_sems, [(2 - off, 2 - side) for off, side in TAPS]
    )
    for group in copies:
        for copy in group:
            copy.start()
    pick_sides(place[1], from_core, from_chip, low, high)

    def frame_of(t):
        if t >= count:
            return rim[t - count]
        return grad[t]

    build_shifted(frame_of, low, high, even, odd)
    conv_taps(even, odd, folded, copies, total, NT)
    for j in range(count // 8):
        part = total[64 * j : 64 * (j + 1), :]
        for h in range(2):
            mine = part[:, h * chans : (h + 1) * chans].reshape(8, cols, chans)
            result[8 * j : 8 * (j + 1), h] = (
                out_grad[8 * j : 8 * (j + 1), h].astype(F32) + mine
            ).astype(BF16)


def backward(place, grad, rim, from_core, from_chip, out_grad, weight):
    count, _, cols, chans = out_grad.shape
    rows, wide = count * cols, 2 * chans
    return pl.pallas_call(
        backward_kernel,
        out_shape=jax.ShapeDtypeStruct(out_grad.shape, BF16),
        in_specs=[SMEM, VMEM, VMEM, VMEM, VMEM, VMEM, ANY],
        out_specs=VMEM,
        scratch_shapes=[
            pltpu.VMEM((count + 8, wide), F32),
            pltpu.VMEM((count + 8, wide), F32),
            pltpu.VMEM((3, rows + 16, wide), BF16),
            pltpu.VMEM((3, rows, wide), BF16),
            pltpu.VMEM((9, wide, wide), BF16),
            pltpu.VMEM((rows, wide), F32),
            pltpu.SemaphoreType.DMA((9, 4)),
        ],
        compiler_params=pltpu.CompilerParams(vmem_limit_bytes=40 * 2**20),
        cost_estimate=pl.CostEstimate(
            flops=2 * 9 * rows * wide * wide, bytes_accessed=12 * 2**20, transcendentals=0
        ),
        name="backward",
    )(place, grad, rim, from_core, from_chip, out_grad, weight)


def mix_kernel(place, lengths, latent, sums, tails, mixed):
    lat = latent.shape[0]
    peers = tails.shape[0]
    me = place[0]
    starts = [jnp.int32(0)]
    for k in range(lengths.shape[0] - 1):
        starts.append(starts[-1] + lengths[k])
    opened = jnp.int32(0)
    for start in starts:
        opened = jnp.where(start < me * lat, jnp.maximum(start, opened), opened)
    carried = jnp.zeros(latent.shape[1:], F32)
    for k in range(peers):
        counts = jnp.logical_and(k < me, (k + 1) * lat > opened)
        carried = carried + jnp.where(counts, tails[k], 0.0)
    for j in range(lat):
        now = me * lat + j
        begin = jnp.int32(0)
        for start in starts:
            begin = jnp.where(start <= now, jnp.maximum(start, begin), begin)
        shot = sums[j] + jnp.where(begin < me * lat, carried, 0.0)
        length = jnp.full(shot.shape, now - begin + 1, jnp.int32).astype(F32)
        mixed[16 * j : 16 * (j + 1), :] = (latent[j] + shot / length).astype(BF16)


def mix(place, lengths, latent, sums, tails):
    return pl.pallas_call(
        mix_kernel,
        out_shape=jax.ShapeDtypeStruct((latent.shape[0] * 16, latent.shape[2]), BF16),
        in_specs=[SMEM, SMEM, VMEM, VMEM, VMEM],
        out_specs=VMEM,
        name="mix",
    )(place, lengths, latent, sums, tails)


def attend_kernel(labels, mine, *refs):
    pieces, (w_query, w_key, w_value, w_out, result, keys, values) = refs[:-7], refs[-7:]
    tokens, chans = mine.shape
    lat = labels.shape[0]
    per = tokens // lat
    at = 0
    for piece in pieces:
        block = piece[...]
        size = block.shape[0]
        keys[at : at + size, :] = dot(block, w_key[...]).astype(BF16)
        values[at : at + size, :] = dot(block, w_value[...]).astype(BF16)
        at += size
    query = (dot(mine[...], w_query[...]).astype(BF16) * BF16(1.0 / math.sqrt(HEAD))).astype(BF16)
    row = lax.broadcasted_iota(jnp.int32, (tokens, 1), 0) // per
    col = (lax.broadcasted_iota(jnp.int32, (1, tokens), 1) % tokens) // per
    row_label = jnp.zeros((tokens, 1), jnp.int32)
    col_label = jnp.zeros((1, tokens), jnp.int32)
    for j in range(lat):
        row_label = jnp.where(row == j, labels[j, 0], row_label)
        col_label = jnp.where(col == j, labels[j, 0], col_label)
    same = jnp.logical_and(row_label == col_label, col <= row)
    bias = jnp.where(same, 0.0, -1e30).astype(F32)
    bias = jnp.concatenate([bias] * (at // tokens), axis=1)
    outs = []
    for head in range(chans // HEAD):
        lanes = slice(head * HEAD, (head + 1) * HEAD)
        scores = dot(query[:, lanes], keys[:, lanes], NT) + bias
        top = jnp.max(scores, axis=1, keepdims=True)
        expo = jnp.exp(scores - top)
        norm = jnp.sum(expo, axis=1, keepdims=True)
        outs.append(dot(expo.astype(BF16), values[:, lanes]) / norm)
    heads = jnp.concatenate(outs, axis=1).astype(BF16)
    final = mine[...].astype(F32) + dot(heads, w_out[...])
    for j in range(lat):
        for h in range(2):
            at = per * j + 8 * h
            result[j, h] = final[at : at + 8].astype(BF16)


def attend(labels, mine, pieces, w_query, w_key, w_value, w_out):
    tokens, chans = mine.shape
    total = sum(piece.shape[0] for piece in pieces)
    return pl.pallas_call(
        attend_kernel,
        out_shape=jax.ShapeDtypeStruct((labels.shape[0], 2, 8, chans), BF16),
        in_specs=[SMEM] + [VMEM] * (5 + len(pieces)),
        out_specs=VMEM,
        scratch_shapes=[pltpu.VMEM((total, chans), BF16), pltpu.VMEM((total, chans), BF16)],
        compiler_params=pltpu.CompilerParams(vmem_limit_bytes=32 * 2**20),
        name="attend",
    )(labels, mine, *pieces, w_query, w_key, w_value, w_out)


def shifted(value, axis, steps):
    count = lax.axis_size(axis)
    return lax.ppermute(
        value, axis, [(i, i + steps) for i in range(count) if 0 <= i + steps < count]
    )


def with_core(value):
    count = lax.axis_size("scene")
    return lax.ppermute(value, "scene", [(i, i ^ 1) for i in range(count)])


def with_chip(value):
    count = lax.axis_size("scene")
    pairs = [(i, i + 1) for i in range(1, count - 1, 2)]
    return lax.ppermute(value, "scene", pairs + [(b, a) for a, b in pairs])


def gathered(value):
    count = lax.axis_size("scene")
    chips = [
        lax.ppermute(value, "scene", [(i, (i + 2 * k) % count) for i in range(count)])
        for k in range(1, count // 2)
    ]
    own = jnp.concatenate([value, *chips], axis=0)
    return [own, with_core(own)]


def per_device(
    frames,
    conv_weight,
    down_weight,
    w_query,
    w_key,
    w_value,
    w_out,
    shot_lengths,
    scene_label,
    out_grad,
):
    count, _, cols, chans = frames.shape
    parity = lax.axis_index("scene") % 2
    place = jnp.stack([lax.axis_index("tm"), parity]).astype(jnp.int32)

    def columns(at, top):
        cut = lax.dynamic_slice_in_dim(frames, at, 1, axis=2).reshape(count, 2 * chans)
        rim_cut = lax.dynamic_slice_in_dim(top, at, 1, axis=1).reshape(2, 2 * chans)
        return jnp.concatenate([rim_cut, cut], axis=0)

    rim = shifted(frames[count - 2 :], "tm", 1)
    rim = jnp.swapaxes(rim, 1, 2).reshape(2, cols, 2 * chans)
    inner = (cols - 1) * (1 - parity)
    from_core = with_core(columns(inner, rim))
    from_chip = with_chip(columns(cols - 1 - inner, rim))
    latent, sums, tail, grad, core_cols, chip_cols = forward(
        place, shot_lengths, frames, rim, from_core, from_chip, out_grad, conv_weight, down_weight
    )

    peers = lax.axis_size("tm")
    tails = lax.all_to_all(
        jnp.broadcast_to(tail[None], (peers, *tail.shape)), "tm", 0, 0, tiled=True
    )
    mixed = mix(place, shot_lengths, latent, sums, tails)
    pieces = gathered(mixed)
    latent_out = attend(scene_label, mixed, pieces, w_query, w_key, w_value, w_out)

    rim_after = shifted(grad[:2], "tm", -1)

    def extended(own, at):
        corner = lax.dynamic_slice_in_dim(rim_after, at, 1, axis=1).reshape(2, 2 * chans)
        return jnp.concatenate([own.astype(BF16), corner], axis=0)

    grad_core = with_core(extended(core_cols, inner))
    grad_chip = with_chip(extended(chip_cols, cols - 1 - inner))
    frame_grad = backward(place, grad, rim_after, grad_core, grad_chip, out_grad, conv_weight)
    return (latent_out, frame_grad)


def solution(mesh):
    in_specs = (
        P("tm", None, "scene", None),
        P(),
        P(),
        P(),
        P(),
        P(),
        P(),
        P(),
        P("tm", None),
        P("tm", None, "scene", None),
    )
    out_specs = (P("tm", None, "scene", None), P("tm", None, "scene", None))
    return jax.shard_map(
        per_device, mesh=mesh, in_specs=in_specs, out_specs=out_specs, check_vma=False
    )
```

profile of v0, /device:TPU:1, one launch (start us, length us, event | category | flops | bytes accessed | tf_op | source)
XLA Modules:
  0.0 87.1 jit_solution(1437457539130459028)
XLA Ops:
  0.6 0.7 slice.6
  1.4 4.0 %collective-permute-start = (bf16[2,2,8,384]{3,2,1,0:T(8,128)(2,1)S(1)}, bf16[2,2,8,384]{3,2,1,0:T(8,128)(2,1)S(1)}, u32[]{:S(2)}, u32[]{:S(2)}) collective-permute-start(bf16[2,2,8,384]{3,2,1,0:T(8,128)(2,1)S(1)} %slice.6), channel_id=1, source_target_pairs={{0,8},{8,16},{16,24},{24,32},{32,40},{40,48},{48,56},{56,64},{64,7... | collective-permute-start | bytes 73736 | tf_op jit(solution)/shard_map/ppermute | solution.py:400
  5.4 2.8 %dynamic-slice_reduce_fusion = (bf16[64,2,384]{2,1,0:T(2,128)(2,1)S(1)}, bf16[64,2,384]{2,1,0:T(2,128)(2,1)S(1)}) fusion(bf16[64,2,8,384]{3,2,1,0:T(8,128)(2,1)} %frames.1, s32[]{:T(128)S(6)} %select_n.19, s32[]{:T(128)S(6)} %select_n.18), kind=kLoop, calls=%fused_computation.1 | loop fusion | bytes 393224 | tf_op jit(solution)/shard_map/dynamic_slice | solution.py:443
  8.4 4.0 %collective-permute-start.2 = (bf16[66,768]{1,0:T(8,128)(2,1)S(1)}, bf16[66,768]{1,0:T(8,128)(2,1)S(1)}, u32[]{:S(2)}, u32[]{:S(2)}) collective-permute-start(bf16[66,768]{1,0:T(8,128)(2,1)S(1)} %pad_maximum_fusion.2), channel_id=1, source_target_pairs={{1,2},{3,4},{5,6},{2,1},{4,3},{6,5},{9,10},{11,12},{13,14},{10,9},... | collective-permute-start | bytes 304136 | tf_op jit(solution)/shard_map/ppermute | solution.py:413
  12.4 0.1 collective-permute-start.1
  12.6 2.2 %collective-permute-done.2.from_chip = bf16[66,768]{1,0:T(8,128)(2,1)S(1)} collective-permute-done((bf16[66,768]{1,0:T(8,128)(2,1)S(1)}, bf16[66,768]{1,0:T(8,128)(2,1)S(1)}, u32[]{:S(2)}, u32[]{:S(2)}) %collective-permute-start.2) | collective-permute-done | bytes 101408 | tf_op jit(solution)/shard_map/ppermute | solution.py:413
  14.8 1.1 %copy-done.5 = bf16[64,2,8,384]{3,2,1,0:T(8,128)(2,1)S(1)} copy-done((bf16[64,2,8,384]{3,2,1,0:T(8,128)(2,1)S(1)}, bf16[64,2,8,384]{3,2,1,0:T(8,128)(2,1)}, u32[]{:S(2)}) %copy-start.5) | copy-done | bytes 786456
  15.9 0.7 copy-done.8
  16.6 1.7 %copy-done.12 = bf16[8,384,384]{2,1,0:T(8,128)(2,1)S(1)} copy-done((bf16[8,384,384]{2,1,0:T(8,128)(2,1)S(1)}, bf16[8,384,384]{2,1,0:T(8,128)(2,1)}, u32[]{:S(2)}) %copy-start.12) | copy-done | bytes 2359320
  18.2 1.1 %copy-done.13 = bf16[64,2,8,384]{3,2,1,0:T(8,128)(2,1)S(1)} copy-done((bf16[64,2,8,384]{3,2,1,0:T(8,128)(2,1)S(1)}, bf16[64,2,8,384]{3,2,1,0:T(8,128)(2,1)}, u32[]{:S(2)}) %copy-start.13) | copy-done | bytes 786456
  19.4 12.3 %forward.1 = (f32[8,16,384]{2,1,0:T(8,128)S(1)}, f32[8,16,384]{2,1,0:T(8,128)S(1)}, f32[16,384]{1,0:T(8,128)S(1)}, bf16[64,8,768]{2,1,0:T(8,128)(2,1)S(1)}, f32[...) custom-call(s32[2]{0:T(128)S(1)} %pad_add_fusion.place, s32[8]{0:T(128)S(1)} %copy-done.8, ...), custom_call_target="tpu_custom_call" | custom-call | flops 5435817984 | bytes 16777216 | tf_op jit(solution)/shard_map/forward/pallas_call | solution.py:210
  31.7 0.7 copy-done.6
  32.4 0.7 copy-done.7
  33.0 0.8 broadcast_in_dim.2
  33.8 7.5 %all-to-all-start = ((f32[16,16,384]{2,1,0:T(8,128)}), f32[16,16,384]{2,1,0:T(8,128)S(1)}, u32[]{:S(2)}, u32[]{:S(2)}) async-start(f32[16,16,384]{2,1,0:T(8,128)} %broadcast_in_dim.2), calls=%async_computation | async-start | bytes 786432 | tf_op jit(solution)/shard_map/all_to_all | solution.py:457
  41.3 1.3 %collective-permute-start.7 = (bf16[2,8,768]{2,1,0:T(8,128)(2,1)S(1)}, bf16[2,8,768]{2,1,0:T(8,128)(2,1)S(1)}, u32[]{:S(2)}, u32[]{:S(2)}) collective-permute-start(bf16[2,8,768]{2,1,0:T(8,128)(2,1)S(1)} %slice.7), channel_id=1, source_target_pairs={{8,0},{16,8},{24,16},{32,24},{40,32},{48,40},{56,48},{64,56},{72,6... | collective-permute-start | bytes 73736 | tf_op jit(solution)/shard_map/ppermute | solution.py:400
  42.7 6.1 %collective-permute-done.7.rim = bf16[2,8,768]{2,1,0:T(8,128)(2,1)S(1)} collective-permute-done((bf16[2,8,768]{2,1,0:T(8,128)(2,1)S(1)}, bf16[2,8,768]{2,1,0:T(8,128)(2,1)S(1)}, u32[]{:S(2)}, u32[]{:S(2)}) %collective-permute-start.7) | collective-permute-done | bytes 24608 | tf_op jit(solution)/shard_map/ppermute | solution.py:400
  48.9 3.7 %collective-permute-start.9 = (bf16[66,768]{1,0:T(8,128)(2,1)S(1)}, bf16[66,768]{1,0:T(8,128)(2,1)S(1)}, u32[]{:S(2)}, u32[]{:S(2)}) collective-permute-start(bf16[66,768]{1,0:T(8,128)(2,1)S(1)} %pad_maximum_fusion.4), channel_id=1, source_target_pairs={{1,2},{3,4},{5,6},{2,1},{4,3},{6,5},{9,10},{11,12},{13,14},{10,9},... | collective-permute-start | bytes 304136 | tf_op jit(solution)/shard_map/ppermute | solution.py:413
  52.6 0.7 copy-done.15
  53.3 2.0 %mix.1.mine = bf16[128,384]{1,0:T(8,128)(2,1)} custom-call(s32[2]{0:T(128)} %copy-done.9, s32[8]{0:T(128)} %lengths.3, f32[8,16,384]{2,1,0:T(8,128)} %copy-done.6, f32[8,16,384]{2,1,0:T(8,128)} %copy-done.7, f32[16,16,384]{2,1,0:T(8,128)} %copy-done.15), custom_call_target="tpu_custom_call" | custom-call | tf_op jit(solution)/shard_map/mix/pallas_call | solution.py:336
  55.3 1.0 %collective-permute-start.3 = (bf16[128,384]{1,0:T(8,128)(2,1)}, bf16[128,384]{1,0:T(8,128)(2,1)S(1)}, u32[]{:S(2)}, u32[]{:S(2)}) collective-permute-start(bf16[128,384]{1,0:T(8,128)(2,1)} %mix.1.mine), channel_id=1, source_target_pairs={{0,2},{1,3},{2,4},{3,5},{4,6},{5,7},{6,0},{7,1},{8,10},{9,11},{10,... | collective-permute-start | bytes 294920 | tf_op jit(solution)/shard_map/ppermute | solution.py:419
  56.3 0.2 collective-permute-start.4
  56.5 2.1 %collective-permute-start.5 = (bf16[128,384]{1,0:T(8,128)(2,1)}, bf16[128,384]{1,0:T(8,128)(2,1)S(1)}, u32[]{:S(2)}, u32[]{:S(2)}) collective-permute-start(bf16[128,384]{1,0:T(8,128)(2,1)} %mix.1.mine), channel_id=1, source_target_pairs={{0,6},{1,7},{2,0},{3,1},{4,2},{5,3},{6,4},{7,5},{8,14},{9,15},{10,... | collective-permute-start | bytes 294920 | tf_op jit(solution)/shard_map/ppermute | solution.py:419
  58.7 2.1 %collective-permute-start.8 = (bf16[66,768]{1,0:T(8,128)(2,1)S(1)}, bf16[66,768]{1,0:T(8,128)(2,1)S(1)}, u32[]{:S(2)}, u32[]{:S(2)}) collective-permute-start(bf16[66,768]{1,0:T(8,128)(2,1)S(1)} %pad_maximum_fusion.3), channel_id=1, source_target_pairs={{0,1},{1,0},{2,3},{3,2},{4,5},{5,4},{6,7},{7,6},{8,9},{9,8},{10,11... | collective-permute-start | bytes 304136 | tf_op jit(solution)/shard_map/ppermute | solution.py:407
  60.8 2.7 %collective-permute-done.3 = bf16[128,384]{1,0:T(8,128)(2,1)S(1)} collective-permute-done((bf16[128,384]{1,0:T(8,128)(2,1)}, bf16[128,384]{1,0:T(8,128)(2,1)S(1)}, u32[]{:S(2)}, u32[]{:S(2)}) %collective-permute-start.3) | collective-permute-done | bytes 98336 | tf_op jit(solution)/shard_map/ppermute | solution.py:419
  63.5 0.4 collective-permute-done.5
  63.9 0.9 %pad_maximum_fusion.refs_0_ = bf16[512,384]{1,0:T(8,128)(2,1)S(1)} fusion(bf16[128,384]{1,0:T(8,128)(2,1)S(1)} %collective-permute-done.5, bf16[128,384]{1,0:T(8,128)(2,1)S(1)} %collective-permute-done.4, bf16[128,384]{1,0:T(8,128)(2,1)S(1)} %collective-permute-done.3, bf16[128,384]{1,0:T(8,128)(2,1)} %mix.1.mine), kind=kLoop, calls=%fused_computation | loop fusion | flops 1572864 | bytes 786432 | tf_op jit(solution)/shard_map/concatenate | solution.py:422
  64.9 1.0 %collective-permute-start.6 = (bf16[512,384]{1,0:T(8,128)(2,1)S(1)}, bf16[512,384]{1,0:T(8,128)(2,1)S(1)}, u32[]{:S(2)}, u32[]{:S(2)}) collective-permute-start(bf16[512,384]{1,0:T(8,128)(2,1)S(1)} %pad_maximum_fusion.refs_0_), channel_id=1, source_target_pairs={{0,1},{1,0},{2,3},{3,2},{4,5},{5,4},{6,7},{7,6},{8,9},{9,8},{10,11... | collective-permute-start | bytes 1179656 | tf_op jit(solution)/shard_map/ppermute | solution.py:407
  65.9 0.6 copy-done.10
  66.5 3.3 %copy-done.11 = bf16[3,3,3,384,384]{4,3,2,1,0:T(8,128)(2,1)S(1)} copy-done((bf16[3,3,3,384,384]{4,3,2,1,0:T(8,128)(2,1)S(1)}, bf16[3,3,3,384,384]{4,3,2,1,0:T(8,128)(2,1)}, u32[]{:S(2)}) %copy-start.11) | copy-done | bytes 7962648
  69.8 12.2 %backward.1 = bf16[64,2,8,384]{3,2,1,0:T(8,128)(2,1)} custom-call(s32[2]{0:T(128)S(1)} %copy-done.10, bf16[64,8,768]{2,1,0:T(8,128)(2,1)S(1)} %get-tuple-element.11.grad, bf16[2,8,768]{2,1,0:T(8,128)(2,1)S(1)} %collective-permute-done.7.rim, bf16[66,768]{1,0:T(8,128)(2,1)S(1)} %collective-permute-done.8.from_core, ...), custom_call_target="tpu_custom_call" | custom-call | flops 5435817984 | bytes 12582912 | tf_op jit(solution)/shard_map/backward/pallas_call | solution.py:289
  82.0 5.1 %attend.1 = bf16[8,2,8,384]{3,2,1,0:T(8,128)(2,1)} custom-call(s32[8,1]{1,0:T(8,128)S(1)} %copy.13.labels, bf16[128,384]{1,0:T(8,128)(2,1)S(1)} %copy-done, bf16[512,384]{1,0:T(8,128)(2,1)S(1)} %pad_maximum_fusion.refs_0_, bf16[512,384]{1,0:T(8,128)(2,1)S(1)} %collective-permute-done.6.refs_1_, bf16[384,384]{1,0:T(8,128)(2,1)S(1)} %copy-done.1, ...), custom_call_target="tpu_custom_call" | custom-call | tf_op jit(solution)/shard_map/attend/pallas_call | solution.py:387
  (49 shorter events, 0.4 us)
Async XLA Ops:
  1.4 6.9 %collective-permute-start = (bf16[2,2,8,384]{3,2,1,0:T(8,128)(2,1)S(1)}, bf16[2,2,8,384]{3,2,1,0:T(8,128)(2,1)S(1)}, u32[]{:S(2)}, u32[]{:S(2)}) collective-permute-start(bf16[2,2,8,384]{3,2,1,0:T(8,128)(2,1)S(1)} %slice.6), channel_id=1, source_target_pairs={{0,8},{8,16},{16,24},{24,32},{32,40},{40,48},{48,56},{56,64},{64,7... | collective-permute-start | bytes 73736 | tf_op jit(solution)/shard_map/ppermute | solution.py:400
  8.4 6.4 %collective-permute-start.2 = (bf16[66,768]{1,0:T(8,128)(2,1)S(1)}, bf16[66,768]{1,0:T(8,128)(2,1)S(1)}, u32[]{:S(2)}, u32[]{:S(2)}) collective-permute-start(bf16[66,768]{1,0:T(8,128)(2,1)S(1)} %pad_maximum_fusion.2), channel_id=1, source_target_pairs={{1,2},{3,4},{5,6},{2,1},{4,3},{6,5},{9,10},{11,12},{13,14},{10,9},... | collective-permute-start | bytes 304136 | tf_op jit(solution)/shard_map/ppermute | solution.py:413
  12.4 2.4 %collective-permute-start.1 = (bf16[66,768]{1,0:T(8,128)(2,1)S(1)}, bf16[66,768]{1,0:T(8,128)(2,1)S(1)}, u32[]{:S(2)}, u32[]{:S(2)}) collective-permute-start(bf16[66,768]{1,0:T(8,128)(2,1)S(1)} %pad_maximum_fusion.1), channel_id=1, source_target_pairs={{0,1},{1,0},{2,3},{3,2},{4,5},{5,4},{6,7},{7,6},{8,9},{9,8},{10,11... | collective-permute-start | bytes 304136 | tf_op jit(solution)/shard_map/ppermute | solution.py:407
  12.5 30.1 %copy-start.16 = (s32[8,1]{0,1:T(1,128)S(1)}, s32[8,1]{0,1:T(1,128)}, u32[]{:S(2)}) copy-start(s32[8,1]{0,1:T(1,128)} %param.18) | copy-start | bytes 100
  12.6 19.1 %copy-start.9 = (s32[2]{0:T(128)}, s32[2]{0:T(128)S(1)}, u32[]{:S(2)}) copy-start(s32[2]{0:T(128)S(1)} %pad_add_fusion.place) | copy-start | bytes 28
  14.8 1.1 %copy-start.5 = (bf16[64,2,8,384]{3,2,1,0:T(8,128)(2,1)S(1)}, bf16[64,2,8,384]{3,2,1,0:T(8,128)(2,1)}, u32[]{:S(2)}) copy-start(bf16[64,2,8,384]{3,2,1,0:T(8,128)(2,1)} %frames.1) | copy-start | bytes 2359300
  15.9 0.7 copy-start.8
  16.6 1.7 %copy-start.12 = (bf16[8,384,384]{2,1,0:T(8,128)(2,1)S(1)}, bf16[8,384,384]{2,1,0:T(8,128)(2,1)}, u32[]{:S(2)}) copy-start(bf16[8,384,384]{2,1,0:T(8,128)(2,1)} %down.1) | copy-start | bytes 7077892
  18.2 1.1 %copy-start.13 = (bf16[64,2,8,384]{3,2,1,0:T(8,128)(2,1)S(1)}, bf16[64,2,8,384]{3,2,1,0:T(8,128)(2,1)}, u32[]{:S(2)}) copy-start(bf16[64,2,8,384]{3,2,1,0:T(8,128)(2,1)} %out_grad.3) | copy-start | bytes 2359300
  19.4 46.5 %copy-start.14 = (bf16[64,2,8,384]{3,2,1,0:T(8,128)(2,1)S(1)}, bf16[64,2,8,384]{3,2,1,0:T(8,128)(2,1)}, u32[]{:S(2)}) copy-start(bf16[64,2,8,384]{3,2,1,0:T(8,128)(2,1)} %out_grad.3) | copy-start | bytes 2359300
  31.7 0.7 copy-start.6
  32.4 0.7 copy-start.7
  33.8 18.8 %all-to-all-start = ((f32[16,16,384]{2,1,0:T(8,128)}), f32[16,16,384]{2,1,0:T(8,128)S(1)}, u32[]{:S(2)}, u32[]{:S(2)}) async-start(f32[16,16,384]{2,1,0:T(8,128)} %broadcast_in_dim.2), calls=%async_computation | async-start | bytes 786432 | tf_op jit(solution)/shard_map/all_to_all | solution.py:457
  41.3 7.5 %collective-permute-start.7 = (bf16[2,8,768]{2,1,0:T(8,128)(2,1)S(1)}, bf16[2,8,768]{2,1,0:T(8,128)(2,1)S(1)}, u32[]{:S(2)}, u32[]{:S(2)}) collective-permute-start(bf16[2,8,768]{2,1,0:T(8,128)(2,1)S(1)} %slice.7), channel_id=1, source_target_pairs={{8,0},{16,8},{24,16},{32,24},{40,32},{48,40},{56,48},{64,56},{72,6... | collective-permute-start | bytes 73736 | tf_op jit(solution)/shard_map/ppermute | solution.py:400
  48.9 17.0 %collective-permute-start.9 = (bf16[66,768]{1,0:T(8,128)(2,1)S(1)}, bf16[66,768]{1,0:T(8,128)(2,1)S(1)}, u32[]{:S(2)}, u32[]{:S(2)}) collective-permute-start(bf16[66,768]{1,0:T(8,128)(2,1)S(1)} %pad_maximum_fusion.4), channel_id=1, source_target_pairs={{1,2},{3,4},{5,6},{2,1},{4,3},{6,5},{9,10},{11,12},{13,14},{10,9},... | collective-permute-start | bytes 304136 | tf_op jit(solution)/shard_map/ppermute | solution.py:413
  52.6 0.7 copy-start.15
  55.3 8.2 %collective-permute-start.3 = (bf16[128,384]{1,0:T(8,128)(2,1)}, bf16[128,384]{1,0:T(8,128)(2,1)S(1)}, u32[]{:S(2)}, u32[]{:S(2)}) collective-permute-start(bf16[128,384]{1,0:T(8,128)(2,1)} %mix.1.mine), channel_id=1, source_target_pairs={{0,2},{1,3},{2,4},{3,5},{4,6},{5,7},{6,0},{7,1},{8,10},{9,11},{10,... | collective-permute-start | bytes 294920 | tf_op jit(solution)/shard_map/ppermute | solution.py:419
  56.3 7.3 %collective-permute-start.4 = (bf16[128,384]{1,0:T(8,128)(2,1)}, bf16[128,384]{1,0:T(8,128)(2,1)S(1)}, u32[]{:S(2)}, u32[]{:S(2)}) collective-permute-start(bf16[128,384]{1,0:T(8,128)(2,1)} %mix.1.mine), channel_id=1, source_target_pairs={{0,4},{1,5},{2,6},{3,7},{4,0},{5,1},{6,2},{7,3},{8,12},{9,13},{10,... | collective-permute-start | bytes 294920 | tf_op jit(solution)/shard_map/ppermute | solution.py:419
  56.5 7.4 %collective-permute-start.5 = (bf16[128,384]{1,0:T(8,128)(2,1)}, bf16[128,384]{1,0:T(8,128)(2,1)S(1)}, u32[]{:S(2)}, u32[]{:S(2)}) collective-permute-start(bf16[128,384]{1,0:T(8,128)(2,1)} %mix.1.mine), channel_id=1, source_target_pairs={{0,6},{1,7},{2,0},{3,1},{4,2},{5,3},{6,4},{7,5},{8,14},{9,15},{10,... | collective-permute-start | bytes 294920 | tf_op jit(solution)/shard_map/ppermute | solution.py:419
  58.7 7.2 %collective-permute-start.8 = (bf16[66,768]{1,0:T(8,128)(2,1)S(1)}, bf16[66,768]{1,0:T(8,128)(2,1)S(1)}, u32[]{:S(2)}, u32[]{:S(2)}) collective-permute-start(bf16[66,768]{1,0:T(8,128)(2,1)S(1)} %pad_maximum_fusion.3), channel_id=1, source_target_pairs={{0,1},{1,0},{2,3},{3,2},{4,5},{5,4},{6,7},{7,6},{8,9},{9,8},{10,11... | collective-permute-start | bytes 304136 | tf_op jit(solution)/shard_map/ppermute | solution.py:407
  64.9 17.1 %copy-start = (bf16[128,384]{1,0:T(8,128)(2,1)S(1)}, bf16[128,384]{1,0:T(8,128)(2,1)}, u32[]{:S(2)}) copy-start(bf16[128,384]{1,0:T(8,128)(2,1)} %mix.1.mine) | copy-start | bytes 294916
  64.9 17.1 %copy-start.1 = (bf16[384,384]{1,0:T(8,128)(2,1)S(1)}, bf16[384,384]{1,0:T(8,128)(2,1)}, u32[]{:S(2)}) copy-start(bf16[384,384]{1,0:T(8,128)(2,1)} %refs_2_.1) | copy-start | bytes 884740
  64.9 17.1 %copy-start.2 = (bf16[384,384]{1,0:T(8,128)(2,1)S(1)}, bf16[384,384]{1,0:T(8,128)(2,1)}, u32[]{:S(2)}) copy-start(bf16[384,384]{1,0:T(8,128)(2,1)} %refs_3_.1) | copy-start | bytes 884740
  64.9 17.1 %copy-start.3 = (bf16[384,384]{1,0:T(8,128)(2,1)S(1)}, bf16[384,384]{1,0:T(8,128)(2,1)}, u32[]{:S(2)}) copy-start(bf16[384,384]{1,0:T(8,128)(2,1)} %refs_4_.1) | copy-start | bytes 884740
  64.9 17.1 %copy-start.4 = (bf16[384,384]{1,0:T(8,128)(2,1)S(1)}, bf16[384,384]{1,0:T(8,128)(2,1)}, u32[]{:S(2)}) copy-start(bf16[384,384]{1,0:T(8,128)(2,1)} %refs_5_.1) | copy-start | bytes 884740
  64.9 17.0 %collective-permute-start.6 = (bf16[512,384]{1,0:T(8,128)(2,1)S(1)}, bf16[512,384]{1,0:T(8,128)(2,1)S(1)}, u32[]{:S(2)}, u32[]{:S(2)}) collective-permute-start(bf16[512,384]{1,0:T(8,128)(2,1)S(1)} %pad_maximum_fusion.refs_0_), channel_id=1, source_target_pairs={{0,1},{1,0},{2,3},{3,2},{4,5},{5,4},{6,7},{7,6},{8,9},{9,8},{10,11... | collective-permute-start | bytes 1179656 | tf_op jit(solution)/shard_map/ppermute | solution.py:407
  65.9 0.6 copy-start.10
  66.5 3.3 %copy-start.11 = (bf16[3,3,3,384,384]{4,3,2,1,0:T(8,128)(2,1)S(1)}, bf16[3,3,3,384,384]{4,3,2,1,0:T(8,128)(2,1)}, u32[]{:S(2)}) copy-start(bf16[3,3,3,384,384]{4,3,2,1,0:T(8,128)(2,1)} %weight.3) | copy-start | bytes 23887876
where the time goes:
time: 87.7 us; the launch traced here: 87.1 us
  Pallas kernels  31.6 us (36%)
  starting transfers between devices  26.9 us (31%)
  local copies, waits for them, and re-layouts  15.1 us (17%)
  waiting for transfers between devices  11.4 us (13%)
  other arithmetic  1.12 us (1%)
  between operations  1 us (1%)
    pallas_call x1, Pallas kernels, forward(): pl.pallas_call(forward_kernel, out_shape=(jax.ShapeDtypeStruct((lat, 16,...  12.3 us
    pallas_call x1, Pallas kernels, backward(): pl.pallas_call(backward_kernel, out_shape=jax.ShapeDtypeStruct(out_grad.s...  12.2 us
    unnamed x41, local copies, waits for them, and re-layouts  10.7 us
    ppermute x2, starting transfers between devices, with_chip(): return lax.ppermute(value, 'scene', pairs + [(b, a) for a, b in pairs])  7.62 us
    all_to_all x1, starting transfers between devices, per_device(): lax.all_to_all(jnp.broadcast_to(tail[None], (peers, *tail.shape)), 'tm',...  7.47 us
    ppermute x2, waiting for transfers between devices, shifted(): lax.ppermute(value, axis, [(i, i + steps) for i in range(count) if 0 <= i...  6.1 us
    ppermute x2, starting transfers between devices, shifted(): lax.ppermute(value, axis, [(i, i + steps) for i in range(count) if 0 <= i...  5.31 us
    pallas_call x1, Pallas kernels, attend(): pl.pallas_call(attend_kernel, out_shape=jax.ShapeDtypeStruct((labels.shap...  5.1 us
  transfers between devices with their start and end apart: 11, of which 4 were waited for; matrix products, arithmetic and copies ran while one was open for 5% of the time, Pallas kernels for 16%

commit v1 on v0

v1 whole, which is shorter than its diff:
```python
import math

import jax
import jax.numpy as jnp
from jax import lax
from jax.experimental import pallas as pl
from jax.experimental.pallas import tpu as pltpu
from jax.sharding import PartitionSpec as P

HEAD = 64
BF16 = jnp.bfloat16
F32 = jnp.float32
VMEM = pl.BlockSpec(memory_space=pltpu.VMEM)
SMEM = pl.BlockSpec(memory_space=pltpu.SMEM)
ANY = pl.BlockSpec(memory_space=pl.ANY)
NT = (((1,), (1,)), ((), ()))
NN = (((1,), (0,)), ((), ()))

SIDES = (1, 0, 2)


def dot(a, b, dims=NN):
    return lax.dot_general(a, b, dims, preferred_element_type=F32)


def weight_copies(weight_ref, folded, sems, back):
    chans = weight_ref.shape[-1]
    copies = []
    for k, side in enumerate(SIDES):
        for off in range(3):
            for h_in in range(2):
                for h_out in range(2):
                    row, col = h_in * chans, h_out * chans
                    if back:
                        col += 2 * chans * off
                    else:
                        row += 2 * chans * off
                    copies.append(
                        pltpu.make_async_copy(
                            weight_ref.at[
                                2 - off if back else off,
                                h_in - h_out + 1,
                                2 - side if back else side,
                            ],
                            folded.at[k, pl.ds(row, chans), pl.ds(col, chans)],
                            sems.at[k, 4 * off + 2 * h_in + h_out],
                        )
                    )
    return [copies[12 * k : 12 * (k + 1)] for k in range(3)]


def store_pairs(values_of, sides, count, even, odd):
    before = None
    for t in range(count):
        now = values_of(t)
        for at, s in enumerate(sides):
            if t % 2 == 1:
                pair = jnp.concatenate([before[at], now[at]], axis=0).astype(BF16)
                even[s, 8 * (t - 1) : 8 * (t + 1), :] = pair
            elif t > 0:
                pair = jnp.concatenate([before[at], now[at]], axis=0).astype(BF16)
                odd[s, 8 * (t - 2) : 8 * t, :] = pair
        before = now


def build_centre(frame_of, count, even, odd):
    store_pairs(lambda t: (frame_of(t).astype(F32),), (1,), count, even, odd)


def build_sides(frame_of, low_of, high_of, count, even, odd):
    width = even.shape[2]
    sub = lax.broadcasted_iota(jnp.int32, (8, width), 0)

    def both(t):
        own = frame_of(t).astype(F32)
        left = jnp.where(sub == 0, jnp.broadcast_to(low_of(t), (8, width)), pltpu.roll(own, 1, 0))
        right = jnp.where(sub == 7, jnp.broadcast_to(high_of(t), (8, width)), pltpu.roll(own, 7, 0))
        return left, right

    store_pairs(both, (0, 2), count, even, odd)


def window(side, even, odd, rows, extra=None):
    parts = [even[side, 0:rows, :], odd[side, 0:rows, :], even[side, 16 : 16 + rows, :]]
    if extra is not None:
        parts = [jnp.concatenate([part, extra(side, off)], axis=0) for off, part in enumerate(parts)]
    return jnp.concatenate(parts, axis=1)


def pack_kernel(place, frames, out_grad, before, after, core_out, chip_out, wide_f, wide_g):
    count = frames.shape[0]
    chans = frames.shape[3]
    lanes = chans // 128
    for t in range(count + 4):
        for h in range(2):
            if t < 2:
                value = before[t, h]
            elif t < count + 2:
                value = frames[t - 2, h]
            else:
                value = after[t - count - 2, h]
            value = value.astype(F32)
            for k in range(lanes):
                wide_f[lanes * h + k, 8 * t : 8 * (t + 1), :] = value[:, 128 * k : 128 * (k + 1)]
    for t in range(count + 2):
        for h in range(2):
            value = (out_grad[t, h] if t < count else after[t - count + 2, h]).astype(F32)
            for k in range(lanes):
                wide_g[lanes * h + k, 8 * t : 8 * (t + 1), :] = value[:, 128 * k : 128 * (k + 1)]
    even_core = place[1] == 0

    def column(source, at, rows):
        return jnp.concatenate(
            [source[k, pl.ds(at, rows, 8), :] for k in range(2 * lanes)], axis=1
        )

    def packed(first, second, grad):
        return jnp.concatenate(
            [
                column(wide_f, first, count + 4),
                column(wide_f, second, count + 4),
                column(wide_g, grad, count + 2),
                jnp.zeros((6, 2 * chans), F32),
            ],
            axis=0,
        )

    left = packed(0, 1, 0)
    right = packed(6, 7, 7)
    core_out[...] = jnp.where(even_core, right, left).astype(BF16)
    chip_out[...] = jnp.where(even_core, left, right).astype(BF16)


def pack(place, frames, out_grad, before, after):
    count, _, cols, chans = frames.shape
    rows = 3 * count + 16
    return pl.pallas_call(
        pack_kernel,
        out_shape=[jax.ShapeDtypeStruct((rows, 2 * chans), BF16)] * 2,
        in_specs=[SMEM] + [VMEM] * 4,
        out_specs=[VMEM] * 2,
        scratch_shapes=[
            pltpu.VMEM((2 * chans // 128, cols * (count + 4), 128), F32),
            pltpu.VMEM((2 * chans // 128, cols * (count + 2), 128), F32),
        ],
        compiler_params=pltpu.CompilerParams(vmem_limit_bytes=56 * 2**20),
        name="pack",
    )(place, frames, out_grad, before, after)


def forward_kernel(
    place,
    lengths,
    frames,
    before,
    after,
    core_sent,
    chip_sent,
    core_got,
    chip_got,
    out_grad,
    weight,
    down,
    latent_out,
    sums_out,
    tail_out,
    low_out,
    high_out,
    grad_out,
    block,
    grad_block,
    grad_done,
    down_block,
    own_low,
    own_high,
    low,
    high,
    even,
    odd,
    folded,
    total,
    act,
    sems,
    weight_sems,
):
    chans = frames.shape[-1]
    count = frames.shape[0]
    ahead = count + 2
    rows = 8 * ahead
    first = [
        pltpu.make_async_copy(frames.at[:, h], block.at[:, :, pl.ds(h * chans, chans)], sems.at[h])
        for h in range(2)
    ]
    for copy in first:
        copy.start()
    copies = weight_copies(weight, folded, weight_sems, False)
    for copy in copies[0]:
        copy.start()
    later = [
        pltpu.make_async_copy(
            out_grad.at[:, h], grad_block.at[:, :, pl.ds(h * chans, chans)], sems.at[2 + h]
        )
        for h in range(2)
    ] + [pltpu.make_async_copy(down, down_block, sems.at[4])]
    for group in copies[1:]:
        for copy in group:
            copy.start()
    for copy in later:
        copy.start()
    even_core = place[1] == 0

    def pick(core, chip, at_low, at_high):
        core, chip = core[...].astype(F32), chip[...].astype(F32)
        at_low[...] = jnp.where(even_core, chip, core)
        at_high[...] = jnp.where(even_core, core, chip)

    pick(core_sent, chip_sent, own_low, own_high)
    pick(core_got, chip_got, low, high)
    for copy in first:
        copy.wait()

    def frame_of(t):
        if 2 <= t < count + 2:
            return block[t - 2]
        part = (lambda h: before[t, h]) if t < 2 else (lambda h: after[t - count - 2, h])
        return jnp.concatenate([part(0).astype(F32), part(1).astype(F32)], axis=1)

    span = count + 4

    def rim(side, off):
        left = ((low, 0), (low, span), (own_low, 0))[side]
        right = ((own_high, span), (high, 0), (high, span))[side]
        return jnp.concatenate(
            [ref[at + off : at + off + ahead + 6, :] for ref, at in (left, right)], axis=0
        ).astype(BF16)

    build_centre(frame_of, span, even, odd)
    for copy in copies[0]:
        copy.wait()
    total[...] = dot(window(1, even, odd, rows, rim), folded[0])
    build_sides(
        frame_of,
        lambda t: low[span + t : span + t + 1, :],
        lambda t: high[t : t + 1, :],
        span,
        even,
        odd,
    )
    for k in (1, 2):
        for copy in copies[k]:
            copy.wait()
        total[...] += dot(window(SIDES[k], even, odd, rows, rim), folded[k])
    for copy in later:
        copy.wait()

    def gates(pre):
        gate = 1.0 / (1.0 + jnp.exp(-pre))
        return gate, gate * (1.0 + pre * (1.0 - gate))

    for j in range(count // 8):
        pre = total[64 * j : 64 * (j + 1), :]
        gate, slope = gates(pre)
        own = block[8 * j : 8 * (j + 1)].astype(F32)
        act[j] = own + (pre * gate).reshape(own.shape)
        grad = grad_block[8 * j : 8 * (j + 1)].astype(F32) * slope.reshape(own.shape)
        grad_done[8 * j : 8 * (j + 1)] = grad.astype(BF16)
    for t in range(2):
        at = 8 * (count + t)
        _, slope = gates(total[at : at + 8, :])
        grad = jnp.concatenate([after[2 + t, 0].astype(F32), after[2 + t, 1].astype(F32)], axis=1)
        grad_done[count + t] = (grad * slope).astype(BF16)
    write = pltpu.make_async_copy(grad_done, grad_out, sems.at[5])
    write.start()
    for at, (source, target) in enumerate(((low, low_out), (high, high_out))):
        base = rows + at * (ahead + 6)
        _, slope = gates(total[base : base + ahead + 6, :])
        target[...] = slope * source[2 * span : 2 * span + ahead + 6, :]

    latent = jnp.zeros((2 * count, chans), F32)
    for k in range(8):
        lhs = jnp.concatenate(
            [
                act[:, k, :, h * chans : (h + 1) * chans].reshape(count, chans)
                for h in range(2)
            ],
            axis=0,
        ).astype(BF16)
        latent = latent + dot(lhs, down_block[k])
    latent = latent.astype(BF16).astype(F32)
    rounded = [
        jnp.concatenate([latent[8 * j : 8 * j + 8], latent[count + 8 * j : count + 8 * j + 8]], 0)
        for j in range(count // 8)
    ]
    running = jnp.zeros_like(rounded[0])
    for j in range(count // 8):
        now = place[0] * (count // 8) + j
        start = jnp.int32(0)
        begins = jnp.int32(0)
        for k in range(lengths.shape[0]):
            begins = jnp.where(start == now, 1, begins)
            start = start + lengths[k]
        running = jnp.where(begins > 0, rounded[j], running + rounded[j])
        sums_out[j] = running
        latent_out[j] = rounded[j]
    for k in range(tail_out.shape[0]):
        tail_out[k] = running
    write.wait()


def forward(peers, place, lengths, frames, before, after, columns, out_grad, weight, down):
    count, _, cols, chans = frames.shape
    wide = 2 * chans
    lat = count // 8
    ahead = count + 2
    rows = cols * ahead
    received = columns[0].shape
    return pl.pallas_call(
        forward_kernel,
        out_shape=(
            jax.ShapeDtypeStruct((lat, 16, chans), F32),
            jax.ShapeDtypeStruct((lat, 16, chans), F32),
            jax.ShapeDtypeStruct((peers, 16, chans), F32),
            jax.ShapeDtypeStruct((ahead + 6, wide), F32),
            jax.ShapeDtypeStruct((ahead + 6, wide), F32),
            jax.ShapeDtypeStruct((ahead, cols, wide), BF16),
        ),
        in_specs=[SMEM, SMEM, ANY] + [VMEM] * 6 + [ANY] * 3,
        out_specs=[VMEM] * 5 + [ANY],
        scratch_shapes=[
            pltpu.VMEM((count, cols, wide), BF16),
            pltpu.VMEM((count, cols, wide), BF16),
            pltpu.VMEM((ahead, cols, wide), BF16),
            pltpu.VMEM(down.shape, BF16),
            pltpu.VMEM(received, F32),
            pltpu.VMEM(received, F32),
            pltpu.VMEM(received, F32),
            pltpu.VMEM(received, F32),
            pltpu.VMEM((3, rows + 16, wide), BF16),
            pltpu.VMEM((3, rows, wide), BF16),
            pltpu.VMEM((3, 3 * wide, wide), BF16),
            pltpu.VMEM((rows + 2 * (ahead + 6), wide), F32),
            pltpu.VMEM((lat, 8, cols, wide), F32),
            pltpu.SemaphoreType.DMA((6,)),
            pltpu.SemaphoreType.DMA((3, 12)),
        ],
        compiler_params=pltpu.CompilerParams(vmem_limit_bytes=60 * 2**20),
        cost_estimate=pl.CostEstimate(
            flops=2 * 9 * rows * wide * wide, bytes_accessed=16 * 2**20, transcendentals=rows * wide
        ),
        name="forward",
    )(place, lengths, frames, before, after, *columns, out_grad, weight, down)


def backward_kernel(
    grad,
    low,
    high,
    out_grad,
    weight,
    result,
    block,
    source,
    done,
    even,
    odd,
    folded,
    total,
    sems,
    weight_sems,
):
    count, _, cols, chans = out_grad.shape
    first = pltpu.make_async_copy(grad, block, sems.at[0])
    first.start()
    copies = weight_copies(weight, folded, weight_sems, True)
    for group in copies:
        for copy in group:
            copy.start()
    later = pltpu.make_async_copy(out_grad, source, sems.at[1])
    later.start()
    first.wait()

    def frame_of(t):
        return block[t]

    rows = 8 * count
    build_centre(frame_of, count + 2, even, odd)
    for copy in copies[0]:
        copy.wait()
    total[...] = dot(window(1, even, odd, rows), folded[0], NT)
    build_sides(
        frame_of,
        lambda t: low[t : t + 1, :],
        lambda t: high[t : t + 1, :],
        count + 2,
        even,
        odd,
    )
    for copy in copies[1]:
        copy.wait()
    total[...] += dot(window(SIDES[1], even, odd, rows), folded[1], NT)
    for copy in copies[2]:
        copy.wait()
    later.wait()
    writes = []
    step = count // 4
    for j in range(4):
        at = slice(8 * step * j, 8 * step * (j + 1))
        lhs = jnp.concatenate(
            [
                even[2, 8 * step * j : 8 * step * (j + 1), :],
                odd[2, 8 * step * j : 8 * step * (j + 1), :],
                even[2, 16 + 8 * step * j : 16 + 8 * step * (j + 1), :],
            ],
            axis=1,
        )
        part = total[at, :] + dot(lhs, folded[2], NT)
        for h in range(2):
            mine = part[:, h * chans : (h + 1) * chans].reshape(step, cols, chans)
            done[step * j : step * (j + 1), h] = (
                source[step * j : step * (j + 1), h].astype(F32) + mine
            ).astype(BF16)
        write = pltpu.make_async_copy(
            done.at[pl.ds(step * j, step)], result.at[pl.ds(step * j, step)], sems.at[2 + j]
        )
        write.start()
        writes.append(write)
    for write in writes:
        write.wait()


def backward(grad, low, high, out_grad, weight):
    count, _, cols, chans = out_grad.shape
    rows, wide = count * cols, 2 * chans
    return pl.pallas_call(
        backward_kernel,
        out_shape=jax.ShapeDtypeStruct(out_grad.shape, BF16),
        in_specs=[ANY, VMEM, VMEM, ANY, ANY],
        out_specs=ANY,
        scratch_shapes=[
            pltpu.VMEM(grad.shape, BF16),
            pltpu.VMEM(out_grad.shape, BF16),
            pltpu.VMEM(out_grad.shape, BF16),
            pltpu.VMEM((3, rows + 16, wide), BF16),
            pltpu.VMEM((3, rows, wide), BF16),
            pltpu.VMEM((3, wide, 3 * wide), BF16),
            pltpu.VMEM((rows, wide), F32),
            pltpu.SemaphoreType.DMA((6,)),
            pltpu.SemaphoreType.DMA((3, 12)),
        ],
        compiler_params=pltpu.CompilerParams(vmem_limit_bytes=60 * 2**20),
        cost_estimate=pl.CostEstimate(
            flops=2 * 9 * rows * wide * wide, bytes_accessed=12 * 2**20, transcendentals=0
        ),
        name="backward",
    )(grad, low, high, out_grad, weight)


def mix_kernel(place, lengths, latent, sums, tails, mixed):
    lat = latent.shape[0]
    peers = tails.shape[0]
    me = place[0]
    starts = [jnp.int32(0)]
    for k in range(lengths.shape[0] - 1):
        starts.append(starts[-1] + lengths[k])
    opened = jnp.int32(0)
    for start in starts:
        opened = jnp.where(start < me * lat, jnp.maximum(start, opened), opened)
    carried = jnp.zeros(latent.shape[1:], F32)
    for k in range(peers):
        counts = jnp.logical_and(k < me, (k + 1) * lat > opened)
        carried = carried + jnp.where(counts, tails[k], 0.0)
    for j in range(lat):
        now = me * lat + j
        begin = jnp.int32(0)
        for start in starts:
            begin = jnp.where(start <= now, jnp.maximum(start, begin), begin)
        shot = sums[j] + jnp.where(begin < me * lat, carried, 0.0)
        length = jnp.full(shot.shape, now - begin + 1, jnp.int32).astype(F32)
        mixed[16 * j : 16 * (j + 1), :] = (latent[j] + shot / length).astype(BF16)


def mix(place, lengths, latent, sums, tails):
    return pl.pallas_call(
        mix_kernel,
        out_shape=jax.ShapeDtypeStruct((latent.shape[0] * 16, latent.shape[2]), BF16),
        in_specs=[SMEM, SMEM, VMEM, VMEM, VMEM],
        out_specs=VMEM,
        name="mix",
    )(place, lengths, latent, sums, tails)


def attend_kernel(labels, mine, *refs):
    pieces, (w_query, w_key, w_value, w_out, result, keys, values) = refs[:-7], refs[-7:]
    tokens, chans = mine.shape
    lat = labels.shape[0]
    per = tokens // lat
    at = 0
    for piece in pieces:
        block = piece[...]
        size = block.shape[0]
        keys[at : at + size, :] = dot(block, w_key[...]).astype(BF16)
        values[at : at + size, :] = dot(block, w_value[...]).astype(BF16)
        at += size
    query = (dot(mine[...], w_query[...]).astype(BF16) * BF16(1.0 / math.sqrt(HEAD))).astype(BF16)
    row = lax.broadcasted_iota(jnp.int32, (tokens, 1), 0) // per
    col = (lax.broadcasted_iota(jnp.int32, (1, tokens), 1) % tokens) // per
    row_label = jnp.zeros((tokens, 1), jnp.int32)
    col_label = jnp.zeros((1, tokens), jnp.int32)
    for j in range(lat):
        row_label = jnp.where(row == j, labels[j, 0], row_label)
        col_label = jnp.where(col == j, labels[j, 0], col_label)
    same = jnp.logical_and(row_label == col_label, col <= row)
    bias = jnp.where(same, 0.0, -1e30).astype(F32)
    bias = jnp.concatenate([bias] * (at // tokens), axis=1)
    outs = []
    for head in range(chans // HEAD):
        lanes = slice(head * HEAD, (head + 1) * HEAD)
        scores = dot(query[:, lanes], keys[:, lanes], NT) + bias
        top = jnp.max(scores, axis=1, keepdims=True)
        expo = jnp.exp(scores - top)
        norm = jnp.sum(expo, axis=1, keepdims=True)
        outs.append(dot(expo.astype(BF16), values[:, lanes]) / norm)
    heads = jnp.concatenate(outs, axis=1).astype(BF16)
    final = mine[...].astype(F32) + dot(heads, w_out[...])
    for j in range(lat):
        for h in range(2):
            at = per * j + 8 * h
            result[j, h] = final[at : at + 8].astype(BF16)


def attend(labels, mine, pieces, w_query, w_key, w_value, w_out):
    tokens, chans = mine.shape
    total = sum(piece.shape[0] for piece in pieces)
    return pl.pallas_call(
        attend_kernel,
        out_shape=jax.ShapeDtypeStruct((labels.shape[0], 2, 8, chans), BF16),
        in_specs=[SMEM] + [VMEM] * (5 + len(pieces)),
        out_specs=VMEM,
        scratch_shapes=[pltpu.VMEM((total, chans), BF16), pltpu.VMEM((total, chans), BF16)],
        compiler_params=pltpu.CompilerParams(vmem_limit_bytes=32 * 2**20),
        name="attend",
    )(labels, mine, *pieces, w_query, w_key, w_value, w_out)


def shifted(value, axis, steps):
    count = lax.axis_size(axis)
    return lax.ppermute(
        value, axis, [(i, i + steps) for i in range(count) if 0 <= i + steps < count]
    )


def with_core(value):
    count = lax.axis_size("scene")
    return lax.ppermute(value, "scene", [(i, i ^ 1) for i in range(count)])


def with_chip(value):
    count = lax.axis_size("scene")
    pairs = [(i, i + 1) for i in range(1, count - 1, 2)]
    return lax.ppermute(value, "scene", pairs + [(b, a) for a, b in pairs])


def gathered(value):
    count = lax.axis_size("scene")
    chips = [
        lax.ppermute(value, "scene", [(i, (i + 2 * k) % count) for i in range(count)])
        for k in range(1, count // 2)
    ]
    own = jnp.concatenate([value, *chips], axis=0)
    return [own, with_core(own)]


def per_device(
    frames,
    conv_weight,
    down_weight,
    w_query,
    w_key,
    w_value,
    w_out,
    shot_lengths,
    scene_label,
    out_grad,
):
    count = frames.shape[0]
    place = jnp.stack([lax.axis_index("tm"), lax.axis_index("scene") % 2]).astype(jnp.int32)
    before = shifted(frames[count - 2 :], "tm", 1)
    after = shifted(jnp.concatenate([frames[:2], out_grad[:2]], axis=0), "tm", -1)
    sent = pack(place, frames, out_grad, before, after)
    columns = (*sent, with_core(sent[0]), with_chip(sent[1]))
    latent, sums, tail, low, high, grad = forward(
        lax.axis_size("tm"),
        place,
        shot_lengths,
        frames,
        before,
        after,
        columns,
        out_grad,
        conv_weight,
        down_weight,
    )
    tails = lax.all_to_all(tail, "tm", 0, 0, tiled=True)
    mixed = mix(place, shot_lengths, latent, sums, tails)
    pieces = gathered(mixed)
    frame_grad = backward(grad, low, high, out_grad, conv_weight)
    latent_out = attend(scene_label, mixed, pieces, w_query, w_key, w_value, w_out)
    return (latent_out, frame_grad)


def solution(mesh):
    in_specs = (
        P("tm", None, "scene", None),
        P(),
        P(),
        P(),
        P(),
        P(),
        P(),
        P(),
        P("tm", None),
        P("tm", None, "scene", None),
    )
    out_specs = (P("tm", None, "scene", None), P("tm", None, "scene", None))
    return jax.shard_map(
        per_device, mesh=mesh, in_specs=in_specs, out_specs=out_specs, check_vma=False
    )
```

time: 87.7 us -> 102 us (1.16)
  blocking collectives: 0 us -> 18.8 us
  Pallas kernels: 31.6 us -> 48.4 us
  local copies, waits for them, and re-layouts: 15.1 us -> 3.58 us
  starting transfers between devices: 26.9 us -> 19.7 us
  waiting for transfers between devices: 11.4 us -> 8.19 us
    all_to_all x0 -> x1, blocking collectives: none -> 18.8 us  [per_device(): tails = lax.all_to_all(tail, 'tm', 0, 0, tiled=True)]
    unnamed x41 -> x21, local copies, waits for them, and re-layouts: 10.7 us -> 2.08 us
    pallas_call x1, Pallas kernels: 12.3 us -> 19.8 us  [forward(): pl.pallas_call(forward_kernel, out_shape=(jax.ShapeDtypeStruct((lat, 16,...]
    all_to_all x1 -> x0, starting transfers between devices: 7.47 us -> none  [per_device(): lax.all_to_all(jnp.broadcast_to(tail[None], (peers, *tail.shape)), 'tm',...]
    pallas_call x1, Pallas kernels: 12.2 us -> 18.7 us  [backward(): pl.pallas_call(backward_kernel, out_shape=jax.ShapeDtypeStruct(out_grad.s...]
    ppermute x2, waiting for transfers between devices: 6.1 us -> 0.31 us  [shifted(): lax.ppermute(value, axis, [(i, i + steps) for i in range(count) if 0 <= i...]
    ppermute x2 -> x1, starting transfers between devices: 7.62 us -> 3.22 us  [with_chip(): return lax.ppermute(value, 'scene', pairs + [(b, a) for a, b in pairs])]
    ppermute x2 -> x1, waiting for transfers between devices: 2.18 us -> 5.39 us  [with_chip(): return lax.ppermute(value, 'scene', pairs + [(b, a) for a, b in pairs])]
  transfers between devices with their start and end apart: 11 -> 8, of which waited for: 4 -> 4; matrix products, arithmetic and copies ran while one was open for 5% -> 1% of each run, Pallas kernels for 16% -> 18%
where the time goes in v1:
time: 102 us; the launch traced here: 101 us
  Pallas kernels  48.4 us (47%)
  starting transfers between devices  19.7 us (19%)
  blocking collectives  18.8 us (18%)
  waiting for transfers between devices  8.19 us (8%)
  local copies, waits for them, and re-layouts  3.58 us (4%)
  other arithmetic  1.55 us (2%)
    pallas_call x1, Pallas kernels, forward(): pl.pallas_call(forward_kernel, out_shape=(jax.ShapeDtypeStruct((lat, 16,...  19.8 us
    all_to_all x1, blocking collectives, per_device(): tails = lax.all_to_all(tail, 'tm', 0, 0, tiled=True)  18.8 us
    pallas_call x1, Pallas kernels, backward(): pl.pallas_call(backward_kernel, out_shape=jax.ShapeDtypeStruct(out_grad.s...  18.7 us
    ppermute x3, starting transfers between devices, gathered(): lax.ppermute(value, 'scene', [(i, (i + 2 * k) % count) for i in range(cou...  6.21 us
    ppermute x2, starting transfers between devices, shifted(): lax.ppermute(value, axis, [(i, i + steps) for i in range(count) if 0 <= i...  5.95 us
    ppermute x1, waiting for transfers between devices, with_chip(): return lax.ppermute(value, 'scene', pairs + [(b, a) for a, b in pairs])  5.39 us
    pallas_call x1, Pallas kernels, attend(): pl.pallas_call(attend_kernel, out_shape=jax.ShapeDtypeStruct((labels.shap...  5.09 us
    ppermute x2, starting transfers between devices, with_core(): return lax.ppermute(value, 'scene', [(i, i ^ 1) for i in range(count)])  4.34 us
  transfers between devices with their start and end apart: 8, of which 4 were waited for; matrix products, arithmetic and copies ran while one was open for 1% of the time, Pallas kernels for 18%

profile of v1, /device:TPU:1, one launch (start us, length us, event | category | flops | bytes accessed | tf_op | source)
XLA Modules:
  0.0 101.0 jit_solution(7813601836549538122)
XLA Ops:
  0.6 0.8 fusion
  1.4 0.7 slice.11
  2.1 1.3 %collective-permute-start.1 = (bf16[4,2,8,384]{3,2,1,0:T(8,128)(2,1)S(1)}, bf16[4,2,8,384]{3,2,1,0:T(8,128)(2,1)S(1)}, u32[]{:S(2)}, u32[]{:S(2)}) collective-permute-start(bf16[4,2,8,384]{3,2,1,0:T(8,128)(2,1)S(1)} %pad_maximum_fusion.1), channel_id=1, source_target_pairs={{8,0},{16,8},{24,16},{32,24},{40,32},{48,40},{56,48},{64,56},{72,6... | collective-permute-start | bytes 147464 | tf_op jit(solution)/shard_map/ppermute | solution.py:547
  3.4 4.7 %collective-permute-start = (bf16[2,2,8,384]{3,2,1,0:T(8,128)(2,1)S(1)}, bf16[2,2,8,384]{3,2,1,0:T(8,128)(2,1)S(1)}, u32[]{:S(2)}, u32[]{:S(2)}) collective-permute-start(bf16[2,2,8,384]{3,2,1,0:T(8,128)(2,1)S(1)} %get-tuple-element.19), channel_id=1, source_target_pairs={{0,8},{8,16},{16,24},{24,32},{32,40},{40,48},{48,56},{56,64},{64,7... | collective-permute-start | bytes 73736 | tf_op jit(solution)/shard_map/ppermute | solution.py:547
  8.1 0.6 pad_add_fusion.place
  8.7 0.3 collective-permute-done.before
  9.0 0.0 collective-permute-done.1.after
  9.0 0.6 copy-done.6
  9.7 0.6 copy-done.5
  10.3 2.8 %pack.1 = (bf16[208,768]{1,0:T(8,128)(2,1)}, bf16[208,768]{1,0:T(8,128)(2,1)}) custom-call(s32[2]{0:T(128)} %pad_add_fusion.place, bf16[64,2,8,384]{3,2,1,0:T(8,128)(2,1)} %frames.3, bf16[64,2,8,384]{3,2,1,0:T(8,128)(2,1)} %out_grad.5, bf16[2,2,8,384]{3,2,1,0:T(8,128)(2,1)} %copy-done.6, bf16[4,2,8,384]{3,2,1,0:T(8,128)(2,1)} %copy-done.5), custom_call_target="tpu_custom_call" | custom-call | tf_op jit(solution)/shard_map/pack/pallas_call | solution.py:137
  13.1 1.9 %collective-permute-start.2 = (bf16[208,768]{1,0:T(8,128)(2,1)}, bf16[208,768]{1,0:T(8,128)(2,1)S(1)}, u32[]{:S(2)}, u32[]{:S(2)}) collective-permute-start(bf16[208,768]{1,0:T(8,128)(2,1)} %get-tuple-element.10.core_sent), channel_id=1, source_target_pairs={{0,1},{1,0},{2,3},{3,2},{4,5},{5,4},{6,7},{7,6},{8,9},{9,8},{10,11... | collective-permute-start | bytes 958472 | tf_op jit(solution)/shard_map/ppermute | solution.py:554
  15.0 3.2 %collective-permute-start.3 = (bf16[208,768]{1,0:T(8,128)(2,1)}, bf16[208,768]{1,0:T(8,128)(2,1)S(1)}, u32[]{:S(2)}, u32[]{:S(2)}) collective-permute-start(bf16[208,768]{1,0:T(8,128)(2,1)} %get-tuple-element.11.chip_sent), channel_id=1, source_target_pairs={{1,2},{3,4},{5,6},{2,1},{4,3},{6,5},{9,10},{11,12},{13,14},{10,9},... | collective-permute-start | bytes 958472 | tf_op jit(solution)/shard_map/ppermute | solution.py:560
  18.2 0.0 collective-permute-done.2.core_got
  18.2 0.0 copy-start.8
  18.2 5.4 %collective-permute-done.3.chip_got = bf16[208,768]{1,0:T(8,128)(2,1)S(1)} collective-permute-done((bf16[208,768]{1,0:T(8,128)(2,1)}, bf16[208,768]{1,0:T(8,128)(2,1)S(1)}, u32[]{:S(2)}, u32[]{:S(2)}) %collective-permute-start.3) | collective-permute-done | bytes 319520 | tf_op jit(solution)/shard_map/ppermute | solution.py:560
  23.6 0.7 copy-done.9
  24.4 19.8 %forward.1 = (f32[8,16,384]{2,1,0:T(8,128)}, f32[8,16,384]{2,1,0:T(8,128)}, f32[16,16,384]{2,1,0:T(8,128)}, f32[72,768]{1,0:T(8,128)}, f32[72,768]{1,0:T(8,128)}, /*index=5*/bf16[66,8,768]{2,1,0:T(8,128)(2,1)}) custom-call(s32[2]{0:T(128)} %pad_add_fusion.place, s32[8]{0:T(128)} %lengths.3, bf16[64,2,8,384]{3,2,1,0:T(8,128)(2,1)} %frames.3, ...), custom_call_target="tpu_custom_call" | custom-call | flops 5605687296 | bytes 16777216 | tf_op jit(solution)/shard_map/forward/pallas_call | solution.py:317
  44.2 18.8 %all_to_all.5.tails = f32[16,16,384]{2,1,0:T(8,128)} all-to-all(f32[16,16,384]{2,1,0:T(8,128)} %get-tuple-element.14), channel_id=1, replica_groups=mesh['tm'=16,'scene'=8] {'tm'}, dimensions={0} | all-to-all | bytes 786432 | tf_op jit(solution)/shard_map/all_to_all | solution.py:603
  63.0 2.0 %mix.1.mine = bf16[128,384]{1,0:T(8,128)(2,1)} custom-call(s32[2]{0:T(128)} %pad_add_fusion.place, s32[8]{0:T(128)} %lengths.3, f32[8,16,384]{2,1,0:T(8,128)} %get-tuple-element.12.latent, f32[8,16,384]{2,1,0:T(8,128)} %get-tuple-element.13.sums, f32[16,16,384]{2,1,0:T(8,128)} %all_to_all.5.tails), custom_call_target="tpu_custom_call" | custom-call | tf_op jit(solution)/shard_map/mix/pallas_call | solution.py:483
  65.0 2.6 %collective-permute-start.4 = (bf16[128,384]{1,0:T(8,128)(2,1)}, bf16[128,384]{1,0:T(8,128)(2,1)S(1)}, u32[]{:S(2)}, u32[]{:S(2)}) collective-permute-start(bf16[128,384]{1,0:T(8,128)(2,1)} %mix.1.mine), channel_id=1, source_target_pairs={{0,2},{1,3},{2,4},{3,5},{4,6},{5,7},{6,0},{7,1},{8,10},{9,11},{10,... | collective-permute-start | bytes 294920 | tf_op jit(solution)/shard_map/ppermute | solution.py:566
  67.6 1.5 %collective-permute-start.5 = (bf16[128,384]{1,0:T(8,128)(2,1)}, bf16[128,384]{1,0:T(8,128)(2,1)S(1)}, u32[]{:S(2)}, u32[]{:S(2)}) collective-permute-start(bf16[128,384]{1,0:T(8,128)(2,1)} %mix.1.mine), channel_id=1, source_target_pairs={{0,4},{1,5},{2,6},{3,7},{4,0},{5,1},{6,2},{7,3},{8,12},{9,13},{10,... | collective-permute-start | bytes 294920 | tf_op jit(solution)/shard_map/ppermute | solution.py:566
  69.1 2.1 %collective-permute-start.6 = (bf16[128,384]{1,0:T(8,128)(2,1)}, bf16[128,384]{1,0:T(8,128)(2,1)S(1)}, u32[]{:S(2)}, u32[]{:S(2)}) collective-permute-start(bf16[128,384]{1,0:T(8,128)(2,1)} %mix.1.mine), channel_id=1, source_target_pairs={{0,6},{1,7},{2,0},{3,1},{4,2},{5,3},{6,4},{7,5},{8,14},{9,15},{10,... | collective-permute-start | bytes 294920 | tf_op jit(solution)/shard_map/ppermute | solution.py:566
  71.2 0.1 copy.12.labels
  71.3 0.0 collective-permute-done.4
  71.3 2.4 %collective-permute-done.5 = bf16[128,384]{1,0:T(8,128)(2,1)S(1)} collective-permute-done((bf16[128,384]{1,0:T(8,128)(2,1)}, bf16[128,384]{1,0:T(8,128)(2,1)S(1)}, u32[]{:S(2)}, u32[]{:S(2)}) %collective-permute-start.5) | collective-permute-done | bytes 98336 | tf_op jit(solution)/shard_map/ppermute | solution.py:566
  73.7 0.1 collective-permute-done.6
  73.8 0.9 pad_maximum_fusion.refs_0_
  74.7 2.5 %collective-permute-start.7 = (bf16[512,384]{1,0:T(8,128)(2,1)S(1)}, bf16[512,384]{1,0:T(8,128)(2,1)S(1)}, u32[]{:S(2)}, u32[]{:S(2)}) collective-permute-start(bf16[512,384]{1,0:T(8,128)(2,1)S(1)} %pad_maximum_fusion.refs_0_), channel_id=1, source_target_pairs={{0,1},{1,0},{2,3},{3,2},{4,5},{5,4},{6,7},{7,6},{8,9},{9,8},{10,11... | collective-permute-start | bytes 1179656 | tf_op jit(solution)/shard_map/ppermute | solution.py:554
  77.2 0.0 copy-start.4
  77.2 18.7 %backward.1 = bf16[64,2,8,384]{3,2,1,0:T(8,128)(2,1)} custom-call(bf16[66,8,768]{2,1,0:T(8,128)(2,1)} %get-tuple-element.15.grad, f32[72,768]{1,0:T(8,128)} %get-tuple-element.16.low, f32[72,768]{1,0:T(8,128)} %get-tuple-element.17.high, bf16[64,2,8,384]{3,2,1,0:T(8,128)(2,1)} %out_grad.5, bf16[3,3,3,384,384]{4,3,2,1,0:T(8,128)(2,1)} %weight.3), custom_call_target="tpu_custom_call" | custom-call | flops 5435817984 | bytes 12582912 | tf_op jit(solution)/shard_map/backward/pallas_call | solution.py:434
  95.9 0.0 collective-permute-done.7.refs_1_
  96.0 5.1 %attend.1 = bf16[8,2,8,384]{3,2,1,0:T(8,128)(2,1)} custom-call(s32[8,1]{1,0:T(8,128)S(1)} %copy.12.labels, bf16[128,384]{1,0:T(8,128)(2,1)S(1)} %copy-done, bf16[512,384]{1,0:T(8,128)(2,1)S(1)} %pad_maximum_fusion.refs_0_, bf16[512,384]{1,0:T(8,128)(2,1)S(1)} %collective-permute-done.7.refs_1_, bf16[384,384]{1,0:T(8,128)(2,1)S(1)} %copy-done.1, ...), custom_call_target="tpu_custom_call" | custom-call | tf_op jit(solution)/shard_map/attend/pallas_call | solution.py:534
  (16 shorter events, 0.0 us)
Async XLA Ops:
  2.1 6.9 %collective-permute-start.1 = (bf16[4,2,8,384]{3,2,1,0:T(8,128)(2,1)S(1)}, bf16[4,2,8,384]{3,2,1,0:T(8,128)(2,1)S(1)}, u32[]{:S(2)}, u32[]{:S(2)}) collective-permute-start(bf16[4,2,8,384]{3,2,1,0:T(8,128)(2,1)S(1)} %pad_maximum_fusion.1), channel_id=1, source_target_pairs={{8,0},{16,8},{24,16},{32,24},{40,32},{48,40},{56,48},{64,56},{72,6... | collective-permute-start | bytes 147464 | tf_op jit(solution)/shard_map/ppermute | solution.py:547
  3.4 5.6 %collective-permute-start = (bf16[2,2,8,384]{3,2,1,0:T(8,128)(2,1)S(1)}, bf16[2,2,8,384]{3,2,1,0:T(8,128)(2,1)S(1)}, u32[]{:S(2)}, u32[]{:S(2)}) collective-permute-start(bf16[2,2,8,384]{3,2,1,0:T(8,128)(2,1)S(1)} %get-tuple-element.19), channel_id=1, source_target_pairs={{0,8},{8,16},{16,24},{24,32},{32,40},{40,48},{48,56},{56,64},{64,7... | collective-permute-start | bytes 73736 | tf_op jit(solution)/shard_map/ppermute | solution.py:547
  9.0 0.6 copy-start.6
  9.7 0.6 copy-start.5
  13.1 5.1 %collective-permute-start.2 = (bf16[208,768]{1,0:T(8,128)(2,1)}, bf16[208,768]{1,0:T(8,128)(2,1)S(1)}, u32[]{:S(2)}, u32[]{:S(2)}) collective-permute-start(bf16[208,768]{1,0:T(8,128)(2,1)} %get-tuple-element.10.core_sent), channel_id=1, source_target_pairs={{0,1},{1,0},{2,3},{3,2},{4,5},{5,4},{6,7},{7,6},{8,9},{9,8},{10,11... | collective-permute-start | bytes 958472 | tf_op jit(solution)/shard_map/ppermute | solution.py:554
  15.0 56.2 %copy-start.7 = (s32[8,1]{0,1:T(1,128)S(1)}, s32[8,1]{0,1:T(1,128)}, u32[]{:S(2)}) copy-start(s32[8,1]{0,1:T(1,128)} %param.18) | copy-start | bytes 100
  15.0 8.6 %collective-permute-start.3 = (bf16[208,768]{1,0:T(8,128)(2,1)}, bf16[208,768]{1,0:T(8,128)(2,1)S(1)}, u32[]{:S(2)}, u32[]{:S(2)}) collective-permute-start(bf16[208,768]{1,0:T(8,128)(2,1)} %get-tuple-element.11.chip_sent), channel_id=1, source_target_pairs={{1,2},{3,4},{5,6},{2,1},{4,3},{6,5},{9,10},{11,12},{13,14},{10,9},... | collective-permute-start | bytes 958472 | tf_op jit(solution)/shard_map/ppermute | solution.py:560
  18.2 5.4 %copy-start.8 = (bf16[208,768]{1,0:T(8,128)(2,1)}, bf16[208,768]{1,0:T(8,128)(2,1)S(1)}, u32[]{:S(2)}) copy-start(bf16[208,768]{1,0:T(8,128)(2,1)S(1)} %collective-permute-done.2.core_got) | copy-start | bytes 958468
  23.6 0.7 copy-start.9
  65.0 6.3 %collective-permute-start.4 = (bf16[128,384]{1,0:T(8,128)(2,1)}, bf16[128,384]{1,0:T(8,128)(2,1)S(1)}, u32[]{:S(2)}, u32[]{:S(2)}) collective-permute-start(bf16[128,384]{1,0:T(8,128)(2,1)} %mix.1.mine), channel_id=1, source_target_pairs={{0,2},{1,3},{2,4},{3,5},{4,6},{5,7},{6,0},{7,1},{8,10},{9,11},{10,... | collective-permute-start | bytes 294920 | tf_op jit(solution)/shard_map/ppermute | solution.py:566
  67.6 6.1 %collective-permute-start.5 = (bf16[128,384]{1,0:T(8,128)(2,1)}, bf16[128,384]{1,0:T(8,128)(2,1)S(1)}, u32[]{:S(2)}, u32[]{:S(2)}) collective-permute-start(bf16[128,384]{1,0:T(8,128)(2,1)} %mix.1.mine), channel_id=1, source_target_pairs={{0,4},{1,5},{2,6},{3,7},{4,0},{5,1},{6,2},{7,3},{8,12},{9,13},{10,... | collective-permute-start | bytes 294920 | tf_op jit(solution)/shard_map/ppermute | solution.py:566
  69.1 4.6 %collective-permute-start.6 = (bf16[128,384]{1,0:T(8,128)(2,1)}, bf16[128,384]{1,0:T(8,128)(2,1)S(1)}, u32[]{:S(2)}, u32[]{:S(2)}) collective-permute-start(bf16[128,384]{1,0:T(8,128)(2,1)} %mix.1.mine), channel_id=1, source_target_pairs={{0,6},{1,7},{2,0},{3,1},{4,2},{5,3},{6,4},{7,5},{8,14},{9,15},{10,... | collective-permute-start | bytes 294920 | tf_op jit(solution)/shard_map/ppermute | solution.py:566
  74.7 21.2 %collective-permute-start.7 = (bf16[512,384]{1,0:T(8,128)(2,1)S(1)}, bf16[512,384]{1,0:T(8,128)(2,1)S(1)}, u32[]{:S(2)}, u32[]{:S(2)}) collective-permute-start(bf16[512,384]{1,0:T(8,128)(2,1)S(1)} %pad_maximum_fusion.refs_0_), channel_id=1, source_target_pairs={{0,1},{1,0},{2,3},{3,2},{4,5},{5,4},{6,7},{7,6},{8,9},{9,8},{10,11... | collective-permute-start | bytes 1179656 | tf_op jit(solution)/shard_map/ppermute | solution.py:554
  77.2 18.7 %copy-start = (bf16[128,384]{1,0:T(8,128)(2,1)S(1)}, bf16[128,384]{1,0:T(8,128)(2,1)}, u32[]{:S(2)}) copy-start(bf16[128,384]{1,0:T(8,128)(2,1)} %mix.1.mine) | copy-start | bytes 294916
  77.2 18.7 %copy-start.1 = (bf16[384,384]{1,0:T(8,128)(2,1)S(1)}, bf16[384,384]{1,0:T(8,128)(2,1)}, u32[]{:S(2)}) copy-start(bf16[384,384]{1,0:T(8,128)(2,1)} %refs_2_.1) | copy-start | bytes 884740
  77.2 18.7 %copy-start.2 = (bf16[384,384]{1,0:T(8,128)(2,1)S(1)}, bf16[384,384]{1,0:T(8,128)(2,1)}, u32[]{:S(2)}) copy-start(bf16[384,384]{1,0:T(8,128)(2,1)} %refs_3_.1) | copy-start | bytes 884740
  77.2 18.7 %copy-start.3 = (bf16[384,384]{1,0:T(8,128)(2,1)S(1)}, bf16[384,384]{1,0:T(8,128)(2,1)}, u32[]{:S(2)}) copy-start(bf16[384,384]{1,0:T(8,128)(2,1)} %refs_4_.1) | copy-start | bytes 884740
  77.2 18.8 %copy-start.4 = (bf16[384,384]{1,0:T(8,128)(2,1)S(1)}, bf16[384,384]{1,0:T(8,128)(2,1)}, u32[]{:S(2)}) copy-start(bf16[384,384]{1,0:T(8,128)(2,1)} %refs_5_.1) | copy-start | bytes 884740

commit v2 on v1

--- a/solution.py
+++ b/solution.py
@@ -16,37 +16,43 @@
 NT = (((1,), (1,)), ((), ()))
 NN = (((1,), (0,)), ((), ()))
 
-SIDES = (1, 0, 2)
-
-
 def dot(a, b, dims=NN):
     return lax.dot_general(a, b, dims, preferred_element_type=F32)
 
 
-def weight_copies(weight_ref, folded, sems, back):
-    chans = weight_ref.shape[-1]
+def fold_kernel(weight, folded, sems):
+    chans = weight.shape[-1]
     copies = []
-    for k, side in enumerate(SIDES):
-        for off in range(3):
-            for h_in in range(2):
-                for h_out in range(2):
-                    row, col = h_in * chans, h_out * chans
-                    if back:
-                        col += 2 * chans * off
-                    else:
-                        row += 2 * chans * off
-                    copies.append(
-                        pltpu.make_async_copy(
-                            weight_ref.at[
-                                2 - off if back else off,
-                                h_in - h_out + 1,
-                                2 - side if back else side,
-                            ],
-                            folded.at[k, pl.ds(row, chans), pl.ds(col, chans)],
-                            sems.at[k, 4 * off + 2 * h_in + h_out],
-                        )
+    for k in range(9):
+        for h_in in range(2):
+            for h_out in range(2):
+                copies.append(
+                    pltpu.make_async_copy(
+                        weight.at[k // 3, h_in - h_out + 1, k % 3],
+                        folded.at[k, pl.ds(h_in * chans, chans), pl.ds(h_out * chans, chans)],
+                        sems.at[k, 2 * h_in + h_out],
                     )
-    return [copies[12 * k : 12 * (k + 1)] for k in range(3)]
+                )
+    for copy in copies:
+        copy.start()
+    for copy in copies:
+        copy.wait()
+
+
+def fold(weight):
+    wide = 2 * weight.shape[-1]
+    return pl.pallas_call(
+        fold_kernel,
+        out_shape=pltpu.VMEM((9, wide, wide), BF16),
+        in_specs=[ANY],
+        out_specs=VMEM,
+        scratch_shapes=[pltpu.SemaphoreType.DMA((9, 4))],
+        compiler_params=pltpu.CompilerParams(vmem_limit_bytes=4 * 2**20),
+        cost_estimate=pl.CostEstimate(
+            flops=0, bytes_accessed=20 * 2**20, transcendentals=0
+        ),
+        name="fold",
+    )(weight)
 
 
 def store_pairs(values_of, sides, count, even, odd):
@@ -80,11 +86,20 @@
     store_pairs(both, (0, 2), count, even, odd)
 
 
-def window(side, even, odd, rows, extra=None):
-    parts = [even[side, 0:rows, :], odd[side, 0:rows, :], even[side, 16 : 16 + rows, :]]
-    if extra is not None:
-        parts = [jnp.concatenate([part, extra(side, off)], axis=0) for off, part in enumerate(parts)]
-    return jnp.concatenate(parts, axis=1)
+def add_taps(total, side, even, odd, weight_of, dims, extra=None):
+    rows = odd.shape[1]
+    for off in range(3):
+        if off == 1:
+            lhs = odd[side, 0:rows, :]
+        else:
+            lhs = even[side, 8 * off : 8 * off + rows, :]
+        if extra is not None:
+            lhs = jnp.concatenate([lhs, extra(side, off)], axis=0)
+        part = dot(lhs, weight_of(off, side), dims)
+        if (side, off) == (1, 0):
+            total[...] = part
+        else:
+            total[...] += part
 
 
 def pack_kernel(place, frames, out_grad, before, after, core_out, chip_out, wide_f, wide_g):
@@ -143,7 +158,7 @@
             pltpu.VMEM((2 * chans // 128, cols * (count + 4), 128), F32),
             pltpu.VMEM((2 * chans // 128, cols * (count + 2), 128), F32),
         ],
-        compiler_params=pltpu.CompilerParams(vmem_limit_bytes=56 * 2**20),
+        compiler_params=pltpu.CompilerParams(vmem_limit_bytes=24 * 2**20),
         name="pack",
     )(place, frames, out_grad, before, after)
 
@@ -159,8 +174,8 @@
     core_got,
     chip_got,
     out_grad,
-    weight,
     down,
+    folded,
     latent_out,
     sums_out,
     tail_out,
@@ -177,11 +192,9 @@
     high,
     even,
     odd,
-    folded,
     total,
     act,
     sems,
-    weight_sems,
 ):
     chans = frames.shape[-1]
     count = frames.shape[0]
@@ -193,18 +206,12 @@
     ]
     for copy in first:
         copy.start()
-    copies = weight_copies(weight, folded, weight_sems, False)
-    for copy in copies[0]:
-        copy.start()
     later = [
         pltpu.make_async_copy(
             out_grad.at[:, h], grad_block.at[:, :, pl.ds(h * chans, chans)], sems.at[2 + h]
         )
         for h in range(2)
     ] + [pltpu.make_async_copy(down, down_block, sems.at[4])]
-    for group in copies[1:]:
-        for copy in group:
-            copy.start()
     for copy in later:
         copy.start()
     even_core = place[1] == 0
@@ -235,9 +242,10 @@
         ).astype(BF16)
 
     build_centre(frame_of, span, even, odd)
-    for copy in copies[0]:
-        copy.wait()
-    total[...] = dot(window(1, even, odd, rows, rim), folded[0])
+    def weight_of(off, side):
+        return folded[3 * off + side]
+
+    add_taps(total, 1, even, odd, weight_of, NN, rim)
     build_sides(
         frame_of,
         lambda t: low[span + t : span + t + 1, :],
@@ -246,10 +254,8 @@
         even,
         odd,
     )
-    for k in (1, 2):
-        for copy in copies[k]:
-            copy.wait()
-        total[...] += dot(window(SIDES[k], even, odd, rows, rim), folded[k])
+    for side in (0, 2):
+        add_taps(total, side, even, odd, weight_of, NN, rim)
     for copy in later:
         copy.wait()
 
@@ -307,7 +313,7 @@
     write.wait()
 
 
-def forward(peers, place, lengths, frames, before, after, columns, out_grad, weight, down):
+def forward(peers, place, lengths, frames, before, after, columns, out_grad, down, folded):
     count, _, cols, chans = frames.shape
     wide = 2 * chans
     lat = count // 8
@@ -324,7 +330,7 @@
             jax.ShapeDtypeStruct((ahead + 6, wide), F32),
             jax.ShapeDtypeStruct((ahead, cols, wide), BF16),
         ),
-        in_specs=[SMEM, SMEM, ANY] + [VMEM] * 6 + [ANY] * 3,
+        in_specs=[SMEM, SMEM, ANY] + [VMEM] * 6 + [ANY, ANY, VMEM],
         out_specs=[VMEM] * 5 + [ANY],
         scratch_shapes=[
             pltpu.VMEM((count, cols, wide), BF16),
@@ -337,18 +343,16 @@
             pltpu.VMEM(received, F32),
             pltpu.VMEM((3, rows + 16, wide), BF16),
             pltpu.VMEM((3, rows, wide), BF16),
-            pltpu.VMEM((3, 3 * wide, wide), BF16),
             pltpu.VMEM((rows + 2 * (ahead + 6), wide), F32),
             pltpu.VMEM((lat, 8, cols, wide), F32),
             pltpu.SemaphoreType.DMA((6,)),
-            pltpu.SemaphoreType.DMA((3, 12)),
         ],
-        compiler_params=pltpu.CompilerParams(vmem_limit_bytes=60 * 2**20),
+        compiler_params=pltpu.CompilerParams(vmem_limit_bytes=44 * 2**20),
         cost_estimate=pl.CostEstimate(
             flops=2 * 9 * rows * wide * wide, bytes_accessed=16 * 2**20, transcendentals=rows * wide
         ),
         name="forward",
-    )(place, lengths, frames, before, after, *columns, out_grad, weight, down)
+    )(place, lengths, frames, before, after, *columns, out_grad, down, pltpu.with_memory_space_constraint(folded, pltpu.VMEM))
 
 
 def backward_kernel(
@@ -356,25 +360,19 @@
     low,
     high,
     out_grad,
-    weight,
+    folded,
     result,
     block,
     source,
     done,
     even,
     odd,
-    folded,
     total,
     sems,
-    weight_sems,
 ):
     count, _, cols, chans = out_grad.shape
     first = pltpu.make_async_copy(grad, block, sems.at[0])
     first.start()
-    copies = weight_copies(weight, folded, weight_sems, True)
-    for group in copies:
-        for copy in group:
-            copy.start()
     later = pltpu.make_async_copy(out_grad, source, sems.at[1])
     later.start()
     first.wait()
@@ -382,11 +380,11 @@
     def frame_of(t):
         return block[t]
 
-    rows = 8 * count
+    def weight_of(off, side):
+        return folded[3 * (2 - off) + 2 - side]
+
     build_centre(frame_of, count + 2, even, odd)
-    for copy in copies[0]:
-        copy.wait()
-    total[...] = dot(window(1, even, odd, rows), folded[0], NT)
+    add_taps(total, 1, even, odd, weight_of, NT)
     build_sides(
         frame_of,
         lambda t: low[t : t + 1, :],
@@ -395,25 +393,14 @@
         even,
         odd,
     )
-    for copy in copies[1]:
-        copy.wait()
-    total[...] += dot(window(SIDES[1], even, odd, rows), folded[1], NT)
-    for copy in copies[2]:
-        copy.wait()
+    add_taps(total, 0, even, odd, weight_of, NT)
+    add_taps(total, 2, even, odd, weight_of, NT)
     later.wait()
     writes = []
     step = count // 4
     for j in range(4):
         at = slice(8 * step * j, 8 * step * (j + 1))
-        lhs = jnp.concatenate(
-            [
-                even[2, 8 * step * j : 8 * step * (j + 1), :],
-                odd[2, 8 * step * j : 8 * step * (j + 1), :],
-                even[2, 16 + 8 * step * j : 16 + 8 * step * (j + 1), :],
-            ],
-            axis=1,
-        )
-        part = total[at, :] + dot(lhs, folded[2], NT)
+        part = total[at, :]
         for h in range(2):
             mine = part[:, h * chans : (h + 1) * chans].reshape(step, cols, chans)
             done[step * j : step * (j + 1), h] = (
@@ -428,13 +415,13 @@
         write.wait()
 
 
-def backward(grad, low, high, out_grad, weight):
+def backward(grad, low, high, out_grad, folded):
     count, _, cols, chans = out_grad.shape
     rows, wide = count * cols, 2 * chans
     return pl.pallas_call(
         backward_kernel,
         out_shape=jax.ShapeDtypeStruct(out_grad.shape, BF16),
-        in_specs=[ANY, VMEM, VMEM, ANY, ANY],
+        in_specs=[ANY, VMEM, VMEM, ANY, VMEM],
         out_specs=ANY,
         scratch_shapes=[
             pltpu.VMEM(grad.shape, BF16),
@@ -442,17 +429,15 @@
             pltpu.VMEM(out_grad.shape, BF16),
             pltpu.VMEM((3, rows + 16, wide), BF16),
             pltpu.VMEM((3, rows, wide), BF16),
-            pltpu.VMEM((3, wide, 3 * wide), BF16),
             pltpu.VMEM((rows, wide), F32),
             pltpu.SemaphoreType.DMA((6,)),
-            pltpu.SemaphoreType.DMA((3, 12)),
         ],
-        compiler_params=pltpu.CompilerParams(vmem_limit_bytes=60 * 2**20),
+        compiler_params=pltpu.CompilerParams(vmem_limit_bytes=44 * 2**20),
         cost_estimate=pl.CostEstimate(
             flops=2 * 9 * rows * wide * wide, bytes_accessed=12 * 2**20, transcendentals=0
         ),
         name="backward",
-    )(grad, low, high, out_grad, weight)
+    )(grad, low, high, out_grad, pltpu.with_memory_space_constraint(folded, pltpu.VMEM))
 
 
 def mix_kernel(place, lengths, latent, sums, tails, mixed):
@@ -485,6 +470,7 @@
         out_shape=jax.ShapeDtypeStruct((latent.shape[0] * 16, latent.shape[2]), BF16),
         in_specs=[SMEM, SMEM, VMEM, VMEM, VMEM],
         out_specs=VMEM,
+        compiler_params=pltpu.CompilerParams(vmem_limit_bytes=16 * 2**20),
         name="mix",
     )(place, lengths, latent, sums, tails)
 
@@ -537,7 +523,7 @@
         in_specs=[SMEM] + [VMEM] * (5 + len(pieces)),
         out_specs=VMEM,
         scratch_shapes=[pltpu.VMEM((total, chans), BF16), pltpu.VMEM((total, chans), BF16)],
-        compiler_params=pltpu.CompilerParams(vmem_limit_bytes=32 * 2**20),
+        compiler_params=pltpu.CompilerParams(vmem_limit_bytes=24 * 2**20),
         name="attend",
     )(labels, mine, *pieces, w_query, w_key, w_value, w_out)
 
@@ -560,14 +546,12 @@
     return lax.ppermute(value, "scene", pairs + [(b, a) for a, b in pairs])
 
 
-def gathered(value):
+def chip_shifts(value):
     count = lax.axis_size("scene")
-    chips = [
+    return [
         lax.ppermute(value, "scene", [(i, (i + 2 * k) % count) for i in range(count)])
         for k in range(1, count // 2)
     ]
-    own = jnp.concatenate([value, *chips], axis=0)
-    return [own, with_core(own)]
 
 
 def per_device(
@@ -586,6 +570,7 @@
     place = jnp.stack([lax.axis_index("tm"), lax.axis_index("scene") % 2]).astype(jnp.int32)
     before = shifted(frames[count - 2 :], "tm", 1)
     after = shifted(jnp.concatenate([frames[:2], out_grad[:2]], axis=0), "tm", -1)
+    folded = fold(conv_weight)
     sent = pack(place, frames, out_grad, before, after)
     columns = (*sent, with_core(sent[0]), with_chip(sent[1]))
     latent, sums, tail, low, high, grad = forward(
@@ -597,13 +582,16 @@
         after,
         columns,
         out_grad,
-        conv_weight,
         down_weight,
+        folded,
     )
     tails = lax.all_to_all(tail, "tm", 0, 0, tiled=True)
     mixed = mix(place, shot_lengths, latent, sums, tails)
-    pieces = gathered(mixed)
-    frame_grad = backward(grad, low, high, out_grad, conv_weight)
+    chips = chip_shifts(mixed)
+    frame_grad = backward(grad, low, high, out_grad, folded)
+    chips, frame_grad = lax.optimization_barrier((chips, frame_grad))
+    own = jnp.concatenate([mixed, *chips], axis=0)
+    pieces = [own, with_core(own)]
     latent_out = attend(scene_label, mixed, pieces, w_query, w_key, w_value, w_out)
     return (latent_out, frame_grad)
 

time: 102 us -> 83.3 us (0.82)
  Pallas kernels: 48.4 us -> 31.1 us
  local copies, waits for them, and re-layouts: 3.58 us -> 10.1 us
  waiting for transfers between devices: 8.19 us -> 2.44 us
  other arithmetic: 1.55 us -> 0.13 us
    pallas_call x1, Pallas kernels: 18.7 us -> 8.92 us  [backward(): pl.pallas_call(backward_kernel, out_shape=jax.ShapeDtypeStruct(out_grad.s...]
    unnamed x21 -> x39, local copies, waits for them, and re-layouts: 2.08 us -> 8.63 us
    pallas_call x1, Pallas kernels: 19.8 us -> 13.8 us  [forward(): pl.pallas_call(forward_kernel, out_shape=(jax.ShapeDtypeStruct((lat, 16,...]
    ppermute x1, waiting for transfers between devices: 5.39 us -> 0.32 us  [with_chip(): return lax.ppermute(value, 'scene', pairs + [(b, a) for a, b in pairs])]
    ppermute x3, waiting for transfers between devices: 2.49 us -> 0.01 us  [chip_shifts(): lax.ppermute(value, 'scene', [(i, (i + 2 * k) % count) for i in range(cou...]
    pallas_call x1, Pallas kernels: 2.83 us -> 1.14 us  [pack(): pl.pallas_call(pack_kernel, out_shape=[jax.ShapeDtypeStruct((rows, 2 * ch...]
    pallas_call x0 -> x1, Pallas kernels: none -> 1.5 us  [fold(): pl.pallas_call(fold_kernel, out_shape=pltpu.VMEM((9, wide, wide), BF16),...]
    pallas_call x1, Pallas kernels: 2 us -> 0.7 us  [mix(): pl.pallas_call(mix_kernel, out_shape=jax.ShapeDtypeStruct((latent.shape[0...]
  transfers between devices with their start and end apart: 8 -> 8, of which waited for: 4 -> 3; matrix products, arithmetic and copies ran while one was open for 1% -> 0% of each run, Pallas kernels for 18% -> 13%
where the time goes in v2:
time: 83.3 us; the launch traced here: 82.6 us
  Pallas kernels  31.1 us (37%)
  blocking collectives  19.2 us (23%)
  starting transfers between devices  18.8 us (23%)
  local copies, waits for them, and re-layouts  10.1 us (12%)
  waiting for transfers between devices  2.44 us (3%)
  between operations  0.87 us (1%)
    all_to_all x1, blocking collectives, per_device(): tails = lax.all_to_all(tail, 'tm', 0, 0, tiled=True)  19.2 us
    pallas_call x1, Pallas kernels, forward(): pl.pallas_call(forward_kernel, out_shape=(jax.ShapeDtypeStruct((lat, 16,...  13.8 us
    pallas_call x1, Pallas kernels, backward(): pl.pallas_call(backward_kernel, out_shape=jax.ShapeDtypeStruct(out_grad.s...  8.92 us
    unnamed x39, local copies, waits for them, and re-layouts  8.63 us
    ppermute x2, starting transfers between devices, shifted(): lax.ppermute(value, axis, [(i, i + steps) for i in range(count) if 0 <= i...  5.95 us
    ppermute x3, starting transfers between devices, chip_shifts(): lax.ppermute(value, 'scene', [(i, (i + 2 * k) % count) for i in range(cou...  5.46 us
    pallas_call x1, Pallas kernels, attend(): pl.pallas_call(attend_kernel, out_shape=jax.ShapeDtypeStruct((labels.shap...  5.08 us
    ppermute x2, starting transfers between devices, with_core(): return lax.ppermute(value, 'scene', [(i, i ^ 1) for i in range(count)])  4.29 us
  transfers between devices with their start and end apart: 8, of which 3 were waited for; matrix products, arithmetic and copies ran while one was open for 0% of the time, Pallas kernels for 13%

profile of v2, /device:TPU:1, one launch (start us, length us, event | category | flops | bytes accessed | tf_op | source)
XLA Modules:
  0.0 82.6 jit_solution(13832466548016490199)
XLA Ops:
  0.6 0.8 fusion
  1.4 0.7 slice.11
  2.1 1.3 %collective-permute-start.1 = (bf16[4,2,8,384]{3,2,1,0:T(8,128)(2,1)S(1)}, bf16[4,2,8,384]{3,2,1,0:T(8,128)(2,1)S(1)}, u32[]{:S(2)}, u32[]{:S(2)}) collective-permute-start(bf16[4,2,8,384]{3,2,1,0:T(8,128)(2,1)S(1)} %pad_maximum_fusion.1), channel_id=1, source_target_pairs={{8,0},{16,8},{24,16},{32,24},{40,32},{48,40},{56,48},{64,56},{72,6... | collective-permute-start | bytes 147464 | tf_op jit(solution)/shard_map/ppermute | solution.py:533
  3.4 4.7 %collective-permute-start = (bf16[2,2,8,384]{3,2,1,0:T(8,128)(2,1)S(1)}, bf16[2,2,8,384]{3,2,1,0:T(8,128)(2,1)S(1)}, u32[]{:S(2)}, u32[]{:S(2)}) collective-permute-start(bf16[2,2,8,384]{3,2,1,0:T(8,128)(2,1)S(1)} %get-tuple-element.27), channel_id=1, source_target_pairs={{0,8},{8,16},{16,24},{24,32},{32,40},{40,48},{48,56},{56,64},{64,7... | collective-permute-start | bytes 73736 | tf_op jit(solution)/shard_map/ppermute | solution.py:533
  8.1 0.1 pad_add_fusion.place
  8.2 0.8 %collective-permute-done.before = bf16[2,2,8,384]{3,2,1,0:T(8,128)(2,1)S(1)} collective-permute-done((bf16[2,2,8,384]{3,2,1,0:T(8,128)(2,1)S(1)}, bf16[2,2,8,384]{3,2,1,0:T(8,128)(2,1)S(1)}, u32[]{:S(2)}, u32[]{:S(2)}) %collective-permute-start) | collective-permute-done | bytes 24608 | tf_op jit(solution)/shard_map/ppermute | solution.py:533
  9.0 1.1 %copy-done.1 = bf16[64,2,8,384]{3,2,1,0:T(8,128)(2,1)S(1)} copy-done((bf16[64,2,8,384]{3,2,1,0:T(8,128)(2,1)S(1)}, bf16[64,2,8,384]{3,2,1,0:T(8,128)(2,1)}, u32[]{:S(2)}) %copy-start.1) | copy-done | bytes 786456
  10.2 1.1 %copy-done.2 = bf16[64,2,8,384]{3,2,1,0:T(8,128)(2,1)S(1)} copy-done((bf16[64,2,8,384]{3,2,1,0:T(8,128)(2,1)S(1)}, bf16[64,2,8,384]{3,2,1,0:T(8,128)(2,1)}, u32[]{:S(2)}) %copy-start.2) | copy-done | bytes 786456
  11.3 1.1 %pack.1 = (bf16[208,768]{1,0:T(8,128)(2,1)S(1)}, bf16[208,768]{1,0:T(8,128)(2,1)S(1)}) custom-call(s32[2]{0:T(128)S(1)} %pad_add_fusion.place, bf16[64,2,8,384]{3,2,1,0:T(8,128)(2,1)S(1)} %copy-done.1, bf16[64,2,8,384]{3,2,1,0:T(8,128)(2,1)S(1)} %copy-done.2, bf16[2,2,8,384]{3,2,1,0:T(8,128)(2,1)S(1)} %collective-permute-done.before, ...), custom_call_target="tpu_custom_call" | custom-call | tf_op jit(solution)/shard_map/pack/pallas_call | solution.py:152
  12.5 2.0 %collective-permute-start.2 = (bf16[208,768]{1,0:T(8,128)(2,1)S(1)}, bf16[208,768]{1,0:T(8,128)(2,1)S(1)}, u32[]{:S(2)}, u32[]{:S(2)}) collective-permute-start(bf16[208,768]{1,0:T(8,128)(2,1)S(1)} %get-tuple-element.14.core_sent), channel_id=1, source_target_pairs={{0,1},{1,0},{2,3},{3,2},{4,5},{5,4},{6,7},{7,6},{8,9},{9,8},{10,11... | collective-permute-start | bytes 958472 | tf_op jit(solution)/shard_map/ppermute | solution.py:540
  14.5 3.1 %collective-permute-start.3 = (bf16[208,768]{1,0:T(8,128)(2,1)S(1)}, bf16[208,768]{1,0:T(8,128)(2,1)S(1)}, u32[]{:S(2)}, u32[]{:S(2)}) collective-permute-start(bf16[208,768]{1,0:T(8,128)(2,1)S(1)} %get-tuple-element.15.chip_sent), channel_id=1, source_target_pairs={{1,2},{3,4},{5,6},{2,1},{4,3},{6,5},{9,10},{11,12},{13,14},{10,9},... | collective-permute-start | bytes 958472 | tf_op jit(solution)/shard_map/ppermute | solution.py:546
  17.6 0.0 copy-start
  17.6 3.3 %copy-done = bf16[3,3,3,384,384]{4,3,2,1,0:T(8,128)(2,1)S(1)} copy-done((bf16[3,3,3,384,384]{4,3,2,1,0:T(8,128)(2,1)S(1)}, bf16[3,3,3,384,384]{4,3,2,1,0:T(8,128)(2,1)}, u32[]{:S(2)}) %copy-start) | copy-done | bytes 7962648
  20.8 1.5 %fold.1.folded = bf16[9,768,768]{2,1,0:T(8,128)(2,1)S(1)} custom-call(bf16[3,3,3,384,384]{4,3,2,1,0:T(8,128)(2,1)S(1)} %copy-done), custom_call_target="tpu_custom_call" | custom-call | bytes 20971520 | tf_op jit(solution)/shard_map/fold/pallas_call | solution.py:44
  22.4 0.0 copy-start.13
  22.4 0.3 collective-permute-done.3.chip_got
  22.8 0.4 copy-done.17
  23.2 0.7 copy-done.18
  23.9 13.8 %forward.1 = (f32[8,16,384]{2,1,0:T(8,128)}, f32[8,16,384]{2,1,0:T(8,128)}, f32[16,16,384]{2,1,0:T(8,128)}, f32[72,768]{1,0:T(8,128)}, f32[72,768]{1,0:T(8,128)}, /*index=5*/bf16[66,8,768]{2,1,0:T(8,128)(2,1)}) custom-call(s32[2]{0:T(128)} %copy-done.11, s32[8]{0:T(128)} %lengths.3, bf16[64,2,8,384]{3,2,1,0:T(8,128)(2,1)} %frames.3, ...), custom_call_target="tpu_custom_call" | custom-call | flops 5605687296 | bytes 16777216 | tf_op jit(solution)/shard_map/forward/pallas_call | solution.py:323
  37.6 19.2 %all_to_all.5.tails = f32[16,16,384]{2,1,0:T(8,128)S(1)} all-to-all(f32[16,16,384]{2,1,0:T(8,128)} %get-tuple-element.18), channel_id=1, replica_groups=mesh['tm'=16,'scene'=8] {'tm'}, dimensions={0} | all-to-all | bytes 786432 | tf_op jit(solution)/shard_map/all_to_all | solution.py:588
  56.8 0.9 %copy-done.7 = f32[8,16,384]{2,1,0:T(8,128)S(1)} copy-done((f32[8,16,384]{2,1,0:T(8,128)S(1)}, f32[8,16,384]{2,1,0:T(8,128)}, u32[]{:S(2)}) %copy-start.7) | copy-done | bytes 196632
  57.7 0.9 %copy-done.8 = f32[8,16,384]{2,1,0:T(8,128)S(1)} copy-done((f32[8,16,384]{2,1,0:T(8,128)S(1)}, f32[8,16,384]{2,1,0:T(8,128)}, u32[]{:S(2)}) %copy-start.8) | copy-done | bytes 196632
  58.7 0.7 mix.1.mine
  59.4 2.5 %collective-permute-start.4 = (bf16[128,384]{1,0:T(8,128)(2,1)S(1)}, bf16[128,384]{1,0:T(8,128)(2,1)S(1)}, u32[]{:S(2)}, u32[]{:S(2)}) collective-permute-start(bf16[128,384]{1,0:T(8,128)(2,1)S(1)} %mix.1.mine), channel_id=1, source_target_pairs={{0,2},{1,3},{2,4},{3,5},{4,6},{5,7},{6,0},{7,1},{8,10},{9,11},{10,... | collective-permute-start | bytes 294920 | tf_op jit(solution)/shard_map/ppermute | solution.py:552
  61.9 1.0 %collective-permute-start.5 = (bf16[128,384]{1,0:T(8,128)(2,1)S(1)}, bf16[128,384]{1,0:T(8,128)(2,1)S(1)}, u32[]{:S(2)}, u32[]{:S(2)}) collective-permute-start(bf16[128,384]{1,0:T(8,128)(2,1)S(1)} %mix.1.mine), channel_id=1, source_target_pairs={{0,4},{1,5},{2,6},{3,7},{4,0},{5,1},{6,2},{7,3},{8,12},{9,13},{10,... | collective-permute-start | bytes 294920 | tf_op jit(solution)/shard_map/ppermute | solution.py:552
  62.9 2.0 %collective-permute-start.6 = (bf16[128,384]{1,0:T(8,128)(2,1)S(1)}, bf16[128,384]{1,0:T(8,128)(2,1)S(1)}, u32[]{:S(2)}, u32[]{:S(2)}) collective-permute-start(bf16[128,384]{1,0:T(8,128)(2,1)S(1)} %mix.1.mine), channel_id=1, source_target_pairs={{0,6},{1,7},{2,0},{3,1},{4,2},{5,3},{6,4},{7,5},{8,14},{9,15},{10,... | collective-permute-start | bytes 294920 | tf_op jit(solution)/shard_map/ppermute | solution.py:552
  64.8 0.0 copy-start.6
  64.9 8.9 %backward.1 = bf16[64,2,8,384]{3,2,1,0:T(8,128)(2,1)} custom-call(bf16[66,8,768]{2,1,0:T(8,128)(2,1)} %get-tuple-element.19.grad, f32[72,768]{1,0:T(8,128)} %get-tuple-element.20.low, f32[72,768]{1,0:T(8,128)} %get-tuple-element.21.high, bf16[64,2,8,384]{3,2,1,0:T(8,128)(2,1)} %out_grad.5, bf16[9,768,768]{2,1,0:T(8,128)(2,1)S(1)} %fold.1.folded), custom_call_target="tpu_custom_call" | custom-call | flops 5435817984 | bytes 12582912 | tf_op jit(solution)/shard_map/backward/pallas_call | solution.py:421
  73.9 2.3 %collective-permute-start.7 = (bf16[512,384]{1,0:T(8,128)(2,1)S(1)}, bf16[512,384]{1,0:T(8,128)(2,1)S(1)}, u32[]{:S(2)}, u32[]{:S(2)}) collective-permute-start(bf16[512,384]{1,0:T(8,128)(2,1)S(1)} %pad_maximum_fusion.refs_0_), channel_id=1, source_target_pairs={{0,1},{1,0},{2,3},{3,2},{4,5},{5,4},{6,7},{7,6},{8,9},{9,8},{10,11... | collective-permute-start | bytes 1179656 | tf_op jit(solution)/shard_map/ppermute | solution.py:540
  76.2 0.1 copy.12.labels
  76.3 1.3 %collective-permute-done.7.refs_1_ = bf16[512,384]{1,0:T(8,128)(2,1)S(1)} collective-permute-done((bf16[512,384]{1,0:T(8,128)(2,1)S(1)}, bf16[512,384]{1,0:T(8,128)(2,1)S(1)}, u32[]{:S(2)}, u32[]{:S(2)}) %collective-permute-start.7) | collective-permute-done | bytes 393248 | tf_op jit(solution)/shard_map/ppermute | solution.py:540
  77.6 5.1 %attend.1 = bf16[8,2,8,384]{3,2,1,0:T(8,128)(2,1)} custom-call(s32[8,1]{1,0:T(8,128)S(1)} %copy.12.labels, bf16[128,384]{1,0:T(8,128)(2,1)S(1)} %mix.1.mine, bf16[512,384]{1,0:T(8,128)(2,1)S(1)} %pad_maximum_fusion.refs_0_, bf16[512,384]{1,0:T(8,128)(2,1)S(1)} %collective-permute-done.7.refs_1_, bf16[384,384]{1,0:T(8,128)(2,1)S(1)} %copy-done.3, ...), custom_call_target="tpu_custom_call" | custom-call | tf_op jit(solution)/shard_map/attend/pallas_call | solution.py:520
  (35 shorter events, 0.1 us)
Async XLA Ops:
  2.1 6.9 %collective-permute-start.1 = (bf16[4,2,8,384]{3,2,1,0:T(8,128)(2,1)S(1)}, bf16[4,2,8,384]{3,2,1,0:T(8,128)(2,1)S(1)}, u32[]{:S(2)}, u32[]{:S(2)}) collective-permute-start(bf16[4,2,8,384]{3,2,1,0:T(8,128)(2,1)S(1)} %pad_maximum_fusion.1), channel_id=1, source_target_pairs={{8,0},{16,8},{24,16},{32,24},{40,32},{48,40},{56,48},{64,56},{72,6... | collective-permute-start | bytes 147464 | tf_op jit(solution)/shard_map/ppermute | solution.py:533
  3.4 5.6 %collective-permute-start = (bf16[2,2,8,384]{3,2,1,0:T(8,128)(2,1)S(1)}, bf16[2,2,8,384]{3,2,1,0:T(8,128)(2,1)S(1)}, u32[]{:S(2)}, u32[]{:S(2)}) collective-permute-start(bf16[2,2,8,384]{3,2,1,0:T(8,128)(2,1)S(1)} %get-tuple-element.27), channel_id=1, source_target_pairs={{0,8},{8,16},{16,24},{24,32},{32,40},{40,48},{48,56},{56,64},{64,7... | collective-permute-start | bytes 73736 | tf_op jit(solution)/shard_map/ppermute | solution.py:533
  8.2 14.1 %copy-start.11 = (s32[2]{0:T(128)}, s32[2]{0:T(128)S(1)}, u32[]{:S(2)}) copy-start(s32[2]{0:T(128)S(1)} %pad_add_fusion.place) | copy-start | bytes 28
  9.0 13.3 %copy-start.10 = (bf16[2,2,8,384]{3,2,1,0:T(8,128)(2,1)}, bf16[2,2,8,384]{3,2,1,0:T(8,128)(2,1)S(1)}, u32[]{:S(2)}) copy-start(bf16[2,2,8,384]{3,2,1,0:T(8,128)(2,1)S(1)} %collective-permute-done.before) | copy-start | bytes 73732
  9.0 1.1 %copy-start.1 = (bf16[64,2,8,384]{3,2,1,0:T(8,128)(2,1)S(1)}, bf16[64,2,8,384]{3,2,1,0:T(8,128)(2,1)}, u32[]{:S(2)}) copy-start(bf16[64,2,8,384]{3,2,1,0:T(8,128)(2,1)} %frames.3) | copy-start | bytes 2359300
  10.2 1.1 %copy-start.2 = (bf16[64,2,8,384]{3,2,1,0:T(8,128)(2,1)S(1)}, bf16[64,2,8,384]{3,2,1,0:T(8,128)(2,1)}, u32[]{:S(2)}) copy-start(bf16[64,2,8,384]{3,2,1,0:T(8,128)(2,1)} %out_grad.5) | copy-start | bytes 2359300
  11.3 11.0 %copy-start.9 = (bf16[4,2,8,384]{3,2,1,0:T(8,128)(2,1)}, bf16[4,2,8,384]{3,2,1,0:T(8,128)(2,1)S(1)}, u32[]{:S(2)}) copy-start(bf16[4,2,8,384]{3,2,1,0:T(8,128)(2,1)S(1)} %collective-permute-done.1.after) | copy-start | bytes 147460
  12.5 9.9 %copy-start.14 = (bf16[208,768]{1,0:T(8,128)(2,1)}, bf16[208,768]{1,0:T(8,128)(2,1)S(1)}, u32[]{:S(2)}) copy-start(bf16[208,768]{1,0:T(8,128)(2,1)S(1)} %get-tuple-element.14.core_sent) | copy-start | bytes 958468
  12.5 9.9 %copy-start.15 = (bf16[208,768]{1,0:T(8,128)(2,1)}, bf16[208,768]{1,0:T(8,128)(2,1)S(1)}, u32[]{:S(2)}) copy-start(bf16[208,768]{1,0:T(8,128)(2,1)S(1)} %get-tuple-element.15.chip_sent) | copy-start | bytes 958468
  12.5 9.9 %collective-permute-start.2 = (bf16[208,768]{1,0:T(8,128)(2,1)S(1)}, bf16[208,768]{1,0:T(8,128)(2,1)S(1)}, u32[]{:S(2)}, u32[]{:S(2)}) collective-permute-start(bf16[208,768]{1,0:T(8,128)(2,1)S(1)} %get-tuple-element.14.core_sent), channel_id=1, source_target_pairs={{0,1},{1,0},{2,3},{3,2},{4,5},{5,4},{6,7},{7,6},{8,9},{9,8},{10,11... | collective-permute-start | bytes 958472 | tf_op jit(solution)/shard_map/ppermute | solution.py:540
  14.5 8.3 %collective-permute-start.3 = (bf16[208,768]{1,0:T(8,128)(2,1)S(1)}, bf16[208,768]{1,0:T(8,128)(2,1)S(1)}, u32[]{:S(2)}, u32[]{:S(2)}) collective-permute-start(bf16[208,768]{1,0:T(8,128)(2,1)S(1)} %get-tuple-element.15.chip_sent), channel_id=1, source_target_pairs={{1,2},{3,4},{5,6},{2,1},{4,3},{6,5},{9,10},{11,12},{13,14},{10,9},... | collective-permute-start | bytes 958472 | tf_op jit(solution)/shard_map/ppermute | solution.py:546
  17.6 3.3 %copy-start = (bf16[3,3,3,384,384]{4,3,2,1,0:T(8,128)(2,1)S(1)}, bf16[3,3,3,384,384]{4,3,2,1,0:T(8,128)(2,1)}, u32[]{:S(2)}) copy-start(bf16[3,3,3,384,384]{4,3,2,1,0:T(8,128)(2,1)} %weight.1) | copy-start | bytes 23887876
  22.4 34.4 %copy-start.13 = (s32[8]{0:T(128)S(1)}, s32[8]{0:T(128)}, u32[]{:S(2)}) copy-start(s32[8]{0:T(128)} %lengths.3) | copy-start | bytes 100
  22.4 0.7 copy-start.17
  22.4 34.4 %copy-start.12 = (s32[2]{0:T(128)S(1)}, s32[2]{0:T(128)}, u32[]{:S(2)}) copy-start(s32[2]{0:T(128)} %copy-done.11) | copy-start | bytes 28
  23.1 0.7 copy-start.18
  56.8 0.9 %copy-start.7 = (f32[8,16,384]{2,1,0:T(8,128)S(1)}, f32[8,16,384]{2,1,0:T(8,128)}, u32[]{:S(2)}) copy-start(f32[8,16,384]{2,1,0:T(8,128)} %get-tuple-element.16.latent) | copy-start | bytes 589828
  57.7 0.9 %copy-start.8 = (f32[8,16,384]{2,1,0:T(8,128)S(1)}, f32[8,16,384]{2,1,0:T(8,128)}, u32[]{:S(2)}) copy-start(f32[8,16,384]{2,1,0:T(8,128)} %get-tuple-element.17.sums) | copy-start | bytes 589828
  59.4 14.4 %collective-permute-start.4 = (bf16[128,384]{1,0:T(8,128)(2,1)S(1)}, bf16[128,384]{1,0:T(8,128)(2,1)S(1)}, u32[]{:S(2)}, u32[]{:S(2)}) collective-permute-start(bf16[128,384]{1,0:T(8,128)(2,1)S(1)} %mix.1.mine), channel_id=1, source_target_pairs={{0,2},{1,3},{2,4},{3,5},{4,6},{5,7},{6,0},{7,1},{8,10},{9,11},{10,... | collective-permute-start | bytes 294920 | tf_op jit(solution)/shard_map/ppermute | solution.py:552
  61.9 11.9 %collective-permute-start.5 = (bf16[128,384]{1,0:T(8,128)(2,1)S(1)}, bf16[128,384]{1,0:T(8,128)(2,1)S(1)}, u32[]{:S(2)}, u32[]{:S(2)}) collective-permute-start(bf16[128,384]{1,0:T(8,128)(2,1)S(1)} %mix.1.mine), channel_id=1, source_target_pairs={{0,4},{1,5},{2,6},{3,7},{4,0},{5,1},{6,2},{7,3},{8,12},{9,13},{10,... | collective-permute-start | bytes 294920 | tf_op jit(solution)/shard_map/ppermute | solution.py:552
  62.9 11.0 %collective-permute-start.6 = (bf16[128,384]{1,0:T(8,128)(2,1)S(1)}, bf16[128,384]{1,0:T(8,128)(2,1)S(1)}, u32[]{:S(2)}, u32[]{:S(2)}) collective-permute-start(bf16[128,384]{1,0:T(8,128)(2,1)S(1)} %mix.1.mine), channel_id=1, source_target_pairs={{0,6},{1,7},{2,0},{3,1},{4,2},{5,3},{6,4},{7,5},{8,14},{9,15},{10,... | collective-permute-start | bytes 294920 | tf_op jit(solution)/shard_map/ppermute | solution.py:552
  64.8 11.4 %copy-start.16 = (s32[8,1]{0,1:T(1,128)S(1)}, s32[8,1]{0,1:T(1,128)}, u32[]{:S(2)}) copy-start(s32[8,1]{0,1:T(1,128)} %param.18) | copy-start | bytes 100
  64.8 12.7 %copy-start.3 = (bf16[384,384]{1,0:T(8,128)(2,1)S(1)}, bf16[384,384]{1,0:T(8,128)(2,1)}, u32[]{:S(2)}) copy-start(bf16[384,384]{1,0:T(8,128)(2,1)} %refs_2_.1) | copy-start | bytes 884740
  64.8 12.7 %copy-start.4 = (bf16[384,384]{1,0:T(8,128)(2,1)S(1)}, bf16[384,384]{1,0:T(8,128)(2,1)}, u32[]{:S(2)}) copy-start(bf16[384,384]{1,0:T(8,128)(2,1)} %refs_3_.1) | copy-start | bytes 884740
  64.8 12.7 %copy-start.5 = (bf16[384,384]{1,0:T(8,128)(2,1)S(1)}, bf16[384,384]{1,0:T(8,128)(2,1)}, u32[]{:S(2)}) copy-start(bf16[384,384]{1,0:T(8,128)(2,1)} %refs_4_.1) | copy-start | bytes 884740
  64.8 12.7 %copy-start.6 = (bf16[384,384]{1,0:T(8,128)(2,1)S(1)}, bf16[384,384]{1,0:T(8,128)(2,1)}, u32[]{:S(2)}) copy-start(bf16[384,384]{1,0:T(8,128)(2,1)} %refs_5_.1) | copy-start | bytes 884740
  73.9 3.7 %collective-permute-start.7 = (bf16[512,384]{1,0:T(8,128)(2,1)S(1)}, bf16[512,384]{1,0:T(8,128)(2,1)S(1)}, u32[]{:S(2)}, u32[]{:S(2)}) collective-permute-start(bf16[512,384]{1,0:T(8,128)(2,1)S(1)} %pad_maximum_fusion.refs_0_), channel_id=1, source_target_pairs={{0,1},{1,0},{2,3},{3,2},{4,5},{5,4},{6,7},{7,6},{8,9},{9,8},{10,11... | collective-permute-start | bytes 1179656 | tf_op jit(solution)/shard_map/ppermute | solution.py:540

commit v3 on v2

--- a/solution.py
+++ b/solution.py
@@ -16,8 +16,40 @@
 NT = (((1,), (1,)), ((), ()))
 NN = (((1,), (0,)), ((), ()))
 
+def near(value):
+    return pltpu.with_memory_space_constraint(value, pltpu.VMEM)
+
+
 def dot(a, b, dims=NN):
     return lax.dot_general(a, b, dims, preferred_element_type=F32)
+
+
+def fetch_kernel(frames, out_grad, weight, frames_out, grad_out, weight_out, sems):
+    copies = [
+        pltpu.make_async_copy(source, target, sems.at[k])
+        for k, (source, target) in enumerate(
+            ((frames, frames_out), (out_grad, grad_out), (weight, weight_out))
+        )
+    ]
+    for copy in copies:
+        copy.start()
+    for copy in copies:
+        copy.wait()
+
+
+def fetch(frames, out_grad, weight):
+    return pl.pallas_call(
+        fetch_kernel,
+        out_shape=[pltpu.VMEM(value.shape, BF16) for value in (frames, out_grad, weight)],
+        in_specs=[ANY] * 3,
+        out_specs=[VMEM] * 3,
+        scratch_shapes=[pltpu.SemaphoreType.DMA((3,))],
+        compiler_params=pltpu.CompilerParams(vmem_limit_bytes=52 * 2**20),
+        cost_estimate=pl.CostEstimate(
+            flops=0, bytes_accessed=20 * 2**20, transcendentals=0
+        ),
+        name="fetch",
+    )(frames, out_grad, weight)
 
 
 def fold_kernel(weight, folded, sems):
@@ -44,7 +76,7 @@
     return pl.pallas_call(
         fold_kernel,
         out_shape=pltpu.VMEM((9, wide, wide), BF16),
-        in_specs=[ANY],
+        in_specs=[VMEM],
         out_specs=VMEM,
         scratch_shapes=[pltpu.SemaphoreType.DMA((9, 4))],
         compiler_params=pltpu.CompilerParams(vmem_limit_bytes=4 * 2**20),
@@ -52,7 +84,7 @@
             flops=0, bytes_accessed=20 * 2**20, transcendentals=0
         ),
         name="fold",
-    )(weight)
+    )(near(weight))
 
 
 def store_pairs(values_of, sides, count, even, odd):
@@ -86,20 +118,22 @@
     store_pairs(both, (0, 2), count, even, odd)
 
 
-def add_taps(total, side, even, odd, weight_of, dims, extra=None):
-    rows = odd.shape[1]
-    for off in range(3):
-        if off == 1:
-            lhs = odd[side, 0:rows, :]
-        else:
-            lhs = even[side, 8 * off : 8 * off + rows, :]
-        if extra is not None:
-            lhs = jnp.concatenate([lhs, extra(side, off)], axis=0)
-        part = dot(lhs, weight_of(off, side), dims)
-        if (side, off) == (1, 0):
-            total[...] = part
-        else:
-            total[...] += part
+def sum_taps(total, at, rows, sides, even, odd, weight_of, dims, extra=None):
+    count = rows
+    for side in sides:
+        for off in range(3):
+            if off == 1:
+                lhs = odd[side, at : at + rows, :]
+            else:
+                lhs = even[side, at + 8 * off : at + 8 * off + rows, :]
+            if extra is not None:
+                lhs = jnp.concatenate([lhs, extra(side, off)], axis=0)
+                count = lhs.shape[0]
+            part = dot(lhs, weight_of(off, side), dims)
+            if (side, off) == (1, 0):
+                total[at : at + count, :] = part
+            else:
+                total[at : at + count, :] += part
 
 
 def pack_kernel(place, frames, out_grad, before, after, core_out, chip_out, wide_f, wide_g):
@@ -151,7 +185,7 @@
     rows = 3 * count + 16
     return pl.pallas_call(
         pack_kernel,
-        out_shape=[jax.ShapeDtypeStruct((rows, 2 * chans), BF16)] * 2,
+        out_shape=[pltpu.VMEM((rows, 2 * chans), BF16)] * 2,
         in_specs=[SMEM] + [VMEM] * 4,
         out_specs=[VMEM] * 2,
         scratch_shapes=[
@@ -160,7 +194,7 @@
         ],
         compiler_params=pltpu.CompilerParams(vmem_limit_bytes=24 * 2**20),
         name="pack",
-    )(place, frames, out_grad, before, after)
+    )(place, near(frames), near(out_grad), near(before), near(after))
 
 
 def forward_kernel(
@@ -182,9 +216,6 @@
     low_out,
     high_out,
     grad_out,
-    block,
-    grad_block,
-    grad_done,
     down_block,
     own_low,
     own_high,
@@ -200,20 +231,8 @@
     count = frames.shape[0]
     ahead = count + 2
     rows = 8 * ahead
-    first = [
-        pltpu.make_async_copy(frames.at[:, h], block.at[:, :, pl.ds(h * chans, chans)], sems.at[h])
-        for h in range(2)
-    ]
-    for copy in first:
-        copy.start()
-    later = [
-        pltpu.make_async_copy(
-            out_grad.at[:, h], grad_block.at[:, :, pl.ds(h * chans, chans)], sems.at[2 + h]
-        )
-        for h in range(2)
-    ] + [pltpu.make_async_copy(down, down_block, sems.at[4])]
-    for copy in later:
-        copy.start()
+    fetch_down = pltpu.make_async_copy(down, down_block, sems.at[0])
+    fetch_down.start()
     even_core = place[1] == 0
 
     def pick(core, chip, at_low, at_high):
@@ -223,13 +242,14 @@
 
     pick(core_sent, chip_sent, own_low, own_high)
     pick(core_got, chip_got, low, high)
-    for copy in first:
-        copy.wait()
 
     def frame_of(t):
-        if 2 <= t < count + 2:
-            return block[t - 2]
-        part = (lambda h: before[t, h]) if t < 2 else (lambda h: after[t - count - 2, h])
+        if t < 2:
+            part = lambda h: before[t, h]
+        elif t < count + 2:
+            part = lambda h: frames[t - 2, h]
+        else:
+            part = lambda h: after[t - count - 2, h]
         return jnp.concatenate([part(0).astype(F32), part(1).astype(F32)], axis=1)
 
     span = count + 4
@@ -245,7 +265,25 @@
     def weight_of(off, side):
         return folded[3 * off + side]
 
-    add_taps(total, 1, even, odd, weight_of, NN, rim)
+    def gates(pre):
+        gate = 0.5 * jnp.tanh(0.5 * pre) + 0.5
+        return gate, gate * (1.0 + pre * (1.0 - gate))
+
+    def finish(first, last):
+        for j in range(first, last):
+            pre = total[64 * j : 64 * (j + 1), :]
+            gate, slope = gates(pre)
+            silu = pre * gate
+            for h in range(2):
+                lanes = slice(h * chans, (h + 1) * chans)
+                own = frames[8 * j : 8 * (j + 1), h].astype(F32)
+                act[j, :, :, lanes] = own + silu[:, lanes].reshape(own.shape)
+                grad = out_grad[8 * j : 8 * (j + 1), h].astype(F32)
+                grad = grad * slope[:, lanes].reshape(own.shape)
+                grad_out[8 * j : 8 * (j + 1), :, lanes] = grad.astype(BF16)
+
+    half = 64 * (count // 16)
+    sum_taps(total, 0, half, (1,), even, odd, weight_of, NN)
     build_sides(
         frame_of,
         lambda t: low[span + t : span + t + 1, :],
@@ -254,34 +292,21 @@
         even,
         odd,
     )
-    for side in (0, 2):
-        add_taps(total, side, even, odd, weight_of, NN, rim)
-    for copy in later:
-        copy.wait()
-
-    def gates(pre):
-        gate = 1.0 / (1.0 + jnp.exp(-pre))
-        return gate, gate * (1.0 + pre * (1.0 - gate))
-
-    for j in range(count // 8):
-        pre = total[64 * j : 64 * (j + 1), :]
-        gate, slope = gates(pre)
-        own = block[8 * j : 8 * (j + 1)].astype(F32)
-        act[j] = own + (pre * gate).reshape(own.shape)
-        grad = grad_block[8 * j : 8 * (j + 1)].astype(F32) * slope.reshape(own.shape)
-        grad_done[8 * j : 8 * (j + 1)] = grad.astype(BF16)
+    sum_taps(total, 0, half, (0, 2), even, odd, weight_of, NN)
+    sum_taps(total, half, rows - half, (1, 0, 2), even, odd, weight_of, NN, rim)
+    finish(0, count // 16)
+    finish(count // 16, count // 8)
     for t in range(2):
         at = 8 * (count + t)
         _, slope = gates(total[at : at + 8, :])
         grad = jnp.concatenate([after[2 + t, 0].astype(F32), after[2 + t, 1].astype(F32)], axis=1)
-        grad_done[count + t] = (grad * slope).astype(BF16)
-    write = pltpu.make_async_copy(grad_done, grad_out, sems.at[5])
-    write.start()
+        grad_out[count + t] = (grad * slope).astype(BF16)
     for at, (source, target) in enumerate(((low, low_out), (high, high_out))):
         base = rows + at * (ahead + 6)
         _, slope = gates(total[base : base + ahead + 6, :])
         target[...] = slope * source[2 * span : 2 * span + ahead + 6, :]
 
+    fetch_down.wait()
     latent = jnp.zeros((2 * count, chans), F32)
     for k in range(8):
         lhs = jnp.concatenate(
@@ -310,7 +335,6 @@
         latent_out[j] = rounded[j]
     for k in range(tail_out.shape[0]):
         tail_out[k] = running
-    write.wait()
 
 
 def forward(peers, place, lengths, frames, before, after, columns, out_grad, down, folded):
@@ -323,19 +347,16 @@
     return pl.pallas_call(
         forward_kernel,
         out_shape=(
-            jax.ShapeDtypeStruct((lat, 16, chans), F32),
-            jax.ShapeDtypeStruct((lat, 16, chans), F32),
-            jax.ShapeDtypeStruct((peers, 16, chans), F32),
-            jax.ShapeDtypeStruct((ahead + 6, wide), F32),
-            jax.ShapeDtypeStruct((ahead + 6, wide), F32),
-            jax.ShapeDtypeStruct((ahead, cols, wide), BF16),
+            pltpu.VMEM((lat, 16, chans), F32),
+            pltpu.VMEM((lat, 16, chans), F32),
+            pltpu.VMEM((peers, 16, chans), F32),
+            pltpu.VMEM((ahead + 6, wide), F32),
+            pltpu.VMEM((ahead + 6, wide), F32),
+            pltpu.VMEM((ahead, cols, wide), BF16),
         ),
-        in_specs=[SMEM, SMEM, ANY] + [VMEM] * 6 + [ANY, ANY, VMEM],
-        out_specs=[VMEM] * 5 + [ANY],
+        in_specs=[SMEM, SMEM] + [VMEM] * 8 + [ANY, VMEM],
+        out_specs=[VMEM] * 6,
         scratch_shapes=[
-            pltpu.VMEM((count, cols, wide), BF16),
-            pltpu.VMEM((count, cols, wide), BF16),
-            pltpu.VMEM((ahead, cols, wide), BF16),
             pltpu.VMEM(down.shape, BF16),
             pltpu.VMEM(received, F32),
             pltpu.VMEM(received, F32),
@@ -345,14 +366,20 @@
             pltpu.VMEM((3, rows, wide), BF16),
             pltpu.VMEM((rows + 2 * (ahead + 6), wide), F32),
             pltpu.VMEM((lat, 8, cols, wide), F32),
-            pltpu.SemaphoreType.DMA((6,)),
+            pltpu.SemaphoreType.DMA((1,)),
         ],
-        compiler_params=pltpu.CompilerParams(vmem_limit_bytes=44 * 2**20),
+        compiler_params=pltpu.CompilerParams(vmem_limit_bytes=28 * 2**20),
         cost_estimate=pl.CostEstimate(
             flops=2 * 9 * rows * wide * wide, bytes_accessed=16 * 2**20, transcendentals=rows * wide
         ),
         name="forward",
-    )(place, lengths, frames, before, after, *columns, out_grad, down, pltpu.with_memory_space_constraint(folded, pltpu.VMEM))
+    )(
+        place,
+        lengths,
+        *(near(value) for value in (frames, before, after, *columns, out_grad)),
+        down,
+        near(folded),
+    )
 
 
 def backward_kernel(
@@ -362,8 +389,6 @@
     out_grad,
     folded,
     result,
-    block,
-    source,
     done,
     even,
     odd,
@@ -371,20 +396,32 @@
     sems,
 ):
     count, _, cols, chans = out_grad.shape
-    first = pltpu.make_async_copy(grad, block, sems.at[0])
-    first.start()
-    later = pltpu.make_async_copy(out_grad, source, sems.at[1])
-    later.start()
-    first.wait()
 
     def frame_of(t):
-        return block[t]
+        return grad[t]
 
     def weight_of(off, side):
         return folded[3 * (2 - off) + 2 - side]
 
+    writes = []
+    half = count // 2
+
+    def finish(first, last):
+        for j in range(first, last, 8):
+            part = total[8 * j : 8 * (j + 8), :]
+            for h in range(2):
+                mine = part[:, h * chans : (h + 1) * chans].reshape(8, cols, chans)
+                done[j : j + 8, h] = (out_grad[j : j + 8, h].astype(F32) + mine).astype(BF16)
+        write = pltpu.make_async_copy(
+            done.at[pl.ds(first, last - first)],
+            result.at[pl.ds(first, last - first)],
+            sems.at[len(writes)],
+        )
+        write.start()
+        writes.append(write)
+
     build_centre(frame_of, count + 2, even, odd)
-    add_taps(total, 1, even, odd, weight_of, NT)
+    sum_taps(total, 0, 8 * half, (1,), even, odd, weight_of, NT)
     build_sides(
         frame_of,
         lambda t: low[t : t + 1, :],
@@ -393,24 +430,11 @@
         even,
         odd,
     )
-    add_taps(total, 0, even, odd, weight_of, NT)
-    add_taps(total, 2, even, odd, weight_of, NT)
-    later.wait()
-    writes = []
-    step = count // 4
-    for j in range(4):
-        at = slice(8 * step * j, 8 * step * (j + 1))
-        part = total[at, :]
-        for h in range(2):
-            mine = part[:, h * chans : (h + 1) * chans].reshape(step, cols, chans)
-            done[step * j : step * (j + 1), h] = (
-                source[step * j : step * (j + 1), h].astype(F32) + mine
-            ).astype(BF16)
-        write = pltpu.make_async_copy(
-            done.at[pl.ds(step * j, step)], result.at[pl.ds(step * j, step)], sems.at[2 + j]
-        )
-        write.start()
-        writes.append(write)
+    sum_taps(total, 0, 8 * half, (0, 2), even, odd, weight_of, NT)
+    sum_taps(total, 8 * half, 8 * half, (1, 0, 2), even, odd, weight_of, NT)
+    finish(0, half)
+    finish(half, half + half // 2)
+    finish(half + half // 2, count)
     for write in writes:
         write.wait()
 
@@ -421,23 +445,21 @@
     return pl.pallas_call(
         backward_kernel,
         out_shape=jax.ShapeDtypeStruct(out_grad.shape, BF16),
-        in_specs=[ANY, VMEM, VMEM, ANY, VMEM],
+        in_specs=[VMEM] * 5,
         out_specs=ANY,
         scratch_shapes=[
-            pltpu.VMEM(grad.shape, BF16),
-            pltpu.VMEM(out_grad.shape, BF16),
             pltpu.VMEM(out_grad.shape, BF16),
             pltpu.VMEM((3, rows + 16, wide), BF16),
             pltpu.VMEM((3, rows, wide), BF16),
             pltpu.VMEM((rows, wide), F32),
-            pltpu.SemaphoreType.DMA((6,)),
+            pltpu.SemaphoreType.DMA((3,)),
         ],
-        compiler_params=pltpu.CompilerParams(vmem_limit_bytes=44 * 2**20),
+        compiler_params=pltpu.CompilerParams(vmem_limit_bytes=24 * 2**20),
         cost_estimate=pl.CostEstimate(
             flops=2 * 9 * rows * wide * wide, bytes_accessed=12 * 2**20, transcendentals=0
         ),
         name="backward",
-    )(grad, low, high, out_grad, pltpu.with_memory_space_constraint(folded, pltpu.VMEM))
+    )(*(near(value) for value in (grad, low, high, out_grad, folded)))
 
 
 def mix_kernel(place, lengths, latent, sums, tails, mixed):
@@ -472,7 +494,7 @@
         out_specs=VMEM,
         compiler_params=pltpu.CompilerParams(vmem_limit_bytes=16 * 2**20),
         name="mix",
-    )(place, lengths, latent, sums, tails)
+    )(place, lengths, near(latent), near(sums), near(tails))
 
 
 def attend_kernel(labels, mine, *refs):
@@ -570,25 +592,27 @@
     place = jnp.stack([lax.axis_index("tm"), lax.axis_index("scene") % 2]).astype(jnp.int32)
     before = shifted(frames[count - 2 :], "tm", 1)
     after = shifted(jnp.concatenate([frames[:2], out_grad[:2]], axis=0), "tm", -1)
-    folded = fold(conv_weight)
-    sent = pack(place, frames, out_grad, before, after)
-    columns = (*sent, with_core(sent[0]), with_chip(sent[1]))
+    near_frames, near_grad, near_weight = fetch(frames, out_grad, conv_weight)
+    (before, after), near_weight = lax.optimization_barrier(((before, after), near_weight))
+    sent = pack(place, near_frames, near_grad, before, after)
+    received = (with_core(sent[0]), with_chip(sent[1]))
+    received, folded = lax.optimization_barrier((received, fold(near_weight)))
     latent, sums, tail, low, high, grad = forward(
         lax.axis_size("tm"),
         place,
         shot_lengths,
-        frames,
+        near_frames,
         before,
         after,
-        columns,
-        out_grad,
+        (*sent, *received),
+        near_grad,
         down_weight,
         folded,
     )
     tails = lax.all_to_all(tail, "tm", 0, 0, tiled=True)
     mixed = mix(place, shot_lengths, latent, sums, tails)
     chips = chip_shifts(mixed)
-    frame_grad = backward(grad, low, high, out_grad, folded)
+    frame_grad = backward(grad, low, high, near_grad, folded)
     chips, frame_grad = lax.optimization_barrier((chips, frame_grad))
     own = jnp.concatenate([mixed, *chips], axis=0)
     pieces = [own, with_core(own)]

time: 83.3 us -> 74.3 us (0.89)
  local copies, waits for them, and re-layouts: 10.1 us -> 1.63 us
  waiting for transfers between devices: 2.44 us -> 4.91 us
  Pallas kernels: 31.1 us -> 29.6 us
  blocking collectives: 19.2 us -> 17.7 us
    unnamed x39 -> x19, local copies, waits for them, and re-layouts: 8.63 us -> 0.12 us
    ppermute x1, waiting for transfers between devices: 0.32 us -> 3.62 us  [with_chip(): return lax.ppermute(value, 'scene', pairs + [(b, a) for a, b in pairs])]
    pallas_call x1, Pallas kernels: 8.92 us -> 6.78 us  [backward(): pl.pallas_call(backward_kernel, out_shape=jax.ShapeDtypeStruct(out_grad.s...]
    all_to_all x1, blocking collectives: 19.2 us -> 17.7 us  [per_device(): tails = lax.all_to_all(tail, 'tm', 0, 0, tiled=True)]
    ppermute x2, waiting for transfers between devices: 0.84 us -> 0.01 us  [shifted(): lax.ppermute(value, axis, [(i, i + steps) for i in range(count) if 0 <= i...]
    pallas_call x2 -> x3, Pallas kernels: 14.9 us -> 15.5 us  [the longest x1 10.6 us: forward(): pl.pallas_call(forward_kernel, out_shape=(pltpu.VMEM((lat, 16, chans), F3...]
  transfers between devices with their start and end apart: 8 -> 8, of which waited for: 3 -> 2; matrix products, arithmetic and copies ran while one was open for 0% -> 0% of each run, Pallas kernels for 13% -> 16%
where the time goes in v3:
time: 74.3 us; the launch traced here: 73.9 us
  Pallas kernels  29.6 us (40%)
  starting transfers between devices  19.2 us (26%)
  blocking collectives  17.7 us (24%)
  waiting for transfers between devices  4.91 us (7%)
  local copies, waits for them, and re-layouts  1.63 us (2%)
  between operations  0.82 us (1%)
    all_to_all x1, blocking collectives, per_device(): tails = lax.all_to_all(tail, 'tm', 0, 0, tiled=True)  17.7 us
    pallas_call x1, Pallas kernels, forward(): pl.pallas_call(forward_kernel, out_shape=(pltpu.VMEM((lat, 16, chans), F3...  10.6 us
    pallas_call x1, Pallas kernels, backward(): pl.pallas_call(backward_kernel, out_shape=jax.ShapeDtypeStruct(out_grad.s...  6.78 us
    ppermute x3, starting transfers between devices, chip_shifts(): lax.ppermute(value, 'scene', [(i, (i + 2 * k) % count) for i in range(cou...  6.21 us
    ppermute x2, starting transfers between devices, shifted(): lax.ppermute(value, axis, [(i, i + steps) for i in range(count) if 0 <= i...  5.95 us
    pallas_call x1, Pallas kernels, attend(): pl.pallas_call(attend_kernel, out_shape=jax.ShapeDtypeStruct((labels.shap...  5.09 us
    pallas_call x1, Pallas kernels, fetch(): pl.pallas_call(fetch_kernel, out_shape=[pltpu.VMEM(value.shape, BF16) for...  3.78 us
    ppermute x2, starting transfers between devices, with_core(): return lax.ppermute(value, 'scene', [(i, i ^ 1) for i in range(count)])  3.78 us
  transfers between devices with their start and end apart: 8, of which 2 were waited for; matrix products, arithmetic and copies ran while one was open for 0% of the time, Pallas kernels for 16%

profile of v3, /device:TPU:1, one launch (start us, length us, event | category | flops | bytes accessed | tf_op | source)
XLA Modules:
  0.0 73.9 jit_solution(9153219900653051259)
XLA Ops:
  0.6 0.8 %fusion = (bf16[2,2,8,384]{3,2,1,0:T(8,128)(2,1)S(1)}, bf16[2,2,8,384]{3,2,1,0:T(8,128)(2,1)S(1)}) fusion(bf16[64,2,8,384]{3,2,1,0:T(8,128)(2,1)} %frames.1), kind=kLoop, calls=%fused_computation.3 | loop fusion | bytes 98304 | tf_op jit(solution)/shard_map/slice | solution.py:594
  1.4 0.7 %slice.11 = bf16[2,2,8,384]{3,2,1,0:T(8,128)(2,1)S(1)} slice(bf16[64,2,8,384]{3,2,1,0:T(8,128)(2,1)} %out_grad.1), slice={[0:2], [0:2], [0:8], [0:384]} | slice | bytes 49152 | tf_op jit(solution)/shard_map/slice | solution.py:594
  2.1 1.3 %collective-permute-start.1 = (bf16[4,2,8,384]{3,2,1,0:T(8,128)(2,1)S(1)}, bf16[4,2,8,384]{3,2,1,0:T(8,128)(2,1)S(1)}, u32[]{:S(2)}, u32[]{:S(2)}) collective-permute-start(bf16[4,2,8,384]{3,2,1,0:T(8,128)(2,1)S(1)} %pad_maximum_fusion.1), channel_id=1, source_target_pairs={{8,0},{16,8},{24,16},{32,24},{40,32},{48,40},{56,48},{64,56},{72,6... | collective-permute-start | bytes 147464 | tf_op jit(solution)/shard_map/ppermute | solution.py:555
  3.4 4.7 %collective-permute-start = (bf16[2,2,8,384]{3,2,1,0:T(8,128)(2,1)S(1)}, bf16[2,2,8,384]{3,2,1,0:T(8,128)(2,1)S(1)}, u32[]{:S(2)}, u32[]{:S(2)}) collective-permute-start(bf16[2,2,8,384]{3,2,1,0:T(8,128)(2,1)S(1)} %get-tuple-element.45), channel_id=1, source_target_pairs={{0,8},{8,16},{16,24},{24,32},{32,40},{40,48},{48,56},{56,64},{64,7... | collective-permute-start | bytes 73736 | tf_op jit(solution)/shard_map/ppermute | solution.py:555
  8.1 0.1 pad_add_fusion.place
  8.2 3.8 %fetch.1 = (bf16[64,2,8,384]{3,2,1,0:T(8,128)(2,1)S(1)}, bf16[64,2,8,384]{3,2,1,0:T(8,128)(2,1)S(1)}, bf16[3,3,3,384,384]{4,3,2,1,0:T(8,128)(2,1)S(1)}) custom-call(bf16[64,2,8,384]{3,2,1,0:T(8,128)(2,1)} %frames.1, bf16[64,2,8,384]{3,2,1,0:T(8,128)(2,1)} %out_grad.1, bf16[3,3,3,384,384]{4,3,2,1,0:T(8,128)(2,1)} %weight.1), custom_call_target="tpu_custom_call" | custom-call | bytes 20971520 | tf_op jit(solution)/shard_map/fetch/pallas_call | solution.py:41
  12.0 0.0 copy-start
  12.0 0.0 collective-permute-done.before
  12.0 0.0 collective-permute-done.1.after
  12.0 1.1 %pack.1 = (bf16[208,768]{1,0:T(8,128)(2,1)S(1)}, bf16[208,768]{1,0:T(8,128)(2,1)S(1)}) custom-call(s32[2]{0:T(128)S(1)} %pad_add_fusion.place, bf16[64,2,8,384]{3,2,1,0:T(8,128)(2,1)S(1)} %get-tuple-element.23.frames, bf16[64,2,8,384]{3,2,1,0:T(8,128)(2,1)S(1)} %get-tuple-element.27.out_grad, bf16[2,2,8,384]{3,2,1,0:T(8,128)(2,1)S(1)} %collective-permute-done.before, ...), custom_call_target="tpu_custom_call" | custom-call | tf_op jit(solution)/shard_map/pack/pallas_call | solution.py:186
  13.2 1.4 %collective-permute-start.2 = (bf16[208,768]{1,0:T(8,128)(2,1)S(1)}, bf16[208,768]{1,0:T(8,128)(2,1)S(1)}, u32[]{:S(2)}, u32[]{:S(2)}) collective-permute-start(bf16[208,768]{1,0:T(8,128)(2,1)S(1)} %get-tuple-element.28.core_sent), channel_id=1, source_target_pairs={{0,1},{1,0},{2,3},{3,2},{4,5},{5,4},{6,7},{7,6},{8,9},{9,8},{10,11... | collective-permute-start | bytes 958472 | tf_op jit(solution)/shard_map/ppermute | solution.py:562
  14.6 0.0 copy-done
  14.6 3.3 %collective-permute-start.3 = (bf16[208,768]{1,0:T(8,128)(2,1)S(1)}, bf16[208,768]{1,0:T(8,128)(2,1)S(1)}, u32[]{:S(2)}, u32[]{:S(2)}) collective-permute-start(bf16[208,768]{1,0:T(8,128)(2,1)S(1)} %get-tuple-element.29.chip_sent), channel_id=1, source_target_pairs={{1,2},{3,4},{5,6},{2,1},{4,3},{6,5},{9,10},{11,12},{13,14},{10,9},... | collective-permute-start | bytes 958472 | tf_op jit(solution)/shard_map/ppermute | solution.py:568
  17.8 0.0 copy-start.1
  17.9 1.5 %fold.1.folded = bf16[9,768,768]{2,1,0:T(8,128)(2,1)S(1)} custom-call(bf16[3,3,3,384,384]{4,3,2,1,0:T(8,128)(2,1)S(1)} %get-tuple-element.30.weight), custom_call_target="tpu_custom_call" | custom-call | bytes 20971520 | tf_op jit(solution)/shard_map/fold/pallas_call | solution.py:76
  19.4 0.0 collective-permute-done.2.core_got
  19.4 3.6 %collective-permute-done.3.chip_got = bf16[208,768]{1,0:T(8,128)(2,1)S(1)} collective-permute-done((bf16[208,768]{1,0:T(8,128)(2,1)S(1)}, bf16[208,768]{1,0:T(8,128)(2,1)S(1)}, u32[]{:S(2)}, u32[]{:S(2)}) %collective-permute-start.3) | collective-permute-done | bytes 319520 | tf_op jit(solution)/shard_map/ppermute | solution.py:568
  23.0 10.6 %forward.1 = (f32[8,16,384]{2,1,0:T(8,128)S(1)}, f32[8,16,384]{2,1,0:T(8,128)S(1)}, f32[16,16,384]{2,1,0:T(8,128)S(1)}, f32[72,768]{1,0:T(8,128)S(1)}, f32[72,76...) custom-call(s32[2]{0:T(128)S(1)} %pad_add_fusion.place, s32[8]{0:T(128)S(1)} %copy-done.6, ...), custom_call_target="tpu_custom_call" | custom-call | flops 5605687296 | bytes 16777216 | tf_op jit(solution)/shard_map/forward/pallas_call | solution.py:347
  33.6 17.7 %all_to_all.5.tails = f32[16,16,384]{2,1,0:T(8,128)S(1)} all-to-all(f32[16,16,384]{2,1,0:T(8,128)S(1)} %get-tuple-element.36), channel_id=1, replica_groups=mesh['tm'=16,'scene'=8] {'tm'}, dimensions={0} | all-to-all | bytes 786432 | tf_op jit(solution)/shard_map/all_to_all | solution.py:612
  51.3 0.7 mix.1.mine
  52.0 2.6 %collective-permute-start.4 = (bf16[128,384]{1,0:T(8,128)(2,1)S(1)}, bf16[128,384]{1,0:T(8,128)(2,1)S(1)}, u32[]{:S(2)}, u32[]{:S(2)}) collective-permute-start(bf16[128,384]{1,0:T(8,128)(2,1)S(1)} %mix.1.mine), channel_id=1, source_target_pairs={{0,2},{1,3},{2,4},{3,5},{4,6},{5,7},{6,0},{7,1},{8,10},{9,11},{10,... | collective-permute-start | bytes 294920 | tf_op jit(solution)/shard_map/ppermute | solution.py:574
  54.6 1.6 %collective-permute-start.5 = (bf16[128,384]{1,0:T(8,128)(2,1)S(1)}, bf16[128,384]{1,0:T(8,128)(2,1)S(1)}, u32[]{:S(2)}, u32[]{:S(2)}) collective-permute-start(bf16[128,384]{1,0:T(8,128)(2,1)S(1)} %mix.1.mine), channel_id=1, source_target_pairs={{0,4},{1,5},{2,6},{3,7},{4,0},{5,1},{6,2},{7,3},{8,12},{9,13},{10,... | collective-permute-start | bytes 294920 | tf_op jit(solution)/shard_map/ppermute | solution.py:574
  56.2 2.0 %collective-permute-start.6 = (bf16[128,384]{1,0:T(8,128)(2,1)S(1)}, bf16[128,384]{1,0:T(8,128)(2,1)S(1)}, u32[]{:S(2)}, u32[]{:S(2)}) collective-permute-start(bf16[128,384]{1,0:T(8,128)(2,1)S(1)} %mix.1.mine), channel_id=1, source_target_pairs={{0,6},{1,7},{2,0},{3,1},{4,2},{5,3},{6,4},{7,5},{8,14},{9,15},{10,... | collective-permute-start | bytes 294920 | tf_op jit(solution)/shard_map/ppermute | solution.py:574
  58.2 0.0 copy-start.5
  58.2 6.8 %backward.1 = bf16[64,2,8,384]{3,2,1,0:T(8,128)(2,1)} custom-call(bf16[66,8,768]{2,1,0:T(8,128)(2,1)S(1)} %get-tuple-element.37.grad, f32[72,768]{1,0:T(8,128)S(1)} %get-tuple-element.38.low, f32[72,768]{1,0:T(8,128)S(1)} %get-tuple-element.39.high, bf16[64,2,8,384]{3,2,1,0:T(8,128)(2,1)S(1)} %get-tuple-element.27.out_grad, bf16[9,768,768]{2,1,0:T(8,128)(2,1)S(1)} %fold.1.folded), custom_call_target="tpu_custom_call" | custom-call | flops 5435817984 | bytes 12582912 | tf_op jit(solution)/shard_map/backward/pallas_call | solution.py:445
  65.0 0.0 collective-permute-done.4
  65.0 0.0 collective-permute-done.5
  65.0 0.0 collective-permute-done.6
  65.1 2.4 %collective-permute-start.7 = (bf16[512,384]{1,0:T(8,128)(2,1)S(1)}, bf16[512,384]{1,0:T(8,128)(2,1)S(1)}, u32[]{:S(2)}, u32[]{:S(2)}) collective-permute-start(bf16[512,384]{1,0:T(8,128)(2,1)S(1)} %pad_maximum_fusion.refs_0_), channel_id=1, source_target_pairs={{0,1},{1,0},{2,3},{3,2},{4,5},{5,4},{6,7},{7,6},{8,9},{9,8},{10,11... | collective-permute-start | bytes 1179656 | tf_op jit(solution)/shard_map/ppermute | solution.py:562
  67.5 0.1 copy.12.labels
  67.6 1.3 %collective-permute-done.7.refs_1_ = bf16[512,384]{1,0:T(8,128)(2,1)S(1)} collective-permute-done((bf16[512,384]{1,0:T(8,128)(2,1)S(1)}, bf16[512,384]{1,0:T(8,128)(2,1)S(1)}, u32[]{:S(2)}, u32[]{:S(2)}) %collective-permute-start.7) | collective-permute-done | bytes 393248 | tf_op jit(solution)/shard_map/ppermute | solution.py:562
  68.9 5.1 %attend.1 = bf16[8,2,8,384]{3,2,1,0:T(8,128)(2,1)} custom-call(s32[8,1]{1,0:T(8,128)S(1)} %copy.12.labels, bf16[128,384]{1,0:T(8,128)(2,1)S(1)} %mix.1.mine, bf16[512,384]{1,0:T(8,128)(2,1)S(1)} %pad_maximum_fusion.refs_0_, bf16[512,384]{1,0:T(8,128)(2,1)S(1)} %collective-permute-done.7.refs_1_, bf16[384,384]{1,0:T(8,128)(2,1)S(1)} %copy-done.2, ...), custom_call_target="tpu_custom_call" | custom-call | tf_op jit(solution)/shard_map/attend/pallas_call | solution.py:542
  (16 shorter events, 0.1 us)
Async XLA Ops:
  2.1 9.9 %collective-permute-start.1 = (bf16[4,2,8,384]{3,2,1,0:T(8,128)(2,1)S(1)}, bf16[4,2,8,384]{3,2,1,0:T(8,128)(2,1)S(1)}, u32[]{:S(2)}, u32[]{:S(2)}) collective-permute-start(bf16[4,2,8,384]{3,2,1,0:T(8,128)(2,1)S(1)} %pad_maximum_fusion.1), channel_id=1, source_target_pairs={{8,0},{16,8},{24,16},{32,24},{40,32},{48,40},{56,48},{64,56},{72,6... | collective-permute-start | bytes 147464 | tf_op jit(solution)/shard_map/ppermute | solution.py:555
  3.4 8.6 %collective-permute-start = (bf16[2,2,8,384]{3,2,1,0:T(8,128)(2,1)S(1)}, bf16[2,2,8,384]{3,2,1,0:T(8,128)(2,1)S(1)}, u32[]{:S(2)}, u32[]{:S(2)}) collective-permute-start(bf16[2,2,8,384]{3,2,1,0:T(8,128)(2,1)S(1)} %get-tuple-element.45), channel_id=1, source_target_pairs={{0,8},{8,16},{16,24},{24,32},{32,40},{40,48},{48,56},{56,64},{64,7... | collective-permute-start | bytes 73736 | tf_op jit(solution)/shard_map/ppermute | solution.py:555
  12.0 2.6 %copy-start = (bf16[64,2,8,384]{3,2,1,0:T(8,128)(2,1)}, bf16[64,2,8,384]{3,2,1,0:T(8,128)(2,1)S(1)}, u32[]{:S(2)}) copy-start(bf16[64,2,8,384]{3,2,1,0:T(8,128)(2,1)S(1)} %get-tuple-element.23.frames) | copy-start | bytes 2359300
  13.2 6.2 %collective-permute-start.2 = (bf16[208,768]{1,0:T(8,128)(2,1)S(1)}, bf16[208,768]{1,0:T(8,128)(2,1)S(1)}, u32[]{:S(2)}, u32[]{:S(2)}) collective-permute-start(bf16[208,768]{1,0:T(8,128)(2,1)S(1)} %get-tuple-element.28.core_sent), channel_id=1, source_target_pairs={{0,1},{1,0},{2,3},{3,2},{4,5},{5,4},{6,7},{7,6},{8,9},{9,8},{10,11... | collective-permute-start | bytes 958472 | tf_op jit(solution)/shard_map/ppermute | solution.py:562
  14.6 8.4 %copy-start.6 = (s32[8]{0:T(128)S(1)}, s32[8]{0:T(128)}, u32[]{:S(2)}) copy-start(s32[8]{0:T(128)} %lengths.3) | copy-start | bytes 100
  14.6 8.4 %copy-start.7 = (bf16[8,384,384]{2,1,0:T(8,128)(2,1)S(1)}, bf16[8,384,384]{2,1,0:T(8,128)(2,1)}, u32[]{:S(2)}) copy-start(bf16[8,384,384]{2,1,0:T(8,128)(2,1)} %down.1) | copy-start | bytes 7077892
  14.6 8.4 %collective-permute-start.3 = (bf16[208,768]{1,0:T(8,128)(2,1)S(1)}, bf16[208,768]{1,0:T(8,128)(2,1)S(1)}, u32[]{:S(2)}, u32[]{:S(2)}) collective-permute-start(bf16[208,768]{1,0:T(8,128)(2,1)S(1)} %get-tuple-element.29.chip_sent), channel_id=1, source_target_pairs={{1,2},{3,4},{5,6},{2,1},{4,3},{6,5},{9,10},{11,12},{13,14},{10,9},... | collective-permute-start | bytes 958472 | tf_op jit(solution)/shard_map/ppermute | solution.py:568
  17.8 5.2 %copy-start.1 = (bf16[64,2,8,384]{3,2,1,0:T(8,128)(2,1)S(1)}, bf16[64,2,8,384]{3,2,1,0:T(8,128)(2,1)}, u32[]{:S(2)}) copy-start(bf16[64,2,8,384]{3,2,1,0:T(8,128)(2,1)} %copy-done) | copy-start | bytes 2359300
  52.0 13.0 %collective-permute-start.4 = (bf16[128,384]{1,0:T(8,128)(2,1)S(1)}, bf16[128,384]{1,0:T(8,128)(2,1)S(1)}, u32[]{:S(2)}, u32[]{:S(2)}) collective-permute-start(bf16[128,384]{1,0:T(8,128)(2,1)S(1)} %mix.1.mine), channel_id=1, source_target_pairs={{0,2},{1,3},{2,4},{3,5},{4,6},{5,7},{6,0},{7,1},{8,10},{9,11},{10,... | collective-permute-start | bytes 294920 | tf_op jit(solution)/shard_map/ppermute | solution.py:574
  54.6 10.4 %collective-permute-start.5 = (bf16[128,384]{1,0:T(8,128)(2,1)S(1)}, bf16[128,384]{1,0:T(8,128)(2,1)S(1)}, u32[]{:S(2)}, u32[]{:S(2)}) collective-permute-start(bf16[128,384]{1,0:T(8,128)(2,1)S(1)} %mix.1.mine), channel_id=1, source_target_pairs={{0,4},{1,5},{2,6},{3,7},{4,0},{5,1},{6,2},{7,3},{8,12},{9,13},{10,... | collective-permute-start | bytes 294920 | tf_op jit(solution)/shard_map/ppermute | solution.py:574
  56.2 8.8 %collective-permute-start.6 = (bf16[128,384]{1,0:T(8,128)(2,1)S(1)}, bf16[128,384]{1,0:T(8,128)(2,1)S(1)}, u32[]{:S(2)}, u32[]{:S(2)}) collective-permute-start(bf16[128,384]{1,0:T(8,128)(2,1)S(1)} %mix.1.mine), channel_id=1, source_target_pairs={{0,6},{1,7},{2,0},{3,1},{4,2},{5,3},{6,4},{7,5},{8,14},{9,15},{10,... | collective-permute-start | bytes 294920 | tf_op jit(solution)/shard_map/ppermute | solution.py:574
  58.2 9.3 %copy-start.8 = (s32[8,1]{0,1:T(1,128)S(1)}, s32[8,1]{0,1:T(1,128)}, u32[]{:S(2)}) copy-start(s32[8,1]{0,1:T(1,128)} %param.18) | copy-start | bytes 100
  58.2 10.6 %copy-start.2 = (bf16[384,384]{1,0:T(8,128)(2,1)S(1)}, bf16[384,384]{1,0:T(8,128)(2,1)}, u32[]{:S(2)}) copy-start(bf16[384,384]{1,0:T(8,128)(2,1)} %refs_2_.1) | copy-start | bytes 884740
  58.2 10.6 %copy-start.3 = (bf16[384,384]{1,0:T(8,128)(2,1)S(1)}, bf16[384,384]{1,0:T(8,128)(2,1)}, u32[]{:S(2)}) copy-start(bf16[384,384]{1,0:T(8,128)(2,1)} %refs_3_.1) | copy-start | bytes 884740
  58.2 10.6 %copy-start.4 = (bf16[384,384]{1,0:T(8,128)(2,1)S(1)}, bf16[384,384]{1,0:T(8,128)(2,1)}, u32[]{:S(2)}) copy-start(bf16[384,384]{1,0:T(8,128)(2,1)} %refs_4_.1) | copy-start | bytes 884740
  58.2 10.6 %copy-start.5 = (bf16[384,384]{1,0:T(8,128)(2,1)S(1)}, bf16[384,384]{1,0:T(8,128)(2,1)}, u32[]{:S(2)}) copy-start(bf16[384,384]{1,0:T(8,128)(2,1)} %refs_5_.1) | copy-start | bytes 884740
  65.1 3.7 %collective-permute-start.7 = (bf16[512,384]{1,0:T(8,128)(2,1)S(1)}, bf16[512,384]{1,0:T(8,128)(2,1)S(1)}, u32[]{:S(2)}, u32[]{:S(2)}) collective-permute-start(bf16[512,384]{1,0:T(8,128)(2,1)S(1)} %pad_maximum_fusion.refs_0_), channel_id=1, source_target_pairs={{0,1},{1,0},{2,3},{3,2},{4,5},{5,4},{6,7},{7,6},{8,9},{9,8},{10,11... | collective-permute-start | bytes 1179656 | tf_op jit(solution)/shard_map/ppermute | solution.py:562

commit v4 on v3

--- a/solution.py
+++ b/solution.py
@@ -497,57 +497,77 @@
     )(place, lengths, near(latent), near(sums), near(tails))
 
 
-def attend_kernel(labels, mine, *refs):
+def attend_kernel(labels, *refs):
     pieces, (w_query, w_key, w_value, w_out, result, keys, values) = refs[:-7], refs[-7:]
+    mine = pieces[0]
     tokens, chans = mine.shape
     lat = labels.shape[0]
     per = tokens // lat
-    at = 0
-    for piece in pieces:
-        block = piece[...]
-        size = block.shape[0]
-        keys[at : at + size, :] = dot(block, w_key[...]).astype(BF16)
-        values[at : at + size, :] = dot(block, w_value[...]).astype(BF16)
-        at += size
-    query = (dot(mine[...], w_query[...]).astype(BF16) * BF16(1.0 / math.sqrt(HEAD))).astype(BF16)
-    row = lax.broadcasted_iota(jnp.int32, (tokens, 1), 0) // per
-    col = (lax.broadcasted_iota(jnp.int32, (1, tokens), 1) % tokens) // per
-    row_label = jnp.zeros((tokens, 1), jnp.int32)
-    col_label = jnp.zeros((1, tokens), jnp.int32)
+    heads = chans // HEAD
+    group = len(pieces) // 2
+    for first in range(0, len(pieces), group):
+        block = jnp.concatenate([piece[...] for piece in pieces[first : first + group]], axis=0)
+        for weight, target in ((w_key, keys), (w_value, values)):
+            made = dot(block, weight[...]).astype(BF16)
+            for k in range(group):
+                for j in range(lat):
+                    row = tokens * k + per * j
+                    at = per * (first + k)
+                    target[j, at : at + per, :] = made[row : row + per, :]
+    query = dot(mine[...], w_query[...]).astype(BF16).astype(F32) * (1.0 / math.sqrt(HEAD))
+    head_of = lax.broadcasted_iota(jnp.int32, (per, chans), 1) // HEAD
+    partners, scores = [], []
     for j in range(lat):
-        row_label = jnp.where(row == j, labels[j, 0], row_label)
-        col_label = jnp.where(col == j, labels[j, 0], col_label)
-    same = jnp.logical_and(row_label == col_label, col <= row)
-    bias = jnp.where(same, 0.0, -1e30).astype(F32)
-    bias = jnp.concatenate([bias] * (at // tokens), axis=1)
+        partner = jnp.int32(-1)
+        for k in range(j):
+            partner = jnp.where(labels[k, 0] == labels[j, 0], k, partner)
+        partners.append(jnp.maximum(partner, 0))
+        own = query[per * j : per * (j + 1), :]
+        stacked = jnp.concatenate(
+            [jnp.where(head_of == h, own, 0.0) for h in range(heads)], axis=0
+        ).astype(BF16)
+        bias = jnp.where(partner >= 0, 0.0, -1e30).astype(F32)
+        both = jnp.concatenate([keys[j], keys[partners[j]]], axis=0)
+        made = dot(stacked, both, NT)
+        half = made.shape[1] // 2
+        scores.append(jnp.concatenate([made[:, :half], made[:, half:] + bias], axis=1))
+    weights, norms = [], []
+    for j in range(lat):
+        expo = jnp.exp(scores[j] - jnp.max(scores[j], axis=1, keepdims=True))
+        norms.append(jnp.sum(expo, axis=1, keepdims=True))
+        weights.append(expo.astype(BF16))
+    mixes = []
+    for j in range(lat):
+        both = jnp.concatenate([values[j], values[partners[j]]], axis=0)
+        mixes.append(dot(weights[j], both))
     outs = []
-    for head in range(chans // HEAD):
-        lanes = slice(head * HEAD, (head + 1) * HEAD)
-        scores = dot(query[:, lanes], keys[:, lanes], NT) + bias
-        top = jnp.max(scores, axis=1, keepdims=True)
-        expo = jnp.exp(scores - top)
-        norm = jnp.sum(expo, axis=1, keepdims=True)
-        outs.append(dot(expo.astype(BF16), values[:, lanes]) / norm)
-    heads = jnp.concatenate(outs, axis=1).astype(BF16)
-    final = mine[...].astype(F32) + dot(heads, w_out[...])
+    for j in range(lat):
+        mixed = mixes[j] / norms[j]
+        total = jnp.zeros((per, chans), F32)
+        for h in range(heads):
+            total = jnp.where(head_of == h, mixed[per * h : per * (h + 1), :], total)
+        outs.append(total)
+    attended = jnp.concatenate(outs, axis=0).astype(BF16)
+    final = mine[...].astype(F32) + dot(attended, w_out[...])
     for j in range(lat):
         for h in range(2):
             at = per * j + 8 * h
             result[j, h] = final[at : at + 8].astype(BF16)
 
 
-def attend(labels, mine, pieces, w_query, w_key, w_value, w_out):
-    tokens, chans = mine.shape
-    total = sum(piece.shape[0] for piece in pieces)
+def attend(labels, pieces, w_query, w_key, w_value, w_out):
+    tokens, chans = pieces[0].shape
+    lat = labels.shape[0]
+    held = (lat, len(pieces) * tokens // lat, chans)
     return pl.pallas_call(
         attend_kernel,
-        out_shape=jax.ShapeDtypeStruct((labels.shape[0], 2, 8, chans), BF16),
-        in_specs=[SMEM] + [VMEM] * (5 + len(pieces)),
+        out_shape=jax.ShapeDtypeStruct((lat, 2, 8, chans), BF16),
+        in_specs=[SMEM] + [VMEM] * (4 + len(pieces)),
         out_specs=VMEM,
-        scratch_shapes=[pltpu.VMEM((total, chans), BF16), pltpu.VMEM((total, chans), BF16)],
+        scratch_shapes=[pltpu.VMEM(held, BF16), pltpu.VMEM(held, BF16)],
         compiler_params=pltpu.CompilerParams(vmem_limit_bytes=24 * 2**20),
         name="attend",
-    )(labels, mine, *pieces, w_query, w_key, w_value, w_out)
+    )(labels, *(near(piece) for piece in pieces), w_query, w_key, w_value, w_out)
 
 
 def shifted(value, axis, steps):
@@ -612,11 +632,11 @@
     tails = lax.all_to_all(tail, "tm", 0, 0, tiled=True)
     mixed = mix(place, shot_lengths, latent, sums, tails)
     chips = chip_shifts(mixed)
+    beside = with_core(mixed)
     frame_grad = backward(grad, low, high, near_grad, folded)
-    chips, frame_grad = lax.optimization_barrier((chips, frame_grad))
-    own = jnp.concatenate([mixed, *chips], axis=0)
-    pieces = [own, with_core(own)]
-    latent_out = attend(scene_label, mixed, pieces, w_query, w_key, w_value, w_out)
+    (chips, beside), frame_grad = lax.optimization_barrier(((chips, beside), frame_grad))
+    pieces = [mixed, *chips, beside, *(with_core(piece) for piece in chips)]
+    latent_out = attend(scene_label, pieces, w_query, w_key, w_value, w_out)
     return (latent_out, frame_grad)
 
 

time: 74.3 us -> 73 us (0.983)
  Pallas kernels: 29.6 us -> 27.9 us
    pallas_call x1, Pallas kernels: 5.09 us -> 3.4 us  [attend(): pl.pallas_call(attend_kernel, out_shape=jax.ShapeDtypeStruct((lat, 2, 8,...]
    ppermute x2 -> x5, starting transfers between devices: 3.78 us -> 4.38 us  [with_core(): return lax.ppermute(value, 'scene', [(i, i ^ 1) for i in range(count)])]
  transfers between devices with their start and end apart: 8 -> 11, of which waited for: 2 -> 4; matrix products, arithmetic and copies ran while one was open for 0% -> 0% of each run, Pallas kernels for 16% -> 17%
where the time goes in v4:
time: 73 us; the launch traced here: 72.7 us
  Pallas kernels  27.9 us (38%)
  starting transfers between devices  19.8 us (27%)
  blocking collectives  17.7 us (24%)
  waiting for transfers between devices  4.77 us (7%)
  local copies, waits for them, and re-layouts  1.63 us (2%)
  between operations  0.83 us (1%)
    all_to_all x1, blocking collectives, per_device(): tails = lax.all_to_all(tail, 'tm', 0, 0, tiled=True)  17.7 us
    pallas_call x1, Pallas kernels, forward(): pl.pallas_call(forward_kernel, out_shape=(pltpu.VMEM((lat, 16, chans), F3...  10.6 us
    pallas_call x1, Pallas kernels, backward(): pl.pallas_call(backward_kernel, out_shape=jax.ShapeDtypeStruct(out_grad.s...  6.78 us
    ppermute x3, starting transfers between devices, chip_shifts(): lax.ppermute(value, 'scene', [(i, (i + 2 * k) % count) for i in range(cou...  6.21 us
    ppermute x2, starting transfers between devices, shifted(): lax.ppermute(value, axis, [(i, i + steps) for i in range(count) if 0 <= i...  5.95 us
    ppermute x5, starting transfers between devices, with_core(): return lax.ppermute(value, 'scene', [(i, i ^ 1) for i in range(count)])  4.38 us
    pallas_call x1, Pallas kernels, fetch(): pl.pallas_call(fetch_kernel, out_shape=[pltpu.VMEM(value.shape, BF16) for...  3.78 us
    ppermute x1, waiting for transfers between devices, with_chip(): return lax.ppermute(value, 'scene', pairs + [(b, a) for a, b in pairs])  3.62 us
  transfers between devices with their start and end apart: 11, of which 4 were waited for; matrix products, arithmetic and copies ran while one was open for 0% of the time, Pallas kernels for 17%

profile of v4, /device:TPU:1, one launch (start us, length us, event | category | flops | bytes accessed | tf_op | source)
XLA Modules:
  0.0 72.7 jit_solution(2805607026224262153)
XLA Ops:
  0.6 0.8 %fusion = (bf16[2,2,8,384]{3,2,1,0:T(8,128)(2,1)S(1)}, bf16[2,2,8,384]{3,2,1,0:T(8,128)(2,1)S(1)}) fusion(bf16[64,2,8,384]{3,2,1,0:T(8,128)(2,1)} %frames.1), kind=kLoop, calls=%fused_computation.2 | loop fusion | bytes 98304 | tf_op jit(solution)/shard_map/slice | solution.py:614
  1.4 0.7 %slice.11 = bf16[2,2,8,384]{3,2,1,0:T(8,128)(2,1)S(1)} slice(bf16[64,2,8,384]{3,2,1,0:T(8,128)(2,1)} %out_grad.1), slice={[0:2], [0:2], [0:8], [0:384]} | slice | bytes 49152 | tf_op jit(solution)/shard_map/slice | solution.py:614
  2.1 1.3 %collective-permute-start.1 = (bf16[4,2,8,384]{3,2,1,0:T(8,128)(2,1)S(1)}, bf16[4,2,8,384]{3,2,1,0:T(8,128)(2,1)S(1)}, u32[]{:S(2)}, u32[]{:S(2)}) collective-permute-start(bf16[4,2,8,384]{3,2,1,0:T(8,128)(2,1)S(1)} %pad_maximum_fusion), channel_id=1, source_target_pairs={{8,0},{16,8},{24,16},{32,24},{40,32},{48,40},{56,48},{64,56},{72,6... | collective-permute-start | bytes 147464 | tf_op jit(solution)/shard_map/ppermute | solution.py:575
  3.4 4.7 %collective-permute-start = (bf16[2,2,8,384]{3,2,1,0:T(8,128)(2,1)S(1)}, bf16[2,2,8,384]{3,2,1,0:T(8,128)(2,1)S(1)}, u32[]{:S(2)}, u32[]{:S(2)}) collective-permute-start(bf16[2,2,8,384]{3,2,1,0:T(8,128)(2,1)S(1)} %get-tuple-element.47), channel_id=1, source_target_pairs={{0,8},{8,16},{16,24},{24,32},{32,40},{40,48},{48,56},{56,64},{64,7... | collective-permute-start | bytes 73736 | tf_op jit(solution)/shard_map/ppermute | solution.py:575
  8.1 0.1 pad_add_fusion.place
  8.2 3.8 %fetch.1 = (bf16[64,2,8,384]{3,2,1,0:T(8,128)(2,1)S(1)}, bf16[64,2,8,384]{3,2,1,0:T(8,128)(2,1)S(1)}, bf16[3,3,3,384,384]{4,3,2,1,0:T(8,128)(2,1)S(1)}) custom-call(bf16[64,2,8,384]{3,2,1,0:T(8,128)(2,1)} %frames.1, bf16[64,2,8,384]{3,2,1,0:T(8,128)(2,1)} %out_grad.1, bf16[3,3,3,384,384]{4,3,2,1,0:T(8,128)(2,1)} %weight.1), custom_call_target="tpu_custom_call" | custom-call | bytes 20971520 | tf_op jit(solution)/shard_map/fetch/pallas_call | solution.py:41
  12.0 0.0 copy-start
  12.0 1.1 %pack.1 = (bf16[208,768]{1,0:T(8,128)(2,1)S(1)}, bf16[208,768]{1,0:T(8,128)(2,1)S(1)}) custom-call(s32[2]{0:T(128)S(1)} %pad_add_fusion.place, bf16[64,2,8,384]{3,2,1,0:T(8,128)(2,1)S(1)} %get-tuple-element.24.frames, bf16[64,2,8,384]{3,2,1,0:T(8,128)(2,1)S(1)} %get-tuple-element.28.out_grad, bf16[2,2,8,384]{3,2,1,0:T(8,128)(2,1)S(1)} %collective-permute-done.before, ...), custom_call_target="tpu_custom_call" | custom-call | tf_op jit(solution)/shard_map/pack/pallas_call | solution.py:186
  13.2 1.4 %collective-permute-start.2 = (bf16[208,768]{1,0:T(8,128)(2,1)S(1)}, bf16[208,768]{1,0:T(8,128)(2,1)S(1)}, u32[]{:S(2)}, u32[]{:S(2)}) collective-permute-start(bf16[208,768]{1,0:T(8,128)(2,1)S(1)} %get-tuple-element.29.core_sent), channel_id=1, source_target_pairs={{0,1},{1,0},{2,3},{3,2},{4,5},{5,4},{6,7},{7,6},{8,9},{9,8},{10,11... | collective-permute-start | bytes 958472 | tf_op jit(solution)/shard_map/ppermute | solution.py:582
  14.6 3.3 %collective-permute-start.3 = (bf16[208,768]{1,0:T(8,128)(2,1)S(1)}, bf16[208,768]{1,0:T(8,128)(2,1)S(1)}, u32[]{:S(2)}, u32[]{:S(2)}) collective-permute-start(bf16[208,768]{1,0:T(8,128)(2,1)S(1)} %get-tuple-element.30.chip_sent), channel_id=1, source_target_pairs={{1,2},{3,4},{5,6},{2,1},{4,3},{6,5},{9,10},{11,12},{13,14},{10,9},... | collective-permute-start | bytes 958472 | tf_op jit(solution)/shard_map/ppermute | solution.py:588
  17.8 0.0 copy-start.1
  17.9 1.5 %fold.1.folded = bf16[9,768,768]{2,1,0:T(8,128)(2,1)S(1)} custom-call(bf16[3,3,3,384,384]{4,3,2,1,0:T(8,128)(2,1)S(1)} %get-tuple-element.31.weight), custom_call_target="tpu_custom_call" | custom-call | bytes 20971520 | tf_op jit(solution)/shard_map/fold/pallas_call | solution.py:76
  19.4 3.6 %collective-permute-done.3.chip_got = bf16[208,768]{1,0:T(8,128)(2,1)S(1)} collective-permute-done((bf16[208,768]{1,0:T(8,128)(2,1)S(1)}, bf16[208,768]{1,0:T(8,128)(2,1)S(1)}, u32[]{:S(2)}, u32[]{:S(2)}) %collective-permute-start.3) | collective-permute-done | bytes 319520 | tf_op jit(solution)/shard_map/ppermute | solution.py:588
  23.0 10.6 %forward.1 = (f32[8,16,384]{2,1,0:T(8,128)S(1)}, f32[8,16,384]{2,1,0:T(8,128)S(1)}, f32[16,16,384]{2,1,0:T(8,128)S(1)}, f32[72,768]{1,0:T(8,128)S(1)}, f32[72,76...) custom-call(s32[2]{0:T(128)S(1)} %pad_add_fusion.place, s32[8]{0:T(128)S(1)} %copy-done.6, ...), custom_call_target="tpu_custom_call" | custom-call | flops 5605687296 | bytes 16777216 | tf_op jit(solution)/shard_map/forward/pallas_call | solution.py:347
  33.6 17.7 %all_to_all.5.tails = f32[16,16,384]{2,1,0:T(8,128)S(1)} all-to-all(f32[16,16,384]{2,1,0:T(8,128)S(1)} %get-tuple-element.37), channel_id=1, replica_groups=mesh['tm'=16,'scene'=8] {'tm'}, dimensions={0} | all-to-all | bytes 786432 | tf_op jit(solution)/shard_map/all_to_all | solution.py:632
  51.3 0.7 mix.1.refs_0_
  52.0 2.6 %collective-permute-start.4 = (bf16[128,384]{1,0:T(8,128)(2,1)S(1)}, bf16[128,384]{1,0:T(8,128)(2,1)S(1)}, u32[]{:S(2)}, u32[]{:S(2)}) collective-permute-start(bf16[128,384]{1,0:T(8,128)(2,1)S(1)} %mix.1.refs_0_), channel_id=1, source_target_pairs={{0,2},{1,3},{2,4},{3,5},{4,6},{5,7},{6,0},{7,1},{8,10},{9,11},{10,... | collective-permute-start | bytes 294920 | tf_op jit(solution)/shard_map/ppermute | solution.py:594
  54.6 1.6 %collective-permute-start.5 = (bf16[128,384]{1,0:T(8,128)(2,1)S(1)}, bf16[128,384]{1,0:T(8,128)(2,1)S(1)}, u32[]{:S(2)}, u32[]{:S(2)}) collective-permute-start(bf16[128,384]{1,0:T(8,128)(2,1)S(1)} %mix.1.refs_0_), channel_id=1, source_target_pairs={{0,4},{1,5},{2,6},{3,7},{4,0},{5,1},{6,2},{7,3},{8,12},{9,13},{10,... | collective-permute-start | bytes 294920 | tf_op jit(solution)/shard_map/ppermute | solution.py:594
  56.2 2.0 %collective-permute-start.6 = (bf16[128,384]{1,0:T(8,128)(2,1)S(1)}, bf16[128,384]{1,0:T(8,128)(2,1)S(1)}, u32[]{:S(2)}, u32[]{:S(2)}) collective-permute-start(bf16[128,384]{1,0:T(8,128)(2,1)S(1)} %mix.1.refs_0_), channel_id=1, source_target_pairs={{0,6},{1,7},{2,0},{3,1},{4,2},{5,3},{6,4},{7,5},{8,14},{9,15},{10,... | collective-permute-start | bytes 294920 | tf_op jit(solution)/shard_map/ppermute | solution.py:594
  58.2 2.3 %collective-permute-start.7 = (bf16[128,384]{1,0:T(8,128)(2,1)S(1)}, bf16[128,384]{1,0:T(8,128)(2,1)S(1)}, u32[]{:S(2)}, u32[]{:S(2)}) collective-permute-start(bf16[128,384]{1,0:T(8,128)(2,1)S(1)} %mix.1.refs_0_), channel_id=1, source_target_pairs={{0,1},{1,0},{2,3},{3,2},{4,5},{5,4},{6,7},{7,6},{8,9},{9,8},{10,11... | collective-permute-start | bytes 294920 | tf_op jit(solution)/shard_map/ppermute | solution.py:582
  60.5 0.0 copy-start.5
  60.5 6.8 %backward.1 = bf16[64,2,8,384]{3,2,1,0:T(8,128)(2,1)} custom-call(bf16[66,8,768]{2,1,0:T(8,128)(2,1)S(1)} %get-tuple-element.38.grad, f32[72,768]{1,0:T(8,128)S(1)} %get-tuple-element.39.low, f32[72,768]{1,0:T(8,128)S(1)} %get-tuple-element.40.high, bf16[64,2,8,384]{3,2,1,0:T(8,128)(2,1)S(1)} %get-tuple-element.28.out_grad, bf16[9,768,768]{2,1,0:T(8,128)(2,1)S(1)} %fold.1.folded), custom_call_target="tpu_custom_call" | custom-call | flops 5435817984 | bytes 12582912 | tf_op jit(solution)/shard_map/backward/pallas_call | solution.py:445
  67.3 0.0 collective-permute-done.4.refs_1_
  67.3 0.0 collective-permute-done.5.refs_2_
  67.4 0.1 collective-permute-start.10
  67.5 0.5 collective-permute-start.8
  68.0 0.1 collective-permute-start.9
  68.1 0.1 copy.12.labels
  68.1 0.6 collective-permute-done.10.refs_7_
  68.8 0.2 collective-permute-done.8.refs_5_
  68.9 0.4 collective-permute-done.9.refs_6_
  69.3 3.4 %attend.1 = bf16[8,2,8,384]{3,2,1,0:T(8,128)(2,1)} custom-call(s32[8,1]{1,0:T(8,128)S(1)} %copy.12.labels, bf16[128,384]{1,0:T(8,128)(2,1)S(1)} %mix.1.refs_0_, bf16[128,384]{1,0:T(8,128)(2,1)S(1)} %collective-permute-done.4.refs_1_, bf16[128,384]{1,0:T(8,128)(2,1)S(1)} %collective-permute-done.5.refs_2_, ...), custom_call_target="tpu_custom_call" | custom-call | tf_op jit(solution)/shard_map/attend/pallas_call | solution.py:562
  (21 shorter events, 0.1 us)
Async XLA Ops:
  2.1 9.9 %collective-permute-start.1 = (bf16[4,2,8,384]{3,2,1,0:T(8,128)(2,1)S(1)}, bf16[4,2,8,384]{3,2,1,0:T(8,128)(2,1)S(1)}, u32[]{:S(2)}, u32[]{:S(2)}) collective-permute-start(bf16[4,2,8,384]{3,2,1,0:T(8,128)(2,1)S(1)} %pad_maximum_fusion), channel_id=1, source_target_pairs={{8,0},{16,8},{24,16},{32,24},{40,32},{48,40},{56,48},{64,56},{72,6... | collective-permute-start | bytes 147464 | tf_op jit(solution)/shard_map/ppermute | solution.py:575
  3.4 8.6 %collective-permute-start = (bf16[2,2,8,384]{3,2,1,0:T(8,128)(2,1)S(1)}, bf16[2,2,8,384]{3,2,1,0:T(8,128)(2,1)S(1)}, u32[]{:S(2)}, u32[]{:S(2)}) collective-permute-start(bf16[2,2,8,384]{3,2,1,0:T(8,128)(2,1)S(1)} %get-tuple-element.47), channel_id=1, source_target_pairs={{0,8},{8,16},{16,24},{24,32},{32,40},{40,48},{48,56},{56,64},{64,7... | collective-permute-start | bytes 73736 | tf_op jit(solution)/shard_map/ppermute | solution.py:575
  12.0 2.6 %copy-start = (bf16[64,2,8,384]{3,2,1,0:T(8,128)(2,1)}, bf16[64,2,8,384]{3,2,1,0:T(8,128)(2,1)S(1)}, u32[]{:S(2)}) copy-start(bf16[64,2,8,384]{3,2,1,0:T(8,128)(2,1)S(1)} %get-tuple-element.24.frames) | copy-start | bytes 2359300
  13.2 6.2 %collective-permute-start.2 = (bf16[208,768]{1,0:T(8,128)(2,1)S(1)}, bf16[208,768]{1,0:T(8,128)(2,1)S(1)}, u32[]{:S(2)}, u32[]{:S(2)}) collective-permute-start(bf16[208,768]{1,0:T(8,128)(2,1)S(1)} %get-tuple-element.29.core_sent), channel_id=1, source_target_pairs={{0,1},{1,0},{2,3},{3,2},{4,5},{5,4},{6,7},{7,6},{8,9},{9,8},{10,11... | collective-permute-start | bytes 958472 | tf_op jit(solution)/shard_map/ppermute | solution.py:582
  14.6 8.4 %copy-start.6 = (s32[8]{0:T(128)S(1)}, s32[8]{0:T(128)}, u32[]{:S(2)}) copy-start(s32[8]{0:T(128)} %lengths.3) | copy-start | bytes 100
  14.6 8.4 %copy-start.7 = (bf16[8,384,384]{2,1,0:T(8,128)(2,1)S(1)}, bf16[8,384,384]{2,1,0:T(8,128)(2,1)}, u32[]{:S(2)}) copy-start(bf16[8,384,384]{2,1,0:T(8,128)(2,1)} %down.1) | copy-start | bytes 7077892
  14.6 8.4 %collective-permute-start.3 = (bf16[208,768]{1,0:T(8,128)(2,1)S(1)}, bf16[208,768]{1,0:T(8,128)(2,1)S(1)}, u32[]{:S(2)}, u32[]{:S(2)}) collective-permute-start(bf16[208,768]{1,0:T(8,128)(2,1)S(1)} %get-tuple-element.30.chip_sent), channel_id=1, source_target_pairs={{1,2},{3,4},{5,6},{2,1},{4,3},{6,5},{9,10},{11,12},{13,14},{10,9},... | collective-permute-start | bytes 958472 | tf_op jit(solution)/shard_map/ppermute | solution.py:588
  17.8 5.2 %copy-start.1 = (bf16[64,2,8,384]{3,2,1,0:T(8,128)(2,1)S(1)}, bf16[64,2,8,384]{3,2,1,0:T(8,128)(2,1)}, u32[]{:S(2)}) copy-start(bf16[64,2,8,384]{3,2,1,0:T(8,128)(2,1)} %copy-done) | copy-start | bytes 2359300
  52.0 15.3 %collective-permute-start.4 = (bf16[128,384]{1,0:T(8,128)(2,1)S(1)}, bf16[128,384]{1,0:T(8,128)(2,1)S(1)}, u32[]{:S(2)}, u32[]{:S(2)}) collective-permute-start(bf16[128,384]{1,0:T(8,128)(2,1)S(1)} %mix.1.refs_0_), channel_id=1, source_target_pairs={{0,2},{1,3},{2,4},{3,5},{4,6},{5,7},{6,0},{7,1},{8,10},{9,11},{10,... | collective-permute-start | bytes 294920 | tf_op jit(solution)/shard_map/ppermute | solution.py:594
  54.6 12.7 %collective-permute-start.5 = (bf16[128,384]{1,0:T(8,128)(2,1)S(1)}, bf16[128,384]{1,0:T(8,128)(2,1)S(1)}, u32[]{:S(2)}, u32[]{:S(2)}) collective-permute-start(bf16[128,384]{1,0:T(8,128)(2,1)S(1)} %mix.1.refs_0_), channel_id=1, source_target_pairs={{0,4},{1,5},{2,6},{3,7},{4,0},{5,1},{6,2},{7,3},{8,12},{9,13},{10,... | collective-permute-start | bytes 294920 | tf_op jit(solution)/shard_map/ppermute | solution.py:594
  56.2 11.1 %collective-permute-start.6 = (bf16[128,384]{1,0:T(8,128)(2,1)S(1)}, bf16[128,384]{1,0:T(8,128)(2,1)S(1)}, u32[]{:S(2)}, u32[]{:S(2)}) collective-permute-start(bf16[128,384]{1,0:T(8,128)(2,1)S(1)} %mix.1.refs_0_), channel_id=1, source_target_pairs={{0,6},{1,7},{2,0},{3,1},{4,2},{5,3},{6,4},{7,5},{8,14},{9,15},{10,... | collective-permute-start | bytes 294920 | tf_op jit(solution)/shard_map/ppermute | solution.py:594
  58.2 9.2 %collective-permute-start.7 = (bf16[128,384]{1,0:T(8,128)(2,1)S(1)}, bf16[128,384]{1,0:T(8,128)(2,1)S(1)}, u32[]{:S(2)}, u32[]{:S(2)}) collective-permute-start(bf16[128,384]{1,0:T(8,128)(2,1)S(1)} %mix.1.refs_0_), channel_id=1, source_target_pairs={{0,1},{1,0},{2,3},{3,2},{4,5},{5,4},{6,7},{7,6},{8,9},{9,8},{10,11... | collective-permute-start | bytes 294920 | tf_op jit(solution)/shard_map/ppermute | solution.py:582
  60.5 7.5 %copy-start.8 = (s32[8,1]{0,1:T(1,128)S(1)}, s32[8,1]{0,1:T(1,128)}, u32[]{:S(2)}) copy-start(s32[8,1]{0,1:T(1,128)} %param.18) | copy-start | bytes 100
  60.5 8.7 %copy-start.2 = (bf16[384,384]{1,0:T(8,128)(2,1)S(1)}, bf16[384,384]{1,0:T(8,128)(2,1)}, u32[]{:S(2)}) copy-start(bf16[384,384]{1,0:T(8,128)(2,1)} %refs_8_.1) | copy-start | bytes 884740
  60.5 8.7 %copy-start.3 = (bf16[384,384]{1,0:T(8,128)(2,1)S(1)}, bf16[384,384]{1,0:T(8,128)(2,1)}, u32[]{:S(2)}) copy-start(bf16[384,384]{1,0:T(8,128)(2,1)} %refs_9_.1) | copy-start | bytes 884740
  60.5 8.8 %copy-start.4 = (bf16[384,384]{1,0:T(8,128)(2,1)S(1)}, bf16[384,384]{1,0:T(8,128)(2,1)}, u32[]{:S(2)}) copy-start(bf16[384,384]{1,0:T(8,128)(2,1)} %refs_10_.1) | copy-start | bytes 884740
  60.5 8.8 %copy-start.5 = (bf16[384,384]{1,0:T(8,128)(2,1)S(1)}, bf16[384,384]{1,0:T(8,128)(2,1)}, u32[]{:S(2)}) copy-start(bf16[384,384]{1,0:T(8,128)(2,1)} %refs_11_.1) | copy-start | bytes 884740
  67.4 1.4 %collective-permute-start.10 = (bf16[128,384]{1,0:T(8,128)(2,1)S(1)}, bf16[128,384]{1,0:T(8,128)(2,1)S(1)}, u32[]{:S(2)}, u32[]{:S(2)}) collective-permute-start(bf16[128,384]{1,0:T(8,128)(2,1)S(1)} %collective-permute-done.6.refs_3_), channel_id=1, source_target_pairs={{0,1},{1,0},{2,3},{3,2},{4,5},{5,4},{6,7},{7,6},{8,9},{9,8},{10,11... | collective-permute-start | bytes 294920 | tf_op jit(solution)/shard_map/ppermute | solution.py:582
  67.5 1.4 %collective-permute-start.8 = (bf16[128,384]{1,0:T(8,128)(2,1)S(1)}, bf16[128,384]{1,0:T(8,128)(2,1)S(1)}, u32[]{:S(2)}, u32[]{:S(2)}) collective-permute-start(bf16[128,384]{1,0:T(8,128)(2,1)S(1)} %collective-permute-done.4.refs_1_), channel_id=1, source_target_pairs={{0,1},{1,0},{2,3},{3,2},{4,5},{5,4},{6,7},{7,6},{8,9},{9,8},{10,11... | collective-permute-start | bytes 294920 | tf_op jit(solution)/shard_map/ppermute | solution.py:582
  68.0 1.3 %collective-permute-start.9 = (bf16[128,384]{1,0:T(8,128)(2,1)S(1)}, bf16[128,384]{1,0:T(8,128)(2,1)S(1)}, u32[]{:S(2)}, u32[]{:S(2)}) collective-permute-start(bf16[128,384]{1,0:T(8,128)(2,1)S(1)} %collective-permute-done.5.refs_2_), channel_id=1, source_target_pairs={{0,1},{1,0},{2,3},{3,2},{4,5},{5,4},{6,7},{7,6},{8,9},{9,8},{10,11... | collective-permute-start | bytes 294920 | tf_op jit(solution)/shard_map/ppermute | solution.py:582

commit v5 on v4

--- a/solution.py
+++ b/solution.py
@@ -44,7 +44,7 @@
         in_specs=[ANY] * 3,
         out_specs=[VMEM] * 3,
         scratch_shapes=[pltpu.SemaphoreType.DMA((3,))],
-        compiler_params=pltpu.CompilerParams(vmem_limit_bytes=52 * 2**20),
+        compiler_params=pltpu.CompilerParams(vmem_limit_bytes=48 * 2**20),
         cost_estimate=pl.CostEstimate(
             flops=0, bytes_accessed=20 * 2**20, transcendentals=0
         ),
@@ -192,9 +192,54 @@
             pltpu.VMEM((2 * chans // 128, cols * (count + 4), 128), F32),
             pltpu.VMEM((2 * chans // 128, cols * (count + 2), 128), F32),
         ],
-        compiler_params=pltpu.CompilerParams(vmem_limit_bytes=24 * 2**20),
+        compiler_params=pltpu.CompilerParams(vmem_limit_bytes=12 * 2**20),
         name="pack",
     )(place, near(frames), near(out_grad), near(before), near(after))
+
+
+def joined_frames(frames, before, after):
+    count = frames.shape[0]
+
+    def frame_of(t):
+        if t < 2:
+            part = lambda h: before[t, h]
+        elif t < count + 2:
+            part = lambda h: frames[t - 2, h]
+        else:
+            part = lambda h: after[t - count - 2, h]
+        return jnp.concatenate([part(0).astype(F32), part(1).astype(F32)], axis=1)
+
+    return frame_of
+
+
+def centre_kernel(frames, before, after, folded, total, even, odd):
+    build_centre(joined_frames(frames, before, after), frames.shape[0] + 4, even, odd)
+    rows = total.shape[0]
+
+    def weight_of(off, side):
+        return folded[3 * off + side]
+
+    sum_taps(total, 0, rows, (1,), even, odd, weight_of, NN)
+
+
+def centre(frames, before, after, folded):
+    count, _, cols, chans = frames.shape
+    rows, wide = cols * (count + 2), 2 * chans
+    return pl.pallas_call(
+        centre_kernel,
+        out_shape=pltpu.VMEM((rows, wide), F32),
+        in_specs=[VMEM] * 4,
+        out_specs=VMEM,
+        scratch_shapes=[
+            pltpu.VMEM((3, rows + 16, wide), BF16),
+            pltpu.VMEM((3, rows, wide), BF16),
+        ],
+        compiler_params=pltpu.CompilerParams(vmem_limit_bytes=10 * 2**20),
+        cost_estimate=pl.CostEstimate(
+            flops=2 * 3 * rows * wide * wide, bytes_accessed=6 * 2**20, transcendentals=0
+        ),
+        name="centre",
+    )(*(near(value) for value in (frames, before, after, folded)))
 
 
 def forward_kernel(
@@ -208,6 +253,7 @@
     core_got,
     chip_got,
     out_grad,
+    middle,
     down,
     folded,
     latent_out,
@@ -243,15 +289,7 @@
     pick(core_sent, chip_sent, own_low, own_high)
     pick(core_got, chip_got, low, high)
 
-    def frame_of(t):
-        if t < 2:
-            part = lambda h: before[t, h]
-        elif t < count + 2:
-            part = lambda h: frames[t - 2, h]
-        else:
-            part = lambda h: after[t - count - 2, h]
-        return jnp.concatenate([part(0).astype(F32), part(1).astype(F32)], axis=1)
-
+    frame_of = joined_frames(frames, before, after)
     span = count + 4
 
     def rim(side, off):
@@ -261,7 +299,6 @@
             [ref[at + off : at + off + ahead + 6, :] for ref, at in (left, right)], axis=0
         ).astype(BF16)
 
-    build_centre(frame_of, span, even, odd)
     def weight_of(off, side):
         return folded[3 * off + side]
 
@@ -283,7 +320,7 @@
                 grad_out[8 * j : 8 * (j + 1), :, lanes] = grad.astype(BF16)
 
     half = 64 * (count // 16)
-    sum_taps(total, 0, half, (1,), even, odd, weight_of, NN)
+    total[0:rows, :] = middle[...]
     build_sides(
         frame_of,
         lambda t: low[span + t : span + t + 1, :],
@@ -292,8 +329,12 @@
         even,
         odd,
     )
+    edges = dot(rim(1, 0), folded[1])
+    edges += dot(rim(1, 1), folded[4])
+    edges += dot(rim(1, 2), folded[7])
+    total[rows:, :] = edges
     sum_taps(total, 0, half, (0, 2), even, odd, weight_of, NN)
-    sum_taps(total, half, rows - half, (1, 0, 2), even, odd, weight_of, NN, rim)
+    sum_taps(total, half, rows - half, (0, 2), even, odd, weight_of, NN, rim)
     finish(0, count // 16)
     finish(count // 16, count // 8)
     for t in range(2):
@@ -337,7 +378,9 @@
         tail_out[k] = running
 
 
-def forward(peers, place, lengths, frames, before, after, columns, out_grad, down, folded):
+def forward(
+    peers, place, lengths, frames, before, after, columns, out_grad, middle, down, folded
+):
     count, _, cols, chans = frames.shape
     wide = 2 * chans
     lat = count // 8
@@ -354,7 +397,7 @@
             pltpu.VMEM((ahead + 6, wide), F32),
             pltpu.VMEM((ahead, cols, wide), BF16),
         ),
-        in_specs=[SMEM, SMEM] + [VMEM] * 8 + [ANY, VMEM],
+        in_specs=[SMEM, SMEM] + [VMEM] * 9 + [ANY, VMEM],
         out_specs=[VMEM] * 6,
         scratch_shapes=[
             pltpu.VMEM(down.shape, BF16),
@@ -368,7 +411,7 @@
             pltpu.VMEM((lat, 8, cols, wide), F32),
             pltpu.SemaphoreType.DMA((1,)),
         ],
-        compiler_params=pltpu.CompilerParams(vmem_limit_bytes=28 * 2**20),
+        compiler_params=pltpu.CompilerParams(vmem_limit_bytes=22 * 2**20),
         cost_estimate=pl.CostEstimate(
             flops=2 * 9 * rows * wide * wide, bytes_accessed=16 * 2**20, transcendentals=rows * wide
         ),
@@ -376,7 +419,7 @@
     )(
         place,
         lengths,
-        *(near(value) for value in (frames, before, after, *columns, out_grad)),
+        *(near(value) for value in (frames, before, after, *columns, out_grad, middle)),
         down,
         near(folded),
     )
@@ -616,7 +659,9 @@
     (before, after), near_weight = lax.optimization_barrier(((before, after), near_weight))
     sent = pack(place, near_frames, near_grad, before, after)
     received = (with_core(sent[0]), with_chip(sent[1]))
-    received, folded = lax.optimization_barrier((received, fold(near_weight)))
+    folded = fold(near_weight)
+    middle = centre(near_frames, before, after, folded)
+    received, middle = lax.optimization_barrier((received, middle))
     latent, sums, tail, low, high, grad = forward(
         lax.axis_size("tm"),
         place,
@@ -626,16 +671,17 @@
         after,
         (*sent, *received),
         near_grad,
+        middle,
         down_weight,
         folded,
     )
     tails = lax.all_to_all(tail, "tm", 0, 0, tiled=True)
     mixed = mix(place, shot_lengths, latent, sums, tails)
     chips = chip_shifts(mixed)
-    beside = with_core(mixed)
     frame_grad = backward(grad, low, high, near_grad, folded)
-    (chips, beside), frame_grad = lax.optimization_barrier(((chips, beside), frame_grad))
-    pieces = [mixed, *chips, beside, *(with_core(piece) for piece in chips)]
+    chips, frame_grad = lax.optimization_barrier((chips, frame_grad))
+    pieces = [mixed, *chips]
+    pieces += [with_core(piece) for piece in pieces]
     latent_out = attend(scene_label, pieces, w_query, w_key, w_value, w_out)
     return (latent_out, frame_grad)
 

time: 73 us -> 70.9 us (0.971)
  waiting for transfers between devices: 4.77 us -> 2.67 us
    pallas_call x0 -> x1, Pallas kernels: none -> 2.1 us  [centre(): pl.pallas_call(centre_kernel, out_shape=pltpu.VMEM((rows, wide), F32), in...]
    ppermute x1, waiting for transfers between devices: 3.62 us -> 1.53 us  [with_chip(): return lax.ppermute(value, 'scene', pairs + [(b, a) for a, b in pairs])]
    pallas_call x1, Pallas kernels: 10.6 us -> 8.59 us  [forward(): pl.pallas_call(forward_kernel, out_shape=(pltpu.VMEM((lat, 16, chans), F3...]
  transfers between devices with their start and end apart: 11 -> 11, of which waited for: 4 -> 5; matrix products, arithmetic and copies ran while one was open for 0% -> 0% of each run, Pallas kernels for 17% -> 20%
where the time goes in v5:
time: 70.9 us; the launch traced here: 70.6 us
  Pallas kernels  28 us (39%)
  starting transfers between devices  19.7 us (28%)
  blocking collectives  17.7 us (25%)
  waiting for transfers between devices  2.67 us (4%)
  local copies, waits for them, and re-layouts  1.62 us (2%)
  between operations  0.8 us (1%)
    all_to_all x1, blocking collectives, per_device(): tails = lax.all_to_all(tail, 'tm', 0, 0, tiled=True)  17.7 us
    pallas_call x1, Pallas kernels, forward(): pl.pallas_call(forward_kernel, out_shape=(pltpu.VMEM((lat, 16, chans), F3...  8.59 us
    pallas_call x1, Pallas kernels, backward(): pl.pallas_call(backward_kernel, out_shape=jax.ShapeDtypeStruct(out_grad.s...  6.78 us
    ppermute x3, starting transfers between devices, chip_shifts(): lax.ppermute(value, 'scene', [(i, (i + 2 * k) % count) for i in range(cou...  6.26 us
    ppermute x2, starting transfers between devices, shifted(): lax.ppermute(value, axis, [(i, i + steps) for i in range(count) if 0 <= i...  5.95 us
    ppermute x5, starting transfers between devices, with_core(): return lax.ppermute(value, 'scene', [(i, i ^ 1) for i in range(count)])  4.41 us
    pallas_call x1, Pallas kernels, fetch(): pl.pallas_call(fetch_kernel, out_shape=[pltpu.VMEM(value.shape, BF16) for...  3.78 us
    pallas_call x1, Pallas kernels, attend(): pl.pallas_call(attend_kernel, out_shape=jax.ShapeDtypeStruct((lat, 2, 8,...  3.4 us
  transfers between devices with their start and end apart: 11, of which 5 were waited for; matrix products, arithmetic and copies ran while one was open for 0% of the time, Pallas kernels for 20%

profile of v5, /device:TPU:1, one launch (start us, length us, event | category | flops | bytes accessed | tf_op | source)
XLA Modules:
  0.0 70.6 jit_solution(17737669285592110845)
XLA Ops:
  0.6 0.8 %fusion = (bf16[2,2,8,384]{3,2,1,0:T(8,128)(2,1)S(1)}, bf16[2,2,8,384]{3,2,1,0:T(8,128)(2,1)S(1)}) fusion(bf16[64,2,8,384]{3,2,1,0:T(8,128)(2,1)} %frames.1), kind=kLoop, calls=%fused_computation.2 | loop fusion | bytes 98304 | tf_op jit(solution)/shard_map/slice | solution.py:657
  1.4 0.7 %slice.11 = bf16[2,2,8,384]{3,2,1,0:T(8,128)(2,1)S(1)} slice(bf16[64,2,8,384]{3,2,1,0:T(8,128)(2,1)} %out_grad.1), slice={[0:2], [0:2], [0:8], [0:384]} | slice | bytes 49152 | tf_op jit(solution)/shard_map/slice | solution.py:657
  2.1 1.3 %collective-permute-start.1 = (bf16[4,2,8,384]{3,2,1,0:T(8,128)(2,1)S(1)}, bf16[4,2,8,384]{3,2,1,0:T(8,128)(2,1)S(1)}, u32[]{:S(2)}, u32[]{:S(2)}) collective-permute-start(bf16[4,2,8,384]{3,2,1,0:T(8,128)(2,1)S(1)} %pad_maximum_fusion), channel_id=1, source_target_pairs={{8,0},{16,8},{24,16},{32,24},{40,32},{48,40},{56,48},{64,56},{72,6... | collective-permute-start | bytes 147464 | tf_op jit(solution)/shard_map/ppermute | solution.py:618
  3.4 4.7 %collective-permute-start = (bf16[2,2,8,384]{3,2,1,0:T(8,128)(2,1)S(1)}, bf16[2,2,8,384]{3,2,1,0:T(8,128)(2,1)S(1)}, u32[]{:S(2)}, u32[]{:S(2)}) collective-permute-start(bf16[2,2,8,384]{3,2,1,0:T(8,128)(2,1)S(1)} %get-tuple-element.45), channel_id=1, source_target_pairs={{0,8},{8,16},{16,24},{24,32},{32,40},{40,48},{48,56},{56,64},{64,7... | collective-permute-start | bytes 73736 | tf_op jit(solution)/shard_map/ppermute | solution.py:618
  8.1 0.1 pad_add_fusion.place
  8.2 3.8 %fetch.1 = (bf16[64,2,8,384]{3,2,1,0:T(8,128)(2,1)S(1)}, bf16[64,2,8,384]{3,2,1,0:T(8,128)(2,1)S(1)}, bf16[3,3,3,384,384]{4,3,2,1,0:T(8,128)(2,1)S(1)}) custom-call(bf16[64,2,8,384]{3,2,1,0:T(8,128)(2,1)} %frames.1, bf16[64,2,8,384]{3,2,1,0:T(8,128)(2,1)} %out_grad.1, bf16[3,3,3,384,384]{4,3,2,1,0:T(8,128)(2,1)} %weight.1), custom_call_target="tpu_custom_call" | custom-call | bytes 20971520 | tf_op jit(solution)/shard_map/fetch/pallas_call | solution.py:41
  12.0 1.1 %pack.1 = (bf16[208,768]{1,0:T(8,128)(2,1)S(1)}, bf16[208,768]{1,0:T(8,128)(2,1)S(1)}) custom-call(s32[2]{0:T(128)S(1)} %pad_add_fusion.place, bf16[64,2,8,384]{3,2,1,0:T(8,128)(2,1)S(1)} %get-tuple-element.23.frames, bf16[64,2,8,384]{3,2,1,0:T(8,128)(2,1)S(1)} %get-tuple-element.27.out_grad, bf16[2,2,8,384]{3,2,1,0:T(8,128)(2,1)S(1)} %collective-permute-done.before, ...), custom_call_target="tpu_custom_call" | custom-call | tf_op jit(solution)/shard_map/pack/pallas_call | solution.py:186
  13.2 1.4 %collective-permute-start.2 = (bf16[208,768]{1,0:T(8,128)(2,1)S(1)}, bf16[208,768]{1,0:T(8,128)(2,1)S(1)}, u32[]{:S(2)}, u32[]{:S(2)}) collective-permute-start(bf16[208,768]{1,0:T(8,128)(2,1)S(1)} %get-tuple-element.28.core_sent), channel_id=1, source_target_pairs={{0,1},{1,0},{2,3},{3,2},{4,5},{5,4},{6,7},{7,6},{8,9},{9,8},{10,11... | collective-permute-start | bytes 958472 | tf_op jit(solution)/shard_map/ppermute | solution.py:625
  14.6 3.1 %collective-permute-start.3 = (bf16[208,768]{1,0:T(8,128)(2,1)S(1)}, bf16[208,768]{1,0:T(8,128)(2,1)S(1)}, u32[]{:S(2)}, u32[]{:S(2)}) collective-permute-start(bf16[208,768]{1,0:T(8,128)(2,1)S(1)} %get-tuple-element.29.chip_sent), channel_id=1, source_target_pairs={{1,2},{3,4},{5,6},{2,1},{4,3},{6,5},{9,10},{11,12},{13,14},{10,9},... | collective-permute-start | bytes 958472 | tf_op jit(solution)/shard_map/ppermute | solution.py:631
  17.7 1.5 %fold.1.folded = bf16[9,768,768]{2,1,0:T(8,128)(2,1)S(1)} custom-call(bf16[3,3,3,384,384]{4,3,2,1,0:T(8,128)(2,1)S(1)} %get-tuple-element.30.weight), custom_call_target="tpu_custom_call" | custom-call | bytes 20971520 | tf_op jit(solution)/shard_map/fold/pallas_call | solution.py:76
  19.2 0.0 copy-start.4
  19.2 0.0 copy-start.5
  19.2 2.1 %centre.1.middle = f32[528,768]{1,0:T(8,128)S(1)} custom-call(bf16[64,2,8,384]{3,2,1,0:T(8,128)(2,1)S(1)} %get-tuple-element.23.frames, bf16[2,2,8,384]{3,2,1,0:T(8,128)(2,1)S(1)} %collective-permute-done.before, bf16[4,2,8,384]{3,2,1,0:T(8,128)(2,1)S(1)} %collective-permute-done.1.after, bf16[9,768,768]{2,1,0:T(8,128)(2,1)S(1)} %fold.1.folded), custom_call_target="tpu_custom_call" | custom-call | flops 1868562432 | bytes 6291456 | tf_op jit(solution)/shard_map/centre/pallas_call | solution.py:228
  21.3 1.5 %collective-permute-done.3.chip_got = bf16[208,768]{1,0:T(8,128)(2,1)S(1)} collective-permute-done((bf16[208,768]{1,0:T(8,128)(2,1)S(1)}, bf16[208,768]{1,0:T(8,128)(2,1)S(1)}, u32[]{:S(2)}, u32[]{:S(2)}) %collective-permute-start.3) | collective-permute-done | bytes 319520 | tf_op jit(solution)/shard_map/ppermute | solution.py:631
  22.9 8.6 %forward.1 = (f32[8,16,384]{2,1,0:T(8,128)S(1)}, f32[8,16,384]{2,1,0:T(8,128)S(1)}, f32[16,16,384]{2,1,0:T(8,128)S(1)}, f32[72,768]{1,0:T(8,128)S(1)}, f32[72,76...) custom-call(s32[2]{0:T(128)S(1)} %pad_add_fusion.place, s32[8]{0:T(128)S(1)} %copy-done.4, ...), custom_call_target="tpu_custom_call" | custom-call | flops 5605687296 | bytes 16777216 | tf_op jit(solution)/shard_map/forward/pallas_call | solution.py:390
  31.5 17.7 %all_to_all.5.tails = f32[16,16,384]{2,1,0:T(8,128)S(1)} all-to-all(f32[16,16,384]{2,1,0:T(8,128)S(1)} %get-tuple-element.36), channel_id=1, replica_groups=mesh['tm'=16,'scene'=8] {'tm'}, dimensions={0} | all-to-all | bytes 786432 | tf_op jit(solution)/shard_map/all_to_all | solution.py:678
  49.1 0.7 mix.1.refs_0_
  49.8 2.7 %collective-permute-start.4 = (bf16[128,384]{1,0:T(8,128)(2,1)S(1)}, bf16[128,384]{1,0:T(8,128)(2,1)S(1)}, u32[]{:S(2)}, u32[]{:S(2)}) collective-permute-start(bf16[128,384]{1,0:T(8,128)(2,1)S(1)} %mix.1.refs_0_), channel_id=1, source_target_pairs={{0,2},{1,3},{2,4},{3,5},{4,6},{5,7},{6,0},{7,1},{8,10},{9,11},{10,... | collective-permute-start | bytes 294920 | tf_op jit(solution)/shard_map/ppermute | solution.py:637
  52.5 1.6 %collective-permute-start.5 = (bf16[128,384]{1,0:T(8,128)(2,1)S(1)}, bf16[128,384]{1,0:T(8,128)(2,1)S(1)}, u32[]{:S(2)}, u32[]{:S(2)}) collective-permute-start(bf16[128,384]{1,0:T(8,128)(2,1)S(1)} %mix.1.refs_0_), channel_id=1, source_target_pairs={{0,4},{1,5},{2,6},{3,7},{4,0},{5,1},{6,2},{7,3},{8,12},{9,13},{10,... | collective-permute-start | bytes 294920 | tf_op jit(solution)/shard_map/ppermute | solution.py:637
  54.1 2.0 %collective-permute-start.6 = (bf16[128,384]{1,0:T(8,128)(2,1)S(1)}, bf16[128,384]{1,0:T(8,128)(2,1)S(1)}, u32[]{:S(2)}, u32[]{:S(2)}) collective-permute-start(bf16[128,384]{1,0:T(8,128)(2,1)S(1)} %mix.1.refs_0_), channel_id=1, source_target_pairs={{0,6},{1,7},{2,0},{3,1},{4,2},{5,3},{6,4},{7,5},{8,14},{9,15},{10,... | collective-permute-start | bytes 294920 | tf_op jit(solution)/shard_map/ppermute | solution.py:637
  56.1 0.0 copy-start.3
  56.1 6.8 %backward.1 = bf16[64,2,8,384]{3,2,1,0:T(8,128)(2,1)} custom-call(bf16[66,8,768]{2,1,0:T(8,128)(2,1)S(1)} %get-tuple-element.37.grad, f32[72,768]{1,0:T(8,128)S(1)} %get-tuple-element.38.low, f32[72,768]{1,0:T(8,128)S(1)} %get-tuple-element.39.high, bf16[64,2,8,384]{3,2,1,0:T(8,128)(2,1)S(1)} %get-tuple-element.27.out_grad, bf16[9,768,768]{2,1,0:T(8,128)(2,1)S(1)} %fold.1.folded), custom_call_target="tpu_custom_call" | custom-call | flops 5435817984 | bytes 12582912 | tf_op jit(solution)/shard_map/backward/pallas_call | solution.py:488
  62.9 2.3 %collective-permute-start.7 = (bf16[128,384]{1,0:T(8,128)(2,1)S(1)}, bf16[128,384]{1,0:T(8,128)(2,1)S(1)}, u32[]{:S(2)}, u32[]{:S(2)}) collective-permute-start(bf16[128,384]{1,0:T(8,128)(2,1)S(1)} %mix.1.refs_0_), channel_id=1, source_target_pairs={{0,1},{1,0},{2,3},{3,2},{4,5},{5,4},{6,7},{7,6},{8,9},{9,8},{10,11... | collective-permute-start | bytes 294920 | tf_op jit(solution)/shard_map/ppermute | solution.py:625
  65.3 0.1 collective-permute-start.10
  65.4 0.5 collective-permute-start.8
  65.8 0.1 collective-permute-start.9
  65.9 0.1 copy.12.labels
  66.0 0.2 collective-permute-done.7.refs_4_
  66.2 0.4 collective-permute-done.10.refs_7_
  66.6 0.2 collective-permute-done.8.refs_5_
  66.8 0.4 collective-permute-done.9.refs_6_
  67.2 3.4 %attend.1 = bf16[8,2,8,384]{3,2,1,0:T(8,128)(2,1)} custom-call(s32[8,1]{1,0:T(8,128)S(1)} %copy.12.labels, bf16[128,384]{1,0:T(8,128)(2,1)S(1)} %mix.1.refs_0_, bf16[128,384]{1,0:T(8,128)(2,1)S(1)} %collective-permute-done.4.refs_1_, bf16[128,384]{1,0:T(8,128)(2,1)S(1)} %collective-permute-done.5.refs_2_, ...), custom_call_target="tpu_custom_call" | custom-call | tf_op jit(solution)/shard_map/attend/pallas_call | solution.py:605
  (18 shorter events, 0.0 us)
Async XLA Ops:
  2.1 9.9 %collective-permute-start.1 = (bf16[4,2,8,384]{3,2,1,0:T(8,128)(2,1)S(1)}, bf16[4,2,8,384]{3,2,1,0:T(8,128)(2,1)S(1)}, u32[]{:S(2)}, u32[]{:S(2)}) collective-permute-start(bf16[4,2,8,384]{3,2,1,0:T(8,128)(2,1)S(1)} %pad_maximum_fusion), channel_id=1, source_target_pairs={{8,0},{16,8},{24,16},{32,24},{40,32},{48,40},{56,48},{64,56},{72,6... | collective-permute-start | bytes 147464 | tf_op jit(solution)/shard_map/ppermute | solution.py:618
  3.4 8.5 %collective-permute-start = (bf16[2,2,8,384]{3,2,1,0:T(8,128)(2,1)S(1)}, bf16[2,2,8,384]{3,2,1,0:T(8,128)(2,1)S(1)}, u32[]{:S(2)}, u32[]{:S(2)}) collective-permute-start(bf16[2,2,8,384]{3,2,1,0:T(8,128)(2,1)S(1)} %get-tuple-element.45), channel_id=1, source_target_pairs={{0,8},{8,16},{16,24},{24,32},{32,40},{40,48},{48,56},{56,64},{64,7... | collective-permute-start | bytes 73736 | tf_op jit(solution)/shard_map/ppermute | solution.py:618
  13.2 8.1 %collective-permute-start.2 = (bf16[208,768]{1,0:T(8,128)(2,1)S(1)}, bf16[208,768]{1,0:T(8,128)(2,1)S(1)}, u32[]{:S(2)}, u32[]{:S(2)}) collective-permute-start(bf16[208,768]{1,0:T(8,128)(2,1)S(1)} %get-tuple-element.28.core_sent), channel_id=1, source_target_pairs={{0,1},{1,0},{2,3},{3,2},{4,5},{5,4},{6,7},{7,6},{8,9},{9,8},{10,11... | collective-permute-start | bytes 958472 | tf_op jit(solution)/shard_map/ppermute | solution.py:625
  14.6 8.3 %collective-permute-start.3 = (bf16[208,768]{1,0:T(8,128)(2,1)S(1)}, bf16[208,768]{1,0:T(8,128)(2,1)S(1)}, u32[]{:S(2)}, u32[]{:S(2)}) collective-permute-start(bf16[208,768]{1,0:T(8,128)(2,1)S(1)} %get-tuple-element.29.chip_sent), channel_id=1, source_target_pairs={{1,2},{3,4},{5,6},{2,1},{4,3},{6,5},{9,10},{11,12},{13,14},{10,9},... | collective-permute-start | bytes 958472 | tf_op jit(solution)/shard_map/ppermute | solution.py:631
  19.2 3.7 %copy-start.4 = (s32[8]{0:T(128)S(1)}, s32[8]{0:T(128)}, u32[]{:S(2)}) copy-start(s32[8]{0:T(128)} %lengths.3) | copy-start | bytes 100
  19.2 3.7 %copy-start.5 = (bf16[8,384,384]{2,1,0:T(8,128)(2,1)S(1)}, bf16[8,384,384]{2,1,0:T(8,128)(2,1)}, u32[]{:S(2)}) copy-start(bf16[8,384,384]{2,1,0:T(8,128)(2,1)} %down.1) | copy-start | bytes 7077892
  49.8 15.4 %collective-permute-start.4 = (bf16[128,384]{1,0:T(8,128)(2,1)S(1)}, bf16[128,384]{1,0:T(8,128)(2,1)S(1)}, u32[]{:S(2)}, u32[]{:S(2)}) collective-permute-start(bf16[128,384]{1,0:T(8,128)(2,1)S(1)} %mix.1.refs_0_), channel_id=1, source_target_pairs={{0,2},{1,3},{2,4},{3,5},{4,6},{5,7},{6,0},{7,1},{8,10},{9,11},{10,... | collective-permute-start | bytes 294920 | tf_op jit(solution)/shard_map/ppermute | solution.py:637
  52.5 12.8 %collective-permute-start.5 = (bf16[128,384]{1,0:T(8,128)(2,1)S(1)}, bf16[128,384]{1,0:T(8,128)(2,1)S(1)}, u32[]{:S(2)}, u32[]{:S(2)}) collective-permute-start(bf16[128,384]{1,0:T(8,128)(2,1)S(1)} %mix.1.refs_0_), channel_id=1, source_target_pairs={{0,4},{1,5},{2,6},{3,7},{4,0},{5,1},{6,2},{7,3},{8,12},{9,13},{10,... | collective-permute-start | bytes 294920 | tf_op jit(solution)/shard_map/ppermute | solution.py:637
  54.1 11.1 %collective-permute-start.6 = (bf16[128,384]{1,0:T(8,128)(2,1)S(1)}, bf16[128,384]{1,0:T(8,128)(2,1)S(1)}, u32[]{:S(2)}, u32[]{:S(2)}) collective-permute-start(bf16[128,384]{1,0:T(8,128)(2,1)S(1)} %mix.1.refs_0_), channel_id=1, source_target_pairs={{0,6},{1,7},{2,0},{3,1},{4,2},{5,3},{6,4},{7,5},{8,14},{9,15},{10,... | collective-permute-start | bytes 294920 | tf_op jit(solution)/shard_map/ppermute | solution.py:637
  56.1 9.8 %copy-start.6 = (s32[8,1]{0,1:T(1,128)S(1)}, s32[8,1]{0,1:T(1,128)}, u32[]{:S(2)}) copy-start(s32[8,1]{0,1:T(1,128)} %param.18) | copy-start | bytes 100
  56.1 11.1 %copy-start = (bf16[384,384]{1,0:T(8,128)(2,1)S(1)}, bf16[384,384]{1,0:T(8,128)(2,1)}, u32[]{:S(2)}) copy-start(bf16[384,384]{1,0:T(8,128)(2,1)} %refs_8_.1) | copy-start | bytes 884740
  56.1 11.1 %copy-start.1 = (bf16[384,384]{1,0:T(8,128)(2,1)S(1)}, bf16[384,384]{1,0:T(8,128)(2,1)}, u32[]{:S(2)}) copy-start(bf16[384,384]{1,0:T(8,128)(2,1)} %refs_9_.1) | copy-start | bytes 884740
  56.1 11.1 %copy-start.2 = (bf16[384,384]{1,0:T(8,128)(2,1)S(1)}, bf16[384,384]{1,0:T(8,128)(2,1)}, u32[]{:S(2)}) copy-start(bf16[384,384]{1,0:T(8,128)(2,1)} %refs_10_.1) | copy-start | bytes 884740
  56.1 11.1 %copy-start.3 = (bf16[384,384]{1,0:T(8,128)(2,1)S(1)}, bf16[384,384]{1,0:T(8,128)(2,1)}, u32[]{:S(2)}) copy-start(bf16[384,384]{1,0:T(8,128)(2,1)} %refs_11_.1) | copy-start | bytes 884740
  62.9 3.3 %collective-permute-start.7 = (bf16[128,384]{1,0:T(8,128)(2,1)S(1)}, bf16[128,384]{1,0:T(8,128)(2,1)S(1)}, u32[]{:S(2)}, u32[]{:S(2)}) collective-permute-start(bf16[128,384]{1,0:T(8,128)(2,1)S(1)} %mix.1.refs_0_), channel_id=1, source_target_pairs={{0,1},{1,0},{2,3},{3,2},{4,5},{5,4},{6,7},{7,6},{8,9},{9,8},{10,11... | collective-permute-start | bytes 294920 | tf_op jit(solution)/shard_map/ppermute | solution.py:625
  65.3 1.4 %collective-permute-start.10 = (bf16[128,384]{1,0:T(8,128)(2,1)S(1)}, bf16[128,384]{1,0:T(8,128)(2,1)S(1)}, u32[]{:S(2)}, u32[]{:S(2)}) collective-permute-start(bf16[128,384]{1,0:T(8,128)(2,1)S(1)} %collective-permute-done.6.refs_3_), channel_id=1, source_target_pairs={{0,1},{1,0},{2,3},{3,2},{4,5},{5,4},{6,7},{7,6},{8,9},{9,8},{10,11... | collective-permute-start | bytes 294920 | tf_op jit(solution)/shard_map/ppermute | solution.py:625
  65.4 1.4 %collective-permute-start.8 = (bf16[128,384]{1,0:T(8,128)(2,1)S(1)}, bf16[128,384]{1,0:T(8,128)(2,1)S(1)}, u32[]{:S(2)}, u32[]{:S(2)}) collective-permute-start(bf16[128,384]{1,0:T(8,128)(2,1)S(1)} %collective-permute-done.4.refs_1_), channel_id=1, source_target_pairs={{0,1},{1,0},{2,3},{3,2},{4,5},{5,4},{6,7},{7,6},{8,9},{9,8},{10,11... | collective-permute-start | bytes 294920 | tf_op jit(solution)/shard_map/ppermute | solution.py:625
  65.8 1.3 %collective-permute-start.9 = (bf16[128,384]{1,0:T(8,128)(2,1)S(1)}, bf16[128,384]{1,0:T(8,128)(2,1)S(1)}, u32[]{:S(2)}, u32[]{:S(2)}) collective-permute-start(bf16[128,384]{1,0:T(8,128)(2,1)S(1)} %collective-permute-done.5.refs_2_), channel_id=1, source_target_pairs={{0,1},{1,0},{2,3},{3,2},{4,5},{5,4},{6,7},{7,6},{8,9},{9,8},{10,11... | collective-permute-start | bytes 294920 | tf_op jit(solution)/shard_map/ppermute | solution.py:625

commit v6 on v5

--- a/solution.py
+++ b/solution.py
@@ -22,6 +22,32 @@
 
 def dot(a, b, dims=NN):
     return lax.dot_general(a, b, dims, preferred_element_type=F32)
+
+
+def cut_kernel(frames, out_grad, last, first, sems):
+    count = frames.shape[0]
+    copies = [
+        pltpu.make_async_copy(frames.at[pl.ds(count - 2, 2)], last, sems.at[0]),
+        pltpu.make_async_copy(frames.at[pl.ds(0, 2)], first.at[pl.ds(0, 2)], sems.at[1]),
+        pltpu.make_async_copy(out_grad.at[pl.ds(0, 2)], first.at[pl.ds(2, 2)], sems.at[2]),
+    ]
+    for copy in copies:
+        copy.start()
+    for copy in copies:
+        copy.wait()
+
+
+def cut(frames, out_grad):
+    shape = frames.shape[1:]
+    return pl.pallas_call(
+        cut_kernel,
+        out_shape=[pltpu.VMEM((2, *shape), BF16), pltpu.VMEM((4, *shape), BF16)],
+        in_specs=[pl.BlockSpec(memory_space=pltpu.HBM)] * 2,
+        out_specs=[VMEM] * 2,
+        scratch_shapes=[pltpu.SemaphoreType.DMA((3,))],
+        compiler_params=pltpu.CompilerParams(vmem_limit_bytes=60 * 2**20),
+        name="cut",
+    )(frames, out_grad)
 
 
 def fetch_kernel(frames, out_grad, weight, frames_out, grad_out, weight_out, sems):
@@ -651,10 +677,12 @@
     scene_label,
     out_grad,
 ):
-    count = frames.shape[0]
     place = jnp.stack([lax.axis_index("tm"), lax.axis_index("scene") % 2]).astype(jnp.int32)
-    before = shifted(frames[count - 2 :], "tm", 1)
-    after = shifted(jnp.concatenate([frames[:2], out_grad[:2]], axis=0), "tm", -1)
+    last, first = cut(
+        *(pltpu.with_memory_space_constraint(value, pltpu.HBM) for value in (frames, out_grad))
+    )
+    before = shifted(last, "tm", 1)
+    after = shifted(first, "tm", -1)
     near_frames, near_grad, near_weight = fetch(frames, out_grad, conv_weight)
     (before, after), near_weight = lax.optimization_barrier(((before, after), near_weight))
     sent = pack(place, near_frames, near_grad, before, after)

time: 70.9 us -> 70.1 us (0.989)
  local copies, waits for them, and re-layouts: 1.62 us -> 0.11 us
  Pallas kernels: 28 us -> 28.8 us
    slice x2 -> x0, local copies, waits for them, and re-layouts: 1.5 us -> none  [the longest x1 0.76 us: per_device(): frames[:2]]
    pallas_call x0 -> x1, Pallas kernels: none -> 0.8 us  [cut(): pl.pallas_call(cut_kernel, out_shape=[pltpu.VMEM((2, *shape), BF16), pltp...]
where the time goes in v6:
time: 70.1 us; the launch traced here: 69.9 us
  Pallas kernels  28.8 us (41%)
  starting transfers between devices  19.7 us (28%)
  blocking collectives  17.7 us (25%)
  waiting for transfers between devices  2.67 us (4%)
  between operations  0.8 us (1%)
    all_to_all x1, blocking collectives, per_device(): tails = lax.all_to_all(tail, 'tm', 0, 0, tiled=True)  17.7 us
    pallas_call x1, Pallas kernels, forward(): pl.pallas_call(forward_kernel, out_shape=(pltpu.VMEM((lat, 16, chans), F3...  8.59 us
    pallas_call x1, Pallas kernels, backward(): pl.pallas_call(backward_kernel, out_shape=jax.ShapeDtypeStruct(out_grad.s...  6.78 us
    ppermute x3, starting transfers between devices, chip_shifts(): lax.ppermute(value, 'scene', [(i, (i + 2 * k) % count) for i in range(cou...  6.25 us
    ppermute x2, starting transfers between devices, shifted(): lax.ppermute(value, axis, [(i, i + steps) for i in range(count) if 0 <= i...  5.95 us
    ppermute x5, starting transfers between devices, with_core(): return lax.ppermute(value, 'scene', [(i, i ^ 1) for i in range(count)])  4.41 us
    pallas_call x1, Pallas kernels, fetch(): pl.pallas_call(fetch_kernel, out_shape=[pltpu.VMEM(value.shape, BF16) for...  3.78 us
    pallas_call x1, Pallas kernels, attend(): pl.pallas_call(attend_kernel, out_shape=jax.ShapeDtypeStruct((lat, 2, 8,...  3.4 us
  transfers between devices with their start and end apart: 11, of which 5 were waited for; matrix products, arithmetic and copies ran while one was open for 0% of the time, Pallas kernels for 20%

profile of v6, /device:TPU:1, one launch (start us, length us, event | category | flops | bytes accessed | tf_op | source)
XLA Modules:
  0.0 69.9 jit_solution(9045406333190199186)
XLA Ops:
  0.6 0.8 %cut.1 = (bf16[2,2,8,384]{3,2,1,0:T(8,128)(2,1)S(1)}, bf16[4,2,8,384]{3,2,1,0:T(8,128)(2,1)S(1)}) custom-call(bf16[64,2,8,384]{3,2,1,0:T(8,128)(2,1)} %frames.3, bf16[64,2,8,384]{3,2,1,0:T(8,128)(2,1)} %out_grad.3), custom_call_target="tpu_custom_call" | custom-call | tf_op jit(solution)/shard_map/cut/pallas_call | solution.py:42
  1.4 1.3 %collective-permute-start.1 = (bf16[4,2,8,384]{3,2,1,0:T(8,128)(2,1)S(1)}, bf16[4,2,8,384]{3,2,1,0:T(8,128)(2,1)S(1)}, u32[]{:S(2)}, u32[]{:S(2)}) collective-permute-start(bf16[4,2,8,384]{3,2,1,0:T(8,128)(2,1)S(1)} %get-tuple-element.27), channel_id=1, source_target_pairs={{8,0},{16,8},{24,16},{32,24},{40,32},{48,40},{56,48},{64,56},{72,6... | collective-permute-start | bytes 147464 | tf_op jit(solution)/shard_map/ppermute | solution.py:644
  2.7 4.7 %collective-permute-start = (bf16[2,2,8,384]{3,2,1,0:T(8,128)(2,1)S(1)}, bf16[2,2,8,384]{3,2,1,0:T(8,128)(2,1)S(1)}, u32[]{:S(2)}, u32[]{:S(2)}) collective-permute-start(bf16[2,2,8,384]{3,2,1,0:T(8,128)(2,1)S(1)} %get-tuple-element.26), channel_id=1, source_target_pairs={{0,8},{8,16},{16,24},{24,32},{32,40},{40,48},{48,56},{56,64},{64,7... | collective-permute-start | bytes 73736 | tf_op jit(solution)/shard_map/ppermute | solution.py:644
  7.4 0.1 pad_add_fusion.place
  7.5 3.8 %fetch.1 = (bf16[64,2,8,384]{3,2,1,0:T(8,128)(2,1)S(1)}, bf16[64,2,8,384]{3,2,1,0:T(8,128)(2,1)S(1)}, bf16[3,3,3,384,384]{4,3,2,1,0:T(8,128)(2,1)S(1)}) custom-call(bf16[64,2,8,384]{3,2,1,0:T(8,128)(2,1)} %frames.3, bf16[64,2,8,384]{3,2,1,0:T(8,128)(2,1)} %out_grad.3, bf16[3,3,3,384,384]{4,3,2,1,0:T(8,128)(2,1)} %weight.1), custom_call_target="tpu_custom_call" | custom-call | bytes 20971520 | tf_op jit(solution)/shard_map/fetch/pallas_call | solution.py:67
  11.3 0.0 collective-permute-done.before
  11.3 1.1 %pack.1 = (bf16[208,768]{1,0:T(8,128)(2,1)S(1)}, bf16[208,768]{1,0:T(8,128)(2,1)S(1)}) custom-call(s32[2]{0:T(128)S(1)} %pad_add_fusion.place, bf16[64,2,8,384]{3,2,1,0:T(8,128)(2,1)S(1)} %get-tuple-element.25.frames, bf16[64,2,8,384]{3,2,1,0:T(8,128)(2,1)S(1)} %get-tuple-element.31.out_grad, bf16[2,2,8,384]{3,2,1,0:T(8,128)(2,1)S(1)} %collective-permute-done.before, ...), custom_call_target="tpu_custom_call" | custom-call | tf_op jit(solution)/shard_map/pack/pallas_call | solution.py:212
  12.5 1.4 %collective-permute-start.2 = (bf16[208,768]{1,0:T(8,128)(2,1)S(1)}, bf16[208,768]{1,0:T(8,128)(2,1)S(1)}, u32[]{:S(2)}, u32[]{:S(2)}) collective-permute-start(bf16[208,768]{1,0:T(8,128)(2,1)S(1)} %get-tuple-element.32.core_sent), channel_id=1, source_target_pairs={{0,1},{1,0},{2,3},{3,2},{4,5},{5,4},{6,7},{7,6},{8,9},{9,8},{10,11... | collective-permute-start | bytes 958472 | tf_op jit(solution)/shard_map/ppermute | solution.py:651
  13.9 3.1 %collective-permute-start.3 = (bf16[208,768]{1,0:T(8,128)(2,1)S(1)}, bf16[208,768]{1,0:T(8,128)(2,1)S(1)}, u32[]{:S(2)}, u32[]{:S(2)}) collective-permute-start(bf16[208,768]{1,0:T(8,128)(2,1)S(1)} %get-tuple-element.33.chip_sent), channel_id=1, source_target_pairs={{1,2},{3,4},{5,6},{2,1},{4,3},{6,5},{9,10},{11,12},{13,14},{10,9},... | collective-permute-start | bytes 958472 | tf_op jit(solution)/shard_map/ppermute | solution.py:657
  17.0 1.5 %fold.1.folded = bf16[9,768,768]{2,1,0:T(8,128)(2,1)S(1)} custom-call(bf16[3,3,3,384,384]{4,3,2,1,0:T(8,128)(2,1)S(1)} %get-tuple-element.34.weight), custom_call_target="tpu_custom_call" | custom-call | bytes 20971520 | tf_op jit(solution)/shard_map/fold/pallas_call | solution.py:102
  18.5 0.0 copy-start.4
  18.5 0.0 copy-start.5
  18.5 2.1 %centre.1.middle = f32[528,768]{1,0:T(8,128)S(1)} custom-call(bf16[64,2,8,384]{3,2,1,0:T(8,128)(2,1)S(1)} %get-tuple-element.25.frames, bf16[2,2,8,384]{3,2,1,0:T(8,128)(2,1)S(1)} %collective-permute-done.before, bf16[4,2,8,384]{3,2,1,0:T(8,128)(2,1)S(1)} %collective-permute-done.1.after, bf16[9,768,768]{2,1,0:T(8,128)(2,1)S(1)} %fold.1.folded), custom_call_target="tpu_custom_call" | custom-call | flops 1868562432 | bytes 6291456 | tf_op jit(solution)/shard_map/centre/pallas_call | solution.py:254
  20.6 1.5 %collective-permute-done.3.chip_got = bf16[208,768]{1,0:T(8,128)(2,1)S(1)} collective-permute-done((bf16[208,768]{1,0:T(8,128)(2,1)S(1)}, bf16[208,768]{1,0:T(8,128)(2,1)S(1)}, u32[]{:S(2)}, u32[]{:S(2)}) %collective-permute-start.3) | collective-permute-done | bytes 319520 | tf_op jit(solution)/shard_map/ppermute | solution.py:657
  22.2 8.6 %forward.1 = (f32[8,16,384]{2,1,0:T(8,128)S(1)}, f32[8,16,384]{2,1,0:T(8,128)S(1)}, f32[16,16,384]{2,1,0:T(8,128)S(1)}, f32[72,768]{1,0:T(8,128)S(1)}, f32[72,76...) custom-call(s32[2]{0:T(128)S(1)} %pad_add_fusion.place, s32[8]{0:T(128)S(1)} %copy-done.4, ...), custom_call_target="tpu_custom_call" | custom-call | flops 5605687296 | bytes 16777216 | tf_op jit(solution)/shard_map/forward/pallas_call | solution.py:416
  30.7 17.7 %all_to_all.5.tails = f32[16,16,384]{2,1,0:T(8,128)S(1)} all-to-all(f32[16,16,384]{2,1,0:T(8,128)S(1)} %get-tuple-element.40), channel_id=1, replica_groups=mesh['tm'=16,'scene'=8] {'tm'}, dimensions={0} | all-to-all | bytes 786432 | tf_op jit(solution)/shard_map/all_to_all | solution.py:706
  48.4 0.7 %mix.1.refs_0_ = bf16[128,384]{1,0:T(8,128)(2,1)S(1)} custom-call(s32[2]{0:T(128)S(1)} %pad_add_fusion.place, s32[8]{0:T(128)S(1)} %copy-done.4, f32[8,16,384]{2,1,0:T(8,128)S(1)} %get-tuple-element.38.latent, f32[8,16,384]{2,1,0:T(8,128)S(1)} %get-tuple-element.39.sums, f32[16,16,384]{2,1,0:T(8,128)S(1)} %all_to_all.5.tails), custom_call_target="tpu_custom_call" | custom-call | tf_op jit(solution)/shard_map/mix/pallas_call | solution.py:559
  49.1 2.6 %collective-permute-start.4 = (bf16[128,384]{1,0:T(8,128)(2,1)S(1)}, bf16[128,384]{1,0:T(8,128)(2,1)S(1)}, u32[]{:S(2)}, u32[]{:S(2)}) collective-permute-start(bf16[128,384]{1,0:T(8,128)(2,1)S(1)} %mix.1.refs_0_), channel_id=1, source_target_pairs={{0,2},{1,3},{2,4},{3,5},{4,6},{5,7},{6,0},{7,1},{8,10},{9,11},{10,... | collective-permute-start | bytes 294920 | tf_op jit(solution)/shard_map/ppermute | solution.py:663
  51.8 1.6 %collective-permute-start.5 = (bf16[128,384]{1,0:T(8,128)(2,1)S(1)}, bf16[128,384]{1,0:T(8,128)(2,1)S(1)}, u32[]{:S(2)}, u32[]{:S(2)}) collective-permute-start(bf16[128,384]{1,0:T(8,128)(2,1)S(1)} %mix.1.refs_0_), channel_id=1, source_target_pairs={{0,4},{1,5},{2,6},{3,7},{4,0},{5,1},{6,2},{7,3},{8,12},{9,13},{10,... | collective-permute-start | bytes 294920 | tf_op jit(solution)/shard_map/ppermute | solution.py:663
  53.4 2.0 %collective-permute-start.6 = (bf16[128,384]{1,0:T(8,128)(2,1)S(1)}, bf16[128,384]{1,0:T(8,128)(2,1)S(1)}, u32[]{:S(2)}, u32[]{:S(2)}) collective-permute-start(bf16[128,384]{1,0:T(8,128)(2,1)S(1)} %mix.1.refs_0_), channel_id=1, source_target_pairs={{0,6},{1,7},{2,0},{3,1},{4,2},{5,3},{6,4},{7,5},{8,14},{9,15},{10,... | collective-permute-start | bytes 294920 | tf_op jit(solution)/shard_map/ppermute | solution.py:663
  55.4 0.0 copy-start.3
  55.4 6.8 %backward.1 = bf16[64,2,8,384]{3,2,1,0:T(8,128)(2,1)} custom-call(bf16[66,8,768]{2,1,0:T(8,128)(2,1)S(1)} %get-tuple-element.41.grad, f32[72,768]{1,0:T(8,128)S(1)} %get-tuple-element.42.low, f32[72,768]{1,0:T(8,128)S(1)} %get-tuple-element.43.high, bf16[64,2,8,384]{3,2,1,0:T(8,128)(2,1)S(1)} %get-tuple-element.31.out_grad, bf16[9,768,768]{2,1,0:T(8,128)(2,1)S(1)} %fold.1.folded), custom_call_target="tpu_custom_call" | custom-call | flops 5435817984 | bytes 12582912 | tf_op jit(solution)/shard_map/backward/pallas_call | solution.py:514
  62.2 2.3 %collective-permute-start.7 = (bf16[128,384]{1,0:T(8,128)(2,1)S(1)}, bf16[128,384]{1,0:T(8,128)(2,1)S(1)}, u32[]{:S(2)}, u32[]{:S(2)}) collective-permute-start(bf16[128,384]{1,0:T(8,128)(2,1)S(1)} %mix.1.refs_0_), channel_id=1, source_target_pairs={{0,1},{1,0},{2,3},{3,2},{4,5},{5,4},{6,7},{7,6},{8,9},{9,8},{10,11... | collective-permute-start | bytes 294920 | tf_op jit(solution)/shard_map/ppermute | solution.py:651
  64.5 0.1 collective-permute-start.10
  64.7 0.5 collective-permute-start.8
  65.1 0.1 collective-permute-start.9
  65.2 0.1 copy.12.labels
  65.3 0.2 collective-permute-done.7.refs_4_
  65.5 0.4 collective-permute-done.10.refs_7_
  65.9 0.2 collective-permute-done.8.refs_5_
  66.1 0.4 collective-permute-done.9.refs_6_
  66.5 3.4 %attend.1 = bf16[8,2,8,384]{3,2,1,0:T(8,128)(2,1)} custom-call(s32[8,1]{1,0:T(8,128)S(1)} %copy.12.labels, bf16[128,384]{1,0:T(8,128)(2,1)S(1)} %mix.1.refs_0_, bf16[128,384]{1,0:T(8,128)(2,1)S(1)} %collective-permute-done.4.refs_1_, bf16[128,384]{1,0:T(8,128)(2,1)S(1)} %collective-permute-done.5.refs_2_, ...), custom_call_target="tpu_custom_call" | custom-call | tf_op jit(solution)/shard_map/attend/pallas_call | solution.py:631
  (16 shorter events, 0.0 us)
Async XLA Ops:
  1.4 9.9 %collective-permute-start.1 = (bf16[4,2,8,384]{3,2,1,0:T(8,128)(2,1)S(1)}, bf16[4,2,8,384]{3,2,1,0:T(8,128)(2,1)S(1)}, u32[]{:S(2)}, u32[]{:S(2)}) collective-permute-start(bf16[4,2,8,384]{3,2,1,0:T(8,128)(2,1)S(1)} %get-tuple-element.27), channel_id=1, source_target_pairs={{8,0},{16,8},{24,16},{32,24},{40,32},{48,40},{56,48},{64,56},{72,6... | collective-permute-start | bytes 147464 | tf_op jit(solution)/shard_map/ppermute | solution.py:644
  2.7 8.5 %collective-permute-start = (bf16[2,2,8,384]{3,2,1,0:T(8,128)(2,1)S(1)}, bf16[2,2,8,384]{3,2,1,0:T(8,128)(2,1)S(1)}, u32[]{:S(2)}, u32[]{:S(2)}) collective-permute-start(bf16[2,2,8,384]{3,2,1,0:T(8,128)(2,1)S(1)} %get-tuple-element.26), channel_id=1, source_target_pairs={{0,8},{8,16},{16,24},{24,32},{32,40},{40,48},{48,56},{56,64},{64,7... | collective-permute-start | bytes 73736 | tf_op jit(solution)/shard_map/ppermute | solution.py:644
  12.5 8.1 %collective-permute-start.2 = (bf16[208,768]{1,0:T(8,128)(2,1)S(1)}, bf16[208,768]{1,0:T(8,128)(2,1)S(1)}, u32[]{:S(2)}, u32[]{:S(2)}) collective-permute-start(bf16[208,768]{1,0:T(8,128)(2,1)S(1)} %get-tuple-element.32.core_sent), channel_id=1, source_target_pairs={{0,1},{1,0},{2,3},{3,2},{4,5},{5,4},{6,7},{7,6},{8,9},{9,8},{10,11... | collective-permute-start | bytes 958472 | tf_op jit(solution)/shard_map/ppermute | solution.py:651
  13.9 8.3 %collective-permute-start.3 = (bf16[208,768]{1,0:T(8,128)(2,1)S(1)}, bf16[208,768]{1,0:T(8,128)(2,1)S(1)}, u32[]{:S(2)}, u32[]{:S(2)}) collective-permute-start(bf16[208,768]{1,0:T(8,128)(2,1)S(1)} %get-tuple-element.33.chip_sent), channel_id=1, source_target_pairs={{1,2},{3,4},{5,6},{2,1},{4,3},{6,5},{9,10},{11,12},{13,14},{10,9},... | collective-permute-start | bytes 958472 | tf_op jit(solution)/shard_map/ppermute | solution.py:657
  18.5 3.7 %copy-start.4 = (s32[8]{0:T(128)S(1)}, s32[8]{0:T(128)}, u32[]{:S(2)}) copy-start(s32[8]{0:T(128)} %lengths.3) | copy-start | bytes 100
  18.5 3.7 %copy-start.5 = (bf16[8,384,384]{2,1,0:T(8,128)(2,1)S(1)}, bf16[8,384,384]{2,1,0:T(8,128)(2,1)}, u32[]{:S(2)}) copy-start(bf16[8,384,384]{2,1,0:T(8,128)(2,1)} %down.1) | copy-start | bytes 7077892
  49.1 15.4 %collective-permute-start.4 = (bf16[128,384]{1,0:T(8,128)(2,1)S(1)}, bf16[128,384]{1,0:T(8,128)(2,1)S(1)}, u32[]{:S(2)}, u32[]{:S(2)}) collective-permute-start(bf16[128,384]{1,0:T(8,128)(2,1)S(1)} %mix.1.refs_0_), channel_id=1, source_target_pairs={{0,2},{1,3},{2,4},{3,5},{4,6},{5,7},{6,0},{7,1},{8,10},{9,11},{10,... | collective-permute-start | bytes 294920 | tf_op jit(solution)/shard_map/ppermute | solution.py:663
  51.8 12.8 %collective-permute-start.5 = (bf16[128,384]{1,0:T(8,128)(2,1)S(1)}, bf16[128,384]{1,0:T(8,128)(2,1)S(1)}, u32[]{:S(2)}, u32[]{:S(2)}) collective-permute-start(bf16[128,384]{1,0:T(8,128)(2,1)S(1)} %mix.1.refs_0_), channel_id=1, source_target_pairs={{0,4},{1,5},{2,6},{3,7},{4,0},{5,1},{6,2},{7,3},{8,12},{9,13},{10,... | collective-permute-start | bytes 294920 | tf_op jit(solution)/shard_map/ppermute | solution.py:663
  53.4 11.1 %collective-permute-start.6 = (bf16[128,384]{1,0:T(8,128)(2,1)S(1)}, bf16[128,384]{1,0:T(8,128)(2,1)S(1)}, u32[]{:S(2)}, u32[]{:S(2)}) collective-permute-start(bf16[128,384]{1,0:T(8,128)(2,1)S(1)} %mix.1.refs_0_), channel_id=1, source_target_pairs={{0,6},{1,7},{2,0},{3,1},{4,2},{5,3},{6,4},{7,5},{8,14},{9,15},{10,... | collective-permute-start | bytes 294920 | tf_op jit(solution)/shard_map/ppermute | solution.py:663
  55.4 9.8 %copy-start.6 = (s32[8,1]{0,1:T(1,128)S(1)}, s32[8,1]{0,1:T(1,128)}, u32[]{:S(2)}) copy-start(s32[8,1]{0,1:T(1,128)} %param.18) | copy-start | bytes 100
  55.4 11.1 %copy-start = (bf16[384,384]{1,0:T(8,128)(2,1)S(1)}, bf16[384,384]{1,0:T(8,128)(2,1)}, u32[]{:S(2)}) copy-start(bf16[384,384]{1,0:T(8,128)(2,1)} %refs_8_.1) | copy-start | bytes 884740
  55.4 11.1 %copy-start.1 = (bf16[384,384]{1,0:T(8,128)(2,1)S(1)}, bf16[384,384]{1,0:T(8,128)(2,1)}, u32[]{:S(2)}) copy-start(bf16[384,384]{1,0:T(8,128)(2,1)} %refs_9_.1) | copy-start | bytes 884740
  55.4 11.1 %copy-start.2 = (bf16[384,384]{1,0:T(8,128)(2,1)S(1)}, bf16[384,384]{1,0:T(8,128)(2,1)}, u32[]{:S(2)}) copy-start(bf16[384,384]{1,0:T(8,128)(2,1)} %refs_10_.1) | copy-start | bytes 884740
  55.4 11.1 %copy-start.3 = (bf16[384,384]{1,0:T(8,128)(2,1)S(1)}, bf16[384,384]{1,0:T(8,128)(2,1)}, u32[]{:S(2)}) copy-start(bf16[384,384]{1,0:T(8,128)(2,1)} %refs_11_.1) | copy-start | bytes 884740
  62.2 3.3 %collective-permute-start.7 = (bf16[128,384]{1,0:T(8,128)(2,1)S(1)}, bf16[128,384]{1,0:T(8,128)(2,1)S(1)}, u32[]{:S(2)}, u32[]{:S(2)}) collective-permute-start(bf16[128,384]{1,0:T(8,128)(2,1)S(1)} %mix.1.refs_0_), channel_id=1, source_target_pairs={{0,1},{1,0},{2,3},{3,2},{4,5},{5,4},{6,7},{7,6},{8,9},{9,8},{10,11... | collective-permute-start | bytes 294920 | tf_op jit(solution)/shard_map/ppermute | solution.py:651
  64.5 1.4 %collective-permute-start.10 = (bf16[128,384]{1,0:T(8,128)(2,1)S(1)}, bf16[128,384]{1,0:T(8,128)(2,1)S(1)}, u32[]{:S(2)}, u32[]{:S(2)}) collective-permute-start(bf16[128,384]{1,0:T(8,128)(2,1)S(1)} %collective-permute-done.6.refs_3_), channel_id=1, source_target_pairs={{0,1},{1,0},{2,3},{3,2},{4,5},{5,4},{6,7},{7,6},{8,9},{9,8},{10,11... | collective-permute-start | bytes 294920 | tf_op jit(solution)/shard_map/ppermute | solution.py:651
  64.7 1.4 %collective-permute-start.8 = (bf16[128,384]{1,0:T(8,128)(2,1)S(1)}, bf16[128,384]{1,0:T(8,128)(2,1)S(1)}, u32[]{:S(2)}, u32[]{:S(2)}) collective-permute-start(bf16[128,384]{1,0:T(8,128)(2,1)S(1)} %collective-permute-done.4.refs_1_), channel_id=1, source_target_pairs={{0,1},{1,0},{2,3},{3,2},{4,5},{5,4},{6,7},{7,6},{8,9},{9,8},{10,11... | collective-permute-start | bytes 294920 | tf_op jit(solution)/shard_map/ppermute | solution.py:651
  65.1 1.3 %collective-permute-start.9 = (bf16[128,384]{1,0:T(8,128)(2,1)S(1)}, bf16[128,384]{1,0:T(8,128)(2,1)S(1)}, u32[]{:S(2)}, u32[]{:S(2)}) collective-permute-start(bf16[128,384]{1,0:T(8,128)(2,1)S(1)} %collective-permute-done.5.refs_2_), channel_id=1, source_target_pairs={{0,1},{1,0},{2,3},{3,2},{4,5},{5,4},{6,7},{7,6},{8,9},{9,8},{10,11... | collective-permute-start | bytes 294920 | tf_op jit(solution)/shard_map/ppermute | solution.py:651

commit v7 on v6

--- a/solution.py
+++ b/solution.py
@@ -54,7 +54,7 @@
     copies = [
         pltpu.make_async_copy(source, target, sems.at[k])
         for k, (source, target) in enumerate(
-            ((frames, frames_out), (out_grad, grad_out), (weight, weight_out))
+            ((frames, frames_out), (out_grad, grad_out), (weight.at[pl.ds(0, 2)], weight_out))
         )
     ]
     for copy in copies:
@@ -66,7 +66,10 @@
 def fetch(frames, out_grad, weight):
     return pl.pallas_call(
         fetch_kernel,
-        out_shape=[pltpu.VMEM(value.shape, BF16) for value in (frames, out_grad, weight)],
+        out_shape=[
+            pltpu.VMEM(shape, BF16)
+            for shape in (frames.shape, out_grad.shape, (2, *weight.shape[1:]))
+        ],
         in_specs=[ANY] * 3,
         out_specs=[VMEM] * 3,
         scratch_shapes=[pltpu.SemaphoreType.DMA((3,))],
@@ -78,15 +81,16 @@
     )(frames, out_grad, weight)
 
 
-def fold_kernel(weight, folded, sems):
+def fold_kernel(held, weight, folded, sems):
     chans = weight.shape[-1]
     copies = []
-    for k in range(9):
+    for k in (6, 7, 8, 0, 1, 2, 3, 4, 5):
+        source = weight if k >= 6 else held
         for h_in in range(2):
             for h_out in range(2):
                 copies.append(
                     pltpu.make_async_copy(
-                        weight.at[k // 3, h_in - h_out + 1, k % 3],
+                        source.at[k // 3, h_in - h_out + 1, k % 3],
                         folded.at[k, pl.ds(h_in * chans, chans), pl.ds(h_out * chans, chans)],
                         sems.at[k, 2 * h_in + h_out],
                     )
@@ -97,12 +101,12 @@
         copy.wait()
 
 
-def fold(weight):
+def fold(held, weight):
     wide = 2 * weight.shape[-1]
     return pl.pallas_call(
         fold_kernel,
         out_shape=pltpu.VMEM((9, wide, wide), BF16),
-        in_specs=[VMEM],
+        in_specs=[VMEM, pl.BlockSpec(memory_space=pltpu.HBM)],
         out_specs=VMEM,
         scratch_shapes=[pltpu.SemaphoreType.DMA((9, 4))],
         compiler_params=pltpu.CompilerParams(vmem_limit_bytes=4 * 2**20),
@@ -110,7 +114,7 @@
             flops=0, bytes_accessed=20 * 2**20, transcendentals=0
         ),
         name="fold",
-    )(near(weight))
+    )(near(held), pltpu.with_memory_space_constraint(weight, pltpu.HBM))
 
 
 def store_pairs(values_of, sides, count, even, odd):
@@ -687,7 +691,7 @@
     (before, after), near_weight = lax.optimization_barrier(((before, after), near_weight))
     sent = pack(place, near_frames, near_grad, before, after)
     received = (with_core(sent[0]), with_chip(sent[1]))
-    folded = fold(near_weight)
+    folded = fold(near_weight, conv_weight)
     middle = centre(near_frames, before, after, folded)
     received, middle = lax.optimization_barrier((received, middle))
     latent, sums, tail, low, high, grad = forward(

time: 70.1 us -> 69.4 us (0.990)
  waiting for transfers between devices: 2.67 us -> 1.68 us
    ppermute x1, waiting for transfers between devices: 1.54 us -> 0.54 us  [with_chip(): return lax.ppermute(value, 'scene', pairs + [(b, a) for a, b in pairs])]
    pallas_call x1, Pallas kernels: 1.5 us -> 2.49 us  [fold(): pl.pallas_call(fold_kernel, out_shape=pltpu.VMEM((9, wide, wide), BF16),...]
    pallas_call x1, Pallas kernels: 3.78 us -> 3.03 us  [fetch(): pl.pallas_call(fetch_kernel, out_shape=[pltpu.VMEM(shape, BF16) for shape...]
  transfers between devices with their start and end apart: 11 -> 11, of which waited for: 5 -> 5; matrix products, arithmetic and copies ran while one was open for 0% -> 0% of each run, Pallas kernels for 20% -> 21%
where the time goes in v7:
time: 69.4 us; the launch traced here: 69.1 us
  Pallas kernels  29.1 us (42%)
  starting transfers between devices  19.7 us (28%)
  blocking collectives  17.7 us (26%)
  waiting for transfers between devices  1.68 us (2%)
  between operations  0.8 us (1%)
    all_to_all x1, blocking collectives, per_device(): tails = lax.all_to_all(tail, 'tm', 0, 0, tiled=True)  17.7 us
    pallas_call x1, Pallas kernels, forward(): pl.pallas_call(forward_kernel, out_shape=(pltpu.VMEM((lat, 16, chans), F3...  8.6 us
    pallas_call x1, Pallas kernels, backward(): pl.pallas_call(backward_kernel, out_shape=jax.ShapeDtypeStruct(out_grad.s...  6.78 us
    ppermute x3, starting transfers between devices, chip_shifts(): lax.ppermute(value, 'scene', [(i, (i + 2 * k) % count) for i in range(cou...  6.26 us
    ppermute x2, starting transfers between devices, shifted(): lax.ppermute(value, axis, [(i, i + steps) for i in range(count) if 0 <= i...  5.95 us
    ppermute x5, starting transfers between devices, with_core(): return lax.ppermute(value, 'scene', [(i, i ^ 1) for i in range(count)])  4.41 us
    pallas_call x1, Pallas kernels, attend(): pl.pallas_call(attend_kernel, out_shape=jax.ShapeDtypeStruct((lat, 2, 8,...  3.4 us
    ppermute x1, starting transfers between devices, with_chip(): return lax.ppermute(value, 'scene', pairs + [(b, a) for a, b in pairs])  3.1 us
  transfers between devices with their start and end apart: 11, of which 5 were waited for; matrix products, arithmetic and copies ran while one was open for 0% of the time, Pallas kernels for 21%

profile of v7, /device:TPU:1, one launch (start us, length us, event | category | flops | bytes accessed | tf_op | source)
XLA Modules:
  0.0 69.1 jit_solution(15594706606200188190)
XLA Ops:
  0.6 0.8 %cut.1 = (bf16[2,2,8,384]{3,2,1,0:T(8,128)(2,1)S(1)}, bf16[4,2,8,384]{3,2,1,0:T(8,128)(2,1)S(1)}) custom-call(bf16[64,2,8,384]{3,2,1,0:T(8,128)(2,1)} %frames.3, bf16[64,2,8,384]{3,2,1,0:T(8,128)(2,1)} %out_grad.3), custom_call_target="tpu_custom_call" | custom-call | tf_op jit(solution)/shard_map/cut/pallas_call | solution.py:42
  1.4 1.3 %collective-permute-start.1 = (bf16[4,2,8,384]{3,2,1,0:T(8,128)(2,1)S(1)}, bf16[4,2,8,384]{3,2,1,0:T(8,128)(2,1)S(1)}, u32[]{:S(2)}, u32[]{:S(2)}) collective-permute-start(bf16[4,2,8,384]{3,2,1,0:T(8,128)(2,1)S(1)} %get-tuple-element.27), channel_id=1, source_target_pairs={{8,0},{16,8},{24,16},{32,24},{40,32},{48,40},{56,48},{64,56},{72,6... | collective-permute-start | bytes 147464 | tf_op jit(solution)/shard_map/ppermute | solution.py:648
  2.7 4.7 %collective-permute-start = (bf16[2,2,8,384]{3,2,1,0:T(8,128)(2,1)S(1)}, bf16[2,2,8,384]{3,2,1,0:T(8,128)(2,1)S(1)}, u32[]{:S(2)}, u32[]{:S(2)}) collective-permute-start(bf16[2,2,8,384]{3,2,1,0:T(8,128)(2,1)S(1)} %get-tuple-element.26), channel_id=1, source_target_pairs={{0,8},{8,16},{16,24},{24,32},{32,40},{40,48},{48,56},{56,64},{64,7... | collective-permute-start | bytes 73736 | tf_op jit(solution)/shard_map/ppermute | solution.py:648
  7.4 0.1 pad_add_fusion.place
  7.5 3.0 %fetch.1 = (bf16[64,2,8,384]{3,2,1,0:T(8,128)(2,1)S(1)}, bf16[64,2,8,384]{3,2,1,0:T(8,128)(2,1)S(1)}, bf16[2,3,3,384,384]{4,3,2,1,0:T(8,128)(2,1)S(1)}) custom-call(bf16[64,2,8,384]{3,2,1,0:T(8,128)(2,1)} %frames.3, bf16[64,2,8,384]{3,2,1,0:T(8,128)(2,1)} %out_grad.3, bf16[3,3,3,384,384]{4,3,2,1,0:T(8,128)(2,1)} %weight.3), custom_call_target="tpu_custom_call" | custom-call | bytes 20971520 | tf_op jit(solution)/shard_map/fetch/pallas_call | solution.py:67
  10.5 0.0 collective-permute-done.1.after
  10.6 1.1 %pack.1 = (bf16[208,768]{1,0:T(8,128)(2,1)S(1)}, bf16[208,768]{1,0:T(8,128)(2,1)S(1)}) custom-call(s32[2]{0:T(128)S(1)} %pad_add_fusion.place, bf16[64,2,8,384]{3,2,1,0:T(8,128)(2,1)S(1)} %get-tuple-element.25.frames, bf16[64,2,8,384]{3,2,1,0:T(8,128)(2,1)S(1)} %get-tuple-element.31.out_grad, bf16[2,2,8,384]{3,2,1,0:T(8,128)(2,1)S(1)} %collective-permute-done.before, ...), custom_call_target="tpu_custom_call" | custom-call | tf_op jit(solution)/shard_map/pack/pallas_call | solution.py:216
  11.7 1.4 %collective-permute-start.2 = (bf16[208,768]{1,0:T(8,128)(2,1)S(1)}, bf16[208,768]{1,0:T(8,128)(2,1)S(1)}, u32[]{:S(2)}, u32[]{:S(2)}) collective-permute-start(bf16[208,768]{1,0:T(8,128)(2,1)S(1)} %get-tuple-element.32.core_sent), channel_id=1, source_target_pairs={{0,1},{1,0},{2,3},{3,2},{4,5},{5,4},{6,7},{7,6},{8,9},{9,8},{10,11... | collective-permute-start | bytes 958472 | tf_op jit(solution)/shard_map/ppermute | solution.py:655
  13.1 3.1 %collective-permute-start.3 = (bf16[208,768]{1,0:T(8,128)(2,1)S(1)}, bf16[208,768]{1,0:T(8,128)(2,1)S(1)}, u32[]{:S(2)}, u32[]{:S(2)}) collective-permute-start(bf16[208,768]{1,0:T(8,128)(2,1)S(1)} %get-tuple-element.33.chip_sent), channel_id=1, source_target_pairs={{1,2},{3,4},{5,6},{2,1},{4,3},{6,5},{9,10},{11,12},{13,14},{10,9},... | collective-permute-start | bytes 958472 | tf_op jit(solution)/shard_map/ppermute | solution.py:661
  16.2 2.5 %fold.1.folded = bf16[9,768,768]{2,1,0:T(8,128)(2,1)S(1)} custom-call(bf16[2,3,3,384,384]{4,3,2,1,0:T(8,128)(2,1)S(1)} %get-tuple-element.34.held, bf16[3,3,3,384,384]{4,3,2,1,0:T(8,128)(2,1)} %weight.3), custom_call_target="tpu_custom_call" | custom-call | bytes 20971520 | tf_op jit(solution)/shard_map/fold/pallas_call | solution.py:106
  18.7 0.0 copy-start.4
  18.7 0.0 copy-start.5
  18.7 2.1 %centre.1.middle = f32[528,768]{1,0:T(8,128)S(1)} custom-call(bf16[64,2,8,384]{3,2,1,0:T(8,128)(2,1)S(1)} %get-tuple-element.25.frames, bf16[2,2,8,384]{3,2,1,0:T(8,128)(2,1)S(1)} %collective-permute-done.before, bf16[4,2,8,384]{3,2,1,0:T(8,128)(2,1)S(1)} %collective-permute-done.1.after, bf16[9,768,768]{2,1,0:T(8,128)(2,1)S(1)} %fold.1.folded), custom_call_target="tpu_custom_call" | custom-call | flops 1868562432 | bytes 6291456 | tf_op jit(solution)/shard_map/centre/pallas_call | solution.py:258
  20.8 0.5 collective-permute-done.3.chip_got
  21.4 8.6 %forward.1 = (f32[8,16,384]{2,1,0:T(8,128)S(1)}, f32[8,16,384]{2,1,0:T(8,128)S(1)}, f32[16,16,384]{2,1,0:T(8,128)S(1)}, f32[72,768]{1,0:T(8,128)S(1)}, f32[72,76...) custom-call(s32[2]{0:T(128)S(1)} %pad_add_fusion.place, s32[8]{0:T(128)S(1)} %copy-done.4, ...), custom_call_target="tpu_custom_call" | custom-call | flops 5605687296 | bytes 16777216 | tf_op jit(solution)/shard_map/forward/pallas_call | solution.py:420
  30.0 17.7 %all_to_all.5.tails = f32[16,16,384]{2,1,0:T(8,128)S(1)} all-to-all(f32[16,16,384]{2,1,0:T(8,128)S(1)} %get-tuple-element.40), channel_id=1, replica_groups=mesh['tm'=16,'scene'=8] {'tm'}, dimensions={0} | all-to-all | bytes 786432 | tf_op jit(solution)/shard_map/all_to_all | solution.py:710
  47.7 0.7 %mix.1.refs_0_ = bf16[128,384]{1,0:T(8,128)(2,1)S(1)} custom-call(s32[2]{0:T(128)S(1)} %pad_add_fusion.place, s32[8]{0:T(128)S(1)} %copy-done.4, f32[8,16,384]{2,1,0:T(8,128)S(1)} %get-tuple-element.38.latent, f32[8,16,384]{2,1,0:T(8,128)S(1)} %get-tuple-element.39.sums, f32[16,16,384]{2,1,0:T(8,128)S(1)} %all_to_all.5.tails), custom_call_target="tpu_custom_call" | custom-call | tf_op jit(solution)/shard_map/mix/pallas_call | solution.py:563
  48.4 2.7 %collective-permute-start.4 = (bf16[128,384]{1,0:T(8,128)(2,1)S(1)}, bf16[128,384]{1,0:T(8,128)(2,1)S(1)}, u32[]{:S(2)}, u32[]{:S(2)}) collective-permute-start(bf16[128,384]{1,0:T(8,128)(2,1)S(1)} %mix.1.refs_0_), channel_id=1, source_target_pairs={{0,2},{1,3},{2,4},{3,5},{4,6},{5,7},{6,0},{7,1},{8,10},{9,11},{10,... | collective-permute-start | bytes 294920 | tf_op jit(solution)/shard_map/ppermute | solution.py:667
  51.0 1.6 %collective-permute-start.5 = (bf16[128,384]{1,0:T(8,128)(2,1)S(1)}, bf16[128,384]{1,0:T(8,128)(2,1)S(1)}, u32[]{:S(2)}, u32[]{:S(2)}) collective-permute-start(bf16[128,384]{1,0:T(8,128)(2,1)S(1)} %mix.1.refs_0_), channel_id=1, source_target_pairs={{0,4},{1,5},{2,6},{3,7},{4,0},{5,1},{6,2},{7,3},{8,12},{9,13},{10,... | collective-permute-start | bytes 294920 | tf_op jit(solution)/shard_map/ppermute | solution.py:667
  52.7 2.0 %collective-permute-start.6 = (bf16[128,384]{1,0:T(8,128)(2,1)S(1)}, bf16[128,384]{1,0:T(8,128)(2,1)S(1)}, u32[]{:S(2)}, u32[]{:S(2)}) collective-permute-start(bf16[128,384]{1,0:T(8,128)(2,1)S(1)} %mix.1.refs_0_), channel_id=1, source_target_pairs={{0,6},{1,7},{2,0},{3,1},{4,2},{5,3},{6,4},{7,5},{8,14},{9,15},{10,... | collective-permute-start | bytes 294920 | tf_op jit(solution)/shard_map/ppermute | solution.py:667
  54.7 0.0 copy-start.3
  54.7 6.8 %backward.1 = bf16[64,2,8,384]{3,2,1,0:T(8,128)(2,1)} custom-call(bf16[66,8,768]{2,1,0:T(8,128)(2,1)S(1)} %get-tuple-element.41.grad, f32[72,768]{1,0:T(8,128)S(1)} %get-tuple-element.42.low, f32[72,768]{1,0:T(8,128)S(1)} %get-tuple-element.43.high, bf16[64,2,8,384]{3,2,1,0:T(8,128)(2,1)S(1)} %get-tuple-element.31.out_grad, bf16[9,768,768]{2,1,0:T(8,128)(2,1)S(1)} %fold.1.folded), custom_call_target="tpu_custom_call" | custom-call | flops 5435817984 | bytes 12582912 | tf_op jit(solution)/shard_map/backward/pallas_call | solution.py:518
  61.5 2.3 %collective-permute-start.7 = (bf16[128,384]{1,0:T(8,128)(2,1)S(1)}, bf16[128,384]{1,0:T(8,128)(2,1)S(1)}, u32[]{:S(2)}, u32[]{:S(2)}) collective-permute-start(bf16[128,384]{1,0:T(8,128)(2,1)S(1)} %mix.1.refs_0_), channel_id=1, source_target_pairs={{0,1},{1,0},{2,3},{3,2},{4,5},{5,4},{6,7},{7,6},{8,9},{9,8},{10,11... | collective-permute-start | bytes 294920 | tf_op jit(solution)/shard_map/ppermute | solution.py:655
  63.8 0.1 collective-permute-start.10
  63.9 0.5 collective-permute-start.8
  64.4 0.1 collective-permute-start.9
  64.5 0.1 copy.12.labels
  64.6 0.2 collective-permute-done.7.refs_4_
  64.7 0.4 collective-permute-done.10.refs_7_
  65.2 0.2 collective-permute-done.8.refs_5_
  65.3 0.4 collective-permute-done.9.refs_6_
  65.7 3.4 %attend.1 = bf16[8,2,8,384]{3,2,1,0:T(8,128)(2,1)} custom-call(s32[8,1]{1,0:T(8,128)S(1)} %copy.12.labels, bf16[128,384]{1,0:T(8,128)(2,1)S(1)} %mix.1.refs_0_, bf16[128,384]{1,0:T(8,128)(2,1)S(1)} %collective-permute-done.4.refs_1_, bf16[128,384]{1,0:T(8,128)(2,1)S(1)} %collective-permute-done.5.refs_2_, ...), custom_call_target="tpu_custom_call" | custom-call | tf_op jit(solution)/shard_map/attend/pallas_call | solution.py:635
  (16 shorter events, 0.0 us)
Async XLA Ops:
  1.4 9.1 %collective-permute-start.1 = (bf16[4,2,8,384]{3,2,1,0:T(8,128)(2,1)S(1)}, bf16[4,2,8,384]{3,2,1,0:T(8,128)(2,1)S(1)}, u32[]{:S(2)}, u32[]{:S(2)}) collective-permute-start(bf16[4,2,8,384]{3,2,1,0:T(8,128)(2,1)S(1)} %get-tuple-element.27), channel_id=1, source_target_pairs={{8,0},{16,8},{24,16},{32,24},{40,32},{48,40},{56,48},{64,56},{72,6... | collective-permute-start | bytes 147464 | tf_op jit(solution)/shard_map/ppermute | solution.py:648
  2.7 7.8 %collective-permute-start = (bf16[2,2,8,384]{3,2,1,0:T(8,128)(2,1)S(1)}, bf16[2,2,8,384]{3,2,1,0:T(8,128)(2,1)S(1)}, u32[]{:S(2)}, u32[]{:S(2)}) collective-permute-start(bf16[2,2,8,384]{3,2,1,0:T(8,128)(2,1)S(1)} %get-tuple-element.26), channel_id=1, source_target_pairs={{0,8},{8,16},{16,24},{24,32},{32,40},{40,48},{48,56},{56,64},{64,7... | collective-permute-start | bytes 73736 | tf_op jit(solution)/shard_map/ppermute | solution.py:648
  11.7 9.1 %collective-permute-start.2 = (bf16[208,768]{1,0:T(8,128)(2,1)S(1)}, bf16[208,768]{1,0:T(8,128)(2,1)S(1)}, u32[]{:S(2)}, u32[]{:S(2)}) collective-permute-start(bf16[208,768]{1,0:T(8,128)(2,1)S(1)} %get-tuple-element.32.core_sent), channel_id=1, source_target_pairs={{0,1},{1,0},{2,3},{3,2},{4,5},{5,4},{6,7},{7,6},{8,9},{9,8},{10,11... | collective-permute-start | bytes 958472 | tf_op jit(solution)/shard_map/ppermute | solution.py:655
  13.1 8.3 %collective-permute-start.3 = (bf16[208,768]{1,0:T(8,128)(2,1)S(1)}, bf16[208,768]{1,0:T(8,128)(2,1)S(1)}, u32[]{:S(2)}, u32[]{:S(2)}) collective-permute-start(bf16[208,768]{1,0:T(8,128)(2,1)S(1)} %get-tuple-element.33.chip_sent), channel_id=1, source_target_pairs={{1,2},{3,4},{5,6},{2,1},{4,3},{6,5},{9,10},{11,12},{13,14},{10,9},... | collective-permute-start | bytes 958472 | tf_op jit(solution)/shard_map/ppermute | solution.py:661
  18.7 2.7 %copy-start.4 = (s32[8]{0:T(128)S(1)}, s32[8]{0:T(128)}, u32[]{:S(2)}) copy-start(s32[8]{0:T(128)} %lengths.3) | copy-start | bytes 100
  18.7 2.7 %copy-start.5 = (bf16[8,384,384]{2,1,0:T(8,128)(2,1)S(1)}, bf16[8,384,384]{2,1,0:T(8,128)(2,1)}, u32[]{:S(2)}) copy-start(bf16[8,384,384]{2,1,0:T(8,128)(2,1)} %down.1) | copy-start | bytes 7077892
  48.4 15.4 %collective-permute-start.4 = (bf16[128,384]{1,0:T(8,128)(2,1)S(1)}, bf16[128,384]{1,0:T(8,128)(2,1)S(1)}, u32[]{:S(2)}, u32[]{:S(2)}) collective-permute-start(bf16[128,384]{1,0:T(8,128)(2,1)S(1)} %mix.1.refs_0_), channel_id=1, source_target_pairs={{0,2},{1,3},{2,4},{3,5},{4,6},{5,7},{6,0},{7,1},{8,10},{9,11},{10,... | collective-permute-start | bytes 294920 | tf_op jit(solution)/shard_map/ppermute | solution.py:667
  51.0 12.8 %collective-permute-start.5 = (bf16[128,384]{1,0:T(8,128)(2,1)S(1)}, bf16[128,384]{1,0:T(8,128)(2,1)S(1)}, u32[]{:S(2)}, u32[]{:S(2)}) collective-permute-start(bf16[128,384]{1,0:T(8,128)(2,1)S(1)} %mix.1.refs_0_), channel_id=1, source_target_pairs={{0,4},{1,5},{2,6},{3,7},{4,0},{5,1},{6,2},{7,3},{8,12},{9,13},{10,... | collective-permute-start | bytes 294920 | tf_op jit(solution)/shard_map/ppermute | solution.py:667
  52.7 11.1 %collective-permute-start.6 = (bf16[128,384]{1,0:T(8,128)(2,1)S(1)}, bf16[128,384]{1,0:T(8,128)(2,1)S(1)}, u32[]{:S(2)}, u32[]{:S(2)}) collective-permute-start(bf16[128,384]{1,0:T(8,128)(2,1)S(1)} %mix.1.refs_0_), channel_id=1, source_target_pairs={{0,6},{1,7},{2,0},{3,1},{4,2},{5,3},{6,4},{7,5},{8,14},{9,15},{10,... | collective-permute-start | bytes 294920 | tf_op jit(solution)/shard_map/ppermute | solution.py:667
  54.6 9.8 %copy-start.6 = (s32[8,1]{0,1:T(1,128)S(1)}, s32[8,1]{0,1:T(1,128)}, u32[]{:S(2)}) copy-start(s32[8,1]{0,1:T(1,128)} %param.18) | copy-start | bytes 100
  54.6 11.1 %copy-start = (bf16[384,384]{1,0:T(8,128)(2,1)S(1)}, bf16[384,384]{1,0:T(8,128)(2,1)}, u32[]{:S(2)}) copy-start(bf16[384,384]{1,0:T(8,128)(2,1)} %refs_8_.1) | copy-start | bytes 884740
  54.7 11.1 %copy-start.1 = (bf16[384,384]{1,0:T(8,128)(2,1)S(1)}, bf16[384,384]{1,0:T(8,128)(2,1)}, u32[]{:S(2)}) copy-start(bf16[384,384]{1,0:T(8,128)(2,1)} %refs_9_.1) | copy-start | bytes 884740
  54.7 11.1 %copy-start.2 = (bf16[384,384]{1,0:T(8,128)(2,1)S(1)}, bf16[384,384]{1,0:T(8,128)(2,1)}, u32[]{:S(2)}) copy-start(bf16[384,384]{1,0:T(8,128)(2,1)} %refs_10_.1) | copy-start | bytes 884740
  54.7 11.1 %copy-start.3 = (bf16[384,384]{1,0:T(8,128)(2,1)S(1)}, bf16[384,384]{1,0:T(8,128)(2,1)}, u32[]{:S(2)}) copy-start(bf16[384,384]{1,0:T(8,128)(2,1)} %refs_11_.1) | copy-start | bytes 884740
  61.5 3.3 %collective-permute-start.7 = (bf16[128,384]{1,0:T(8,128)(2,1)S(1)}, bf16[128,384]{1,0:T(8,128)(2,1)S(1)}, u32[]{:S(2)}, u32[]{:S(2)}) collective-permute-start(bf16[128,384]{1,0:T(8,128)(2,1)S(1)} %mix.1.refs_0_), channel_id=1, source_target_pairs={{0,1},{1,0},{2,3},{3,2},{4,5},{5,4},{6,7},{7,6},{8,9},{9,8},{10,11... | collective-permute-start | bytes 294920 | tf_op jit(solution)/shard_map/ppermute | solution.py:655
  63.8 1.4 %collective-permute-start.10 = (bf16[128,384]{1,0:T(8,128)(2,1)S(1)}, bf16[128,384]{1,0:T(8,128)(2,1)S(1)}, u32[]{:S(2)}, u32[]{:S(2)}) collective-permute-start(bf16[128,384]{1,0:T(8,128)(2,1)S(1)} %collective-permute-done.6.refs_3_), channel_id=1, source_target_pairs={{0,1},{1,0},{2,3},{3,2},{4,5},{5,4},{6,7},{7,6},{8,9},{9,8},{10,11... | collective-permute-start | bytes 294920 | tf_op jit(solution)/shard_map/ppermute | solution.py:655
  63.9 1.4 %collective-permute-start.8 = (bf16[128,384]{1,0:T(8,128)(2,1)S(1)}, bf16[128,384]{1,0:T(8,128)(2,1)S(1)}, u32[]{:S(2)}, u32[]{:S(2)}) collective-permute-start(bf16[128,384]{1,0:T(8,128)(2,1)S(1)} %collective-permute-done.4.refs_1_), channel_id=1, source_target_pairs={{0,1},{1,0},{2,3},{3,2},{4,5},{5,4},{6,7},{7,6},{8,9},{9,8},{10,11... | collective-permute-start | bytes 294920 | tf_op jit(solution)/shard_map/ppermute | solution.py:655
  64.4 1.3 %collective-permute-start.9 = (bf16[128,384]{1,0:T(8,128)(2,1)S(1)}, bf16[128,384]{1,0:T(8,128)(2,1)S(1)}, u32[]{:S(2)}, u32[]{:S(2)}) collective-permute-start(bf16[128,384]{1,0:T(8,128)(2,1)S(1)} %collective-permute-done.5.refs_2_), channel_id=1, source_target_pairs={{0,1},{1,0},{2,3},{3,2},{4,5},{5,4},{6,7},{7,6},{8,9},{9,8},{10,11... | collective-permute-start | bytes 294920 | tf_op jit(solution)/shard_map/ppermute | solution.py:655
